TPU v7x, 128 devices: a whole 4x4x4 slice. The times are simulated.
128 devices in a mesh: section: 2 (over z_lo), tensor: 2 (over core), dp: 32 (over y, z_hi, x).
Axes of the slice: x: 4, y: 4, z: 4 (z_hi: 2, z_lo: 2; z = z_hi * 2 + z_lo), core: 2. Of those that a mesh axis runs over, the one named last changes fastest.
Arguments:
- tokens: bfloat16 [2, 8192, 1024], P(None, ('tensor', 'dp')), may hold values from -6 to 6
- cotangent: bfloat16 [2, 8192, 1024], P(None, ('tensor', 'dp')), may hold values from -6 to 6
- doc_lengths: int32 [2, 4, 4], replicated, may hold values from 1 to 1792, 2048 in all within a row
- gains: float32 [2, 2, 1024], P('section'), may hold values from 0.5 to 1.5
- wqkv: bfloat16 [2, 1024, 3, 1024], P('section', None, None, 'tensor'), may hold values from -0.1875 to 0.1875
- wo: bfloat16 [2, 1024, 1024], P('section', 'tensor'), may hold values from -2 to 2
- wgu: bfloat16 [2, 1024, 2, 2816], P('section', None, None, 'tensor'), may hold values from -0.1875 to 0.1875
- wd: bfloat16 [2, 2816, 1024], P('section', 'tensor'), may hold values from -0.109375 to 0.109375
Outputs:
- acts: bfloat16 [2, 2, 8192, 1024], P('section', None, ('tensor', 'dp'))
- dins: float32 [2, 2, 8192, 1024], P('section', None, ('tensor', 'dp'))
- grad_qkv: float32 [2, 1024, 3, 1024], P('section', 'dp', None, 'tensor')
- grad_out_proj: float32 [2, 1024, 1024], P('section', ('tensor', 'dp'))
- grad_gate_up: float32 [2, 1024, 2, 2816], P('section', 'dp', None, 'tensor')
- grad_down: float32 [2, 2816, 1024], P('section', ('tensor', 'dp'))
- grad_gains: float32 [2, 2, 1024], P('section')
Inputs may be any that keep to these rules, and one draw needn't show every extreme that they name: `doc_lengths`: in each sequence one document has exactly 1792 tokens.
All inputs are finite; a program needn't handle non-finite values.
Results may differ from a plain program's by a relative error of at most 0.04.
Values may be sent and summed in bfloat16 or wider, within the bound.
No kernel may reach another device: no remote copies, remote signals or barrier semaphores. Data moves between devices by JAX's collectives and lax.ppermute only.
A program may use at most 256 MiB of HBM per device.

v0:
```python
import jax
import jax.numpy as jnp
from jax import lax
from jax.sharding import PartitionSpec as P

HD = 64
LEN = 2048
SPLIT = 8


EPSILON = 1e-06
NEGATIVE = -1e30


def swapped(value, axis, stride):
    mask = 2**stride
    pairs = [(source, source ^ mask) for source in range(lax.axis_size(axis))]
    return lax.ppermute(value, axis, pairs)


def passed_along(value, axis, steps):
    count = lax.axis_size(axis)
    first, last = (max(0, -steps), min(count, count - steps))
    return lax.ppermute(value, axis, [(source, source + steps) for source in range(first, last)])


def rms_scale(hidden):
    return lax.rsqrt(jnp.mean(hidden * hidden, axis=-1, keepdims=True) + EPSILON)


def place_index(quarter, within, rows):
    half = rows // 2
    block = jnp.where(within < half, quarter, 2 * SPLIT - 1 - quarter)
    return block * half + within % half


def rotary_tables(places_int):
    places = places_int.astype(jnp.float32)
    half = HD // 2
    freqs = 10000.0 ** (-jnp.arange(half, dtype=jnp.float32) / half)
    angles = places[:, None] * freqs[None, :]
    return (jnp.cos(angles)[:, None, :], jnp.sin(angles)[:, None, :])


def rotate(vectors, tables):
    cosine, sine = tables
    half = vectors.shape[-1] // 2
    first = vectors[..., :half]
    second = vectors[..., half:]
    return jnp.concatenate(
        [first * cosine - second * sine, second * cosine + first * sine], axis=-1
    )


def unrotate(vectors, tables):
    cosine, sine = tables
    half = vectors.shape[-1] // 2
    first = vectors[..., :half]
    second = vectors[..., half:]
    return jnp.concatenate(
        [first * cosine + second * sine, second * cosine - first * sine], axis=-1
    )


def gather_rows(normed):
    return lax.all_gather(normed, "tensor", axis=0, tiled=True)


def gather_grads(grads):
    return lax.all_gather(grads, "tensor", axis=0, tiled=True)


def scatter_rows(term, rows):
    return lax.psum_scatter(
        term(jnp.int32(0), rows // lax.axis_size("tensor") * lax.axis_size("tensor")).astype(
            jnp.bfloat16
        ),
        "tensor",
        scatter_dimension=0,
        tiled=True,
    ).astype(jnp.float32)


def scatter_grads(term, rows):
    return lax.psum_scatter(
        term(jnp.int32(0), rows // lax.axis_size("tensor") * lax.axis_size("tensor")).astype(
            jnp.bfloat16
        ),
        "tensor",
        scatter_dimension=0,
        tiled=True,
    ).astype(jnp.float32)


def swap_keys(held, bit):
    return swapped(held, "dp", bit)


def swap_key_grads(held, bit):
    return swapped(held.astype(jnp.bfloat16), "dp", bit).astype(held.dtype)


def gather_group(block, swapper):
    position = lax.axis_index("dp")
    held = block
    for bit in range(SPLIT.bit_length() - 1):
        arrived = swapper(held, bit)
        lower = position // (1 << bit) % 2 == 0
        held = jnp.where(
            lower,
            jnp.concatenate([held, arrived], axis=1),
            jnp.concatenate([arrived, held], axis=1),
        )
    return held


def reduce_group(full, swapper):
    position = lax.axis_index("dp")
    summed = full
    for bit in reversed(range(SPLIT.bit_length() - 1)):
        half = summed.shape[1] // 2
        lower_part = summed[:, :half]
        upper_part = summed[:, half:]
        lower = position // (1 << bit) % 2 == 0
        keeping = jnp.where(lower, lower_part, upper_part)
        sending = jnp.where(lower, upper_part, lower_part)
        summed = keeping + swapper(sending, bit)
    return summed


def visible_keys(lens_row, query_places, rows):
    ends = jnp.cumsum(lens_row, dtype=jnp.int32)
    gathered_index = jnp.arange(LEN, dtype=jnp.int32)
    key_places = place_index(gathered_index // rows, gathered_index % rows, rows)
    key_docs = jnp.sum(
        (key_places[:, None] >= ends[None, :]).astype(jnp.int32), axis=1, dtype=jnp.int32
    )
    query_docs = jnp.sum(
        (query_places[:, None] >= ends[None, :]).astype(jnp.int32), axis=1, dtype=jnp.int32
    )
    return (key_places[None, :] <= query_places[:, None]) & (
        query_docs[:, None] == key_docs[None, :]
    )


def score_block(queries, keys_all, visible):
    raw = jnp.einsum(
        "qhd,khd->hqk", queries, keys_all, preferred_element_type=jnp.float32
    ) * HD ** (-0.5)
    return jnp.where(visible[None], raw, NEGATIVE)


def norm_backward(hidden, grad_normed, gain_row):
    scale_row = rms_scale(hidden)
    unit = hidden * scale_row
    weighted = grad_normed * gain_row
    grad_hidden = scale_row * (weighted - unit * jnp.mean(weighted * unit, axis=-1, keepdims=True))
    return (grad_hidden, jnp.sum(grad_normed * unit, axis=0))


def forward_block(hidden_in, first, weights, gain_pair, visible, tables, value_first):
    w_qkv, w_out, w_gu, w_down = weights
    rows = visible.shape[0]
    width_dev = w_qkv.shape[2]
    heads_dev = width_dev // HD
    normed = (hidden_in * rms_scale(hidden_in) * gain_pair[0]).astype(jnp.bfloat16)
    gathered = gather_rows(normed)
    projected = jnp.einsum("td,dcf->tcf", gathered, w_qkv, preferred_element_type=jnp.float32)
    queries = rotate(projected[:, 0].reshape(rows, heads_dev, HD), tables).astype(jnp.bfloat16)
    keys_own = rotate(projected[:, 1].reshape(rows, heads_dev, HD), tables).astype(jnp.bfloat16)
    values_raw = projected[:, 2]
    values_mixed = jnp.where(
        first, values_raw, 0.5 * values_raw + 0.5 * value_first.astype(jnp.float32)
    )
    values_own = values_mixed.astype(jnp.bfloat16)
    own_pair = jnp.stack([keys_own.reshape(rows, width_dev), values_own])
    shared = gather_group(own_pair, swap_keys)
    keys_all = shared[0].reshape(LEN, heads_dev, HD)
    values_all = shared[1].reshape(LEN, heads_dev, HD)
    scores = score_block(queries, keys_all, visible)
    highest = jnp.max(scores, axis=-1, keepdims=True)
    expd = jnp.exp(scores - highest)
    totals = jnp.sum(expd, axis=-1, keepdims=True)
    attend = expd / totals
    log_totals = highest + jnp.log(totals)
    attended = jnp.einsum(
        "hqk,khd->qhd", attend.astype(jnp.bfloat16), values_all, preferred_element_type=jnp.float32
    )
    attended = attended.reshape(rows, width_dev).astype(jnp.bfloat16)
    branch = scatter_rows(
        lambda start, count: jnp.dot(attended, w_out, preferred_element_type=jnp.float32), rows
    )
    middle = hidden_in + branch
    normed_two = (middle * rms_scale(middle) * gain_pair[1]).astype(jnp.bfloat16)
    gathered_two = gather_rows(normed_two)
    gate_up = jnp.einsum("td,dcf->tcf", gathered_two, w_gu, preferred_element_type=jnp.float32)
    activated = (jax.nn.silu(gate_up[:, 0]) * gate_up[:, 1]).astype(jnp.bfloat16)
    feed = scatter_rows(
        lambda start, count: jnp.dot(activated, w_down, preferred_element_type=jnp.float32), rows
    )
    result = middle + feed
    saved = (
        hidden_in,
        gathered,
        queries,
        shared,
        log_totals,
        attended,
        middle,
        gathered_two,
        gate_up,
        activated,
    )
    return (result, values_own, saved)


def backward_block(grad_out, first, grad_value_first, weights, gain_pair, saved, visible, tables):
    w_qkv, w_out, w_gu, w_down = weights
    (
        hidden_in,
        gathered,
        queries,
        kept,
        log_totals,
        attended,
        middle,
        gathered_two,
        gate_up,
        activated,
    ) = saved
    rows = visible.shape[0]
    width_dev = w_qkv.shape[2]
    heads_dev = width_dev // HD
    grad_feed = gather_grads(grad_out.astype(jnp.bfloat16))
    grad_w_down = jnp.einsum("tf,td->fd", activated, grad_feed, preferred_element_type=jnp.float32)
    grad_act = jnp.einsum("td,fd->tf", grad_feed, w_down, preferred_element_type=jnp.float32)
    gate = gate_up[:, 0]
    upper = gate_up[:, 1]
    sigma = jax.nn.sigmoid(gate)
    grad_gate = grad_act * upper * sigma * (1.0 + gate * (1.0 - sigma))
    grad_upper = grad_act * gate * sigma
    grad_gu = jnp.stack([grad_gate, grad_upper], axis=1).astype(jnp.bfloat16)
    grad_w_gu = jnp.einsum("td,tcf->dcf", gathered_two, grad_gu, preferred_element_type=jnp.float32)
    grad_normed_two = scatter_grads(
        lambda start, count: jnp.einsum(
            "tcf,dcf->td", grad_gu, w_gu, preferred_element_type=jnp.float32
        ),
        rows,
    )
    grad_mid_norm, grad_gain_two = norm_backward(middle, grad_normed_two, gain_pair[1])
    grad_middle = grad_out + grad_mid_norm
    grad_branch = gather_grads(grad_middle.astype(jnp.bfloat16))
    grad_w_out = jnp.einsum("tf,td->fd", attended, grad_branch, preferred_element_type=jnp.float32)
    grad_attended = jnp.einsum("td,fd->tf", grad_branch, w_out, preferred_element_type=jnp.float32)
    grad_attended = grad_attended.astype(jnp.bfloat16).reshape(rows, heads_dev, HD)
    keys_all = kept[0].reshape(LEN, heads_dev, HD)
    values_all = kept[1].reshape(LEN, heads_dev, HD)
    scores = score_block(queries, keys_all, visible)
    attend = jnp.exp(scores - log_totals)
    grad_attend = jnp.einsum(
        "qhd,khd->hqk", grad_attended, values_all, preferred_element_type=jnp.float32
    )
    inner = jnp.sum(attend * grad_attend, axis=-1, keepdims=True)
    grad_scores = (attend * (grad_attend - inner)).astype(jnp.bfloat16)
    grad_queries = jnp.einsum(
        "hqk,khd->qhd", grad_scores, keys_all, preferred_element_type=jnp.float32
    ) * HD ** (-0.5)
    grad_keys_all = jnp.einsum(
        "hqk,qhd->khd", grad_scores, queries, preferred_element_type=jnp.float32
    ) * HD ** (-0.5)
    grad_values_all = jnp.einsum(
        "hqk,qhd->khd",
        attend.astype(jnp.bfloat16),
        grad_attended,
        preferred_element_type=jnp.float32,
    )
    stacked = jnp.stack(
        [grad_keys_all.reshape(LEN, width_dev), grad_values_all.reshape(LEN, width_dev)]
    )
    summed = reduce_group(stacked, swap_key_grads)
    grad_keys = unrotate(summed[0].reshape(rows, heads_dev, HD), tables).reshape(rows, width_dev)
    grad_queries = unrotate(grad_queries, tables).reshape(rows, width_dev)
    grad_mixed = summed[1]
    grad_value_send = jnp.where(first, 0.0, 0.5 * grad_mixed).astype(jnp.bfloat16)
    grad_values_raw = jnp.where(
        first, grad_mixed + grad_value_first.astype(jnp.float32), 0.5 * grad_mixed
    )
    grad_projected = jnp.stack([grad_queries, grad_keys, grad_values_raw], axis=1).astype(
        jnp.bfloat16
    )
    grad_w_qkv = jnp.einsum(
        "td,tcf->dcf", gathered, grad_projected, preferred_element_type=jnp.float32
    )
    grad_normed = scatter_grads(
        lambda start, count: jnp.einsum(
            "tcf,dcf->td", grad_projected, w_qkv, preferred_element_type=jnp.float32
        ),
        rows,
    )
    grad_in_norm, grad_gain_one = norm_backward(hidden_in, grad_normed, gain_pair[0])
    grad_in = grad_middle + grad_in_norm
    weight_terms = (grad_w_qkv, grad_w_out, grad_w_gu, grad_w_down)
    return (grad_in, grad_value_send, weight_terms, jnp.stack([grad_gain_one, grad_gain_two]))


def per_device(tokens, cotangent, doc_lengths, gains, wqkv, wo, wgu, wd):
    first = lax.axis_index("section") == 0
    position = lax.axis_index("dp")
    quarter = position % SPLIT
    lens_group = lax.dynamic_index_in_dim(doc_lengths, position // SPLIT, 1, keepdims=False)
    weights = (wqkv[0], wo[0], wgu[0], wd[0])
    gain_pair = gains[0]
    count = tokens.shape[0]
    sub_rows = tokens.shape[1]
    width = tokens.shape[2]
    rows = sub_rows * lax.axis_size("tensor")
    own_places = place_index(quarter, jnp.arange(rows, dtype=jnp.int32), rows)
    tables = rotary_tables(own_places)
    incoming = jnp.zeros((2, sub_rows, width), jnp.bfloat16)
    outputs = []
    records = []
    for tick in range(count + 1):
        early = min(tick, count - 1)
        late = max(tick - 1, 0)
        batch = jnp.where(first, early, late)
        visible = visible_keys(
            lax.dynamic_index_in_dim(lens_group, batch, 0, keepdims=False), own_places, rows
        )
        hidden_in = jnp.where(
            first, tokens[early].astype(jnp.float32), incoming[0].astype(jnp.float32)
        )
        value_first = incoming[1].reshape(rows, -1)
        result, values_own, saved = forward_block(
            hidden_in, first, weights, gain_pair, visible, tables, value_first
        )
        outputs.append(result.astype(jnp.bfloat16))
        records.append(saved)
        if tick < count:
            incoming = passed_along(
                jnp.stack([result.astype(jnp.bfloat16), values_own.reshape(sub_rows, width)]),
                "section",
                1,
            )
    acts = jnp.stack([jnp.where(first, outputs[item], outputs[item + 1]) for item in range(count)])[
        None
    ]
    returning = jnp.zeros((2, sub_rows, width), jnp.bfloat16)
    grad_inputs = []
    weight_sums = tuple((jnp.zeros(weight.shape, jnp.float32) for weight in weights))
    shares = None
    gain_sums = jnp.zeros((2, width), jnp.float32)
    for tick in range(count + 1):
        early = max(tick - 1, 0)
        late = min(tick, count - 1)
        live = jnp.where(first, tick >= 1, tick < count)
        batch = jnp.where(first, early, late)
        saved = jax.tree.map(
            lambda left, right: jnp.where(first, left, right),
            records[early],
            records[min(late + 1, count)],
        )
        visible = visible_keys(
            lax.dynamic_index_in_dim(lens_group, batch, 0, keepdims=False), own_places, rows
        )
        grad_out = jnp.where(
            first, returning[0].astype(jnp.float32), cotangent[late].astype(jnp.float32)
        )
        grad_out = jnp.where(live, grad_out, 0.0)
        grad_value_first = returning[1].reshape(rows, -1)
        grad_in, grad_value_send, weight_terms, gain_terms = backward_block(
            grad_out, first, grad_value_first, weights, gain_pair, saved, visible, tables
        )
        grad_inputs.append(grad_in)
        gain_sums = gain_sums + gain_terms
        weight_sums = tuple((total + term for total, term in zip(weight_sums, weight_terms)))
        if tick < count:
            returning = passed_along(
                jnp.stack([grad_in.astype(jnp.bfloat16), grad_value_send.reshape(sub_rows, width)]),
                "section",
                -1,
            )
    shares = (
        lax.psum_scatter(
            weight_sums[0].astype(jnp.bfloat16), "dp", scatter_dimension=0, tiled=True
        ).astype(jnp.float32),
        lax.psum_scatter(
            weight_sums[1].astype(jnp.bfloat16), "dp", scatter_dimension=0, tiled=True
        ).astype(jnp.float32),
        lax.psum_scatter(
            weight_sums[2].astype(jnp.bfloat16), "dp", scatter_dimension=0, tiled=True
        ).astype(jnp.float32),
        lax.psum_scatter(
            weight_sums[3].astype(jnp.bfloat16), "dp", scatter_dimension=0, tiled=True
        ).astype(jnp.float32),
    )
    dins = jnp.stack(
        [jnp.where(first, grad_inputs[item + 1], grad_inputs[item]) for item in range(count)]
    )[None]
    gain_total = lax.psum(gain_sums, ("tensor", "dp"))
    return (
        acts,
        dins,
        shares[0][None],
        shares[1][None],
        shares[2][None],
        shares[3][None],
        gain_total[None],
    )


def solution(mesh):
    placed = (
        P(None, ("tensor", "dp"), None),
        P(None, ("tensor", "dp"), None),
        P(),
        P("section", None, None),
        P("section", None, None, "tensor"),
        P("section", "tensor", None),
        P("section", None, None, "tensor"),
        P("section", "tensor", None),
    )
    return jax.shard_map(
        per_device,
        mesh=mesh,
        in_specs=placed,
        out_specs=(
            P("section", None, ("tensor", "dp"), None),
            P("section", None, ("tensor", "dp"), None),
            P("section", "dp", None, "tensor"),
            P("section", ("tensor", "dp"), None),
            P("section", "dp", None, "tensor"),
            P("section", ("tensor", "dp"), None),
            P("section", None, None),
        ),
        check_vma=False,
    )
```

profile of v0, /device:TPU:0, one launch (start us, length us, event | category | flops | bytes accessed | tf_op | source)
XLA Modules:
  0.0 1784.4 jit_solution(11320981636031774076)
XLA Ops:
  27.2 12.7 collective-permute-done
  45.9 23.1 %collective-permute-done.1 = bf16[2,512,512]{2,1,0:T(8,128)(2,1)} collective-permute-done((bf16[2,512,512]{2,1,0:T(8,128)(2,1)}, bf16[2,512,512]{2,1,0:T(8,128)(2,1)}, u32[]{:S(2)}, u32[]{:S(2)}) %collective-permute-start.1) | collective-permute-done | bytes 1048608 | tf_op jit(solution)/shard_map/ppermute | solution.py:18
  80.9 40.8 %collective-permute-done.2 = bf16[2,1024,512]{2,1,0:T(8,128)(2,1)} collective-permute-done((bf16[2,1024,512]{2,1,0:T(8,128)(2,1)}, bf16[2,1024,512]{2,1,0:T(8,128)(2,1)}, u32[]{:S(2)}, u32[]{:S(2)}) %collective-permute-start.2) | collective-permute-done | bytes 2097184 | tf_op jit(solution)/shard_map/ppermute | solution.py:18
  154.8 12.3 reduce-scatter.18.cloned.1.call-done
  197.7 11.6 collective-permute-done.3
  233.0 12.5 collective-permute-done.4
  250.1 22.9 %collective-permute-done.5 = bf16[2,512,512]{2,1,0:T(8,128)(2,1)S(1)} collective-permute-done((bf16[2,512,512]{2,1,0:T(8,128)(2,1)S(1)}, bf16[2,512,512]{2,1,0:T(8,128)(2,1)S(1)}, u32[]{:S(2)}, u32[]{:S(2)}) %collective-permute-start.5) | collective-permute-done | bytes 1048608 | tf_op jit(solution)/shard_map/ppermute | solution.py:18
  276.5 44.6 %collective-permute-done.6 = bf16[2,1024,512]{2,1,0:T(8,128)(2,1)S(1)} collective-permute-done((bf16[2,1024,512]{2,1,0:T(8,128)(2,1)S(1)}, bf16[2,1024,512]{2,1,0:T(8,128)(2,1)S(1)}, u32[]{:S(2)}, u32[]{:S(2)}) %collective-permute-start.6) | collective-permute-done | bytes 2097184 | tf_op jit(solution)/shard_map/ppermute | solution.py:18
  410.2 12.1 fusion.14
  427.7 15.4 multiply_reduce_fusion.2
  443.1 12.2 multiply_convert_fusion.2
  472.8 46.1 %collective-permute-done.11 = bf16[2,1024,512]{2,1,0:T(8,128)(2,1)S(1)} collective-permute-done((bf16[2,1024,512]{2,1,0:T(8,128)(2,1)S(1)}, bf16[2,1024,512]{2,1,0:T(8,128)(2,1)S(1)}, u32[]{:S(2)}, u32[]{:S(2)}) %collective-permute-start.11) | collective-permute-done | bytes 2097184 | tf_op jit(solution)/shard_map/ppermute | solution.py:18
  535.0 14.8 collective-permute-done.12
  623.8 12.5 collective-permute-done.8
  641.3 22.9 %collective-permute-done.9 = bf16[2,512,512]{2,1,0:T(8,128)(2,1)S(1)} collective-permute-done((bf16[2,512,512]{2,1,0:T(8,128)(2,1)S(1)}, bf16[2,512,512]{2,1,0:T(8,128)(2,1)S(1)}, u32[]{:S(2)}, u32[]{:S(2)}) %collective-permute-start.9) | collective-permute-done | bytes 1048608 | tf_op jit(solution)/shard_map/ppermute | solution.py:18
  673.1 53.1 %collective-permute-done.14 = bf16[2,128,1024]{2,1,0:T(8,128)(2,1)S(1)} collective-permute-done((bf16[2,128,1024]{2,1,0:T(8,128)(2,1)S(1)}, bf16[2,128,1024]{2,1,0:T(8,128)(2,1)S(1)}, u32[]{:S(2)}, u32[]{:S(2)}) %collective-permute-start.14) | collective-permute-done | bytes 524320 | tf_op jit(solution)/shard_map/ppermute | solution.py:24
  825.3 12.1 fusion.12
  842.7 13.7 multiply_reduce_fusion.1
  856.5 12.1 multiply_convert_fusion.1
  884.6 47.0 %collective-permute-done.15 = bf16[2,1024,512]{2,1,0:T(8,128)(2,1)S(1)} collective-permute-done((bf16[2,1024,512]{2,1,0:T(8,128)(2,1)S(1)}, bf16[2,1024,512]{2,1,0:T(8,128)(2,1)S(1)}, u32[]{:S(2)}, u32[]{:S(2)}) %collective-permute-start.15) | collective-permute-done | bytes 2097184 | tf_op jit(solution)/shard_map/ppermute | solution.py:18
  942.5 20.3 %collective-permute-done.16 = bf16[2,512,512]{2,1,0:T(8,128)(2,1)} collective-permute-done((bf16[2,512,512]{2,1,0:T(8,128)(2,1)}, bf16[2,512,512]{2,1,0:T(8,128)(2,1)}, u32[]{:S(2)}, u32[]{:S(2)}) %collective-permute-start.16) | collective-permute-done | bytes 1048608 | tf_op jit(solution)/shard_map/ppermute | solution.py:18
  994.0 10.4 reduce-scatter.36.cloned.1.call-done
  1010.8 14.9 collective-permute-done.18
  1068.4 12.1 fusion.10
  1085.9 13.7 multiply_reduce_fusion
  1099.7 12.1 multiply_convert_fusion
  1135.8 40.5 %collective-permute-done.19 = bf16[2,1024,512]{2,1,0:T(8,128)(2,1)} collective-permute-done((bf16[2,1024,512]{2,1,0:T(8,128)(2,1)}, bf16[2,1024,512]{2,1,0:T(8,128)(2,1)}, u32[]{:S(2)}, u32[]{:S(2)}) %collective-permute-start.19) | collective-permute-done | bytes 2097184 | tf_op jit(solution)/shard_map/ppermute | solution.py:18
  1195.4 13.3 collective-permute-done.20
  1260.0 11.6 add_convert_fusion
  1295.1 112.8 %fusion = bf16[48,1024]{1,0:T(8,128)(2,1)S(1)} fusion(bf16[1408,1024]{1,0:T(8,128)(2,1)} %add_convert_fusion.2), kind=kCustom, calls=%all-reduce-scatter | all-reduce-scatter fusion | flops 1572865 | bytes 2982400
  1425.4 168.3 %psum.7 = f32[1,2,1024]{2,1,0:T(2,128)} all-reduce(f32[1,2,1024]{2,1,0:T(2,128)S(1)} %fusion.263), channel_id=1, replica_groups=mesh['section'=2,'tensor'=2,'dp'=32] {'tensor','dp'}, use_global_device_ids=true, to_apply=%region_61.62 | all-reduce | flops 2048 | bytes 16384 | tf_op jit(solution)/shard_map/psum | solution.py:399
  1599.0 176.5 %reduce-scatter.46.cloned.1.call-done = bf16[32,2,1408]{2,0,1:T(8,128)(2,1)} async-done(((bf16[1024,2,1408]{2,0,1:T(8,128)(2,1)}), bf16[32,2,1408]{2,0,1:T(8,128)(2,1)}) %reduce-scatter.46.cloned.1.call-update) | async-done | bytes 180240 | tf_op jit(solution)/shard_map/reduce_scatter | solution.py:389
  (647 shorter events, 706.6 us)
Async XLA Ops:
  7.2 159.9 %reduce-scatter.18.cloned.1.call-start = ((), (), s32[]{:S(2)}) async-start(), calls=%async_computation.15 | async-start | bytes 786432 | tf_op jit(solution)/shard_map/reduce_scatter | solution.py:74
  25.6 14.3 collective-permute-start
  42.8 26.2 %collective-permute-start.1 = (bf16[2,512,512]{2,1,0:T(8,128)(2,1)}, bf16[2,512,512]{2,1,0:T(8,128)(2,1)}, u32[]{:S(2)}, u32[]{:S(2)}) collective-permute-start(bf16[2,512,512]{2,1,0:T(8,128)(2,1)} %maximum_select_fusion.6), channel_id=1, source_target_pairs={{0,2},{1,3},{2,0},{3,1},{4,6},{5,7},{6,4},{7,5},{8,10},{9,11},{10,... | collective-permute-start | bytes 3145736 | tf_op jit(solution)/shard_map/ppermute | solution.py:18
  73.1 48.7 %collective-permute-start.2 = (bf16[2,1024,512]{2,1,0:T(8,128)(2,1)}, bf16[2,1024,512]{2,1,0:T(8,128)(2,1)}, u32[]{:S(2)}, u32[]{:S(2)}) collective-permute-start(bf16[2,1024,512]{2,1,0:T(8,128)(2,1)} %maximum_select_fusion.3), channel_id=1, source_target_pairs={{0,4},{1,5},{2,6},{3,7},{4,0},{5,1},{6,2},{7,3},{8,12},{9,13},{10,... | collective-permute-start | bytes 6291464 | tf_op jit(solution)/shard_map/ppermute | solution.py:18
  154.7 37.1 %reduce-scatter.20.cloned.1.call-start = ((), (), s32[]{:S(2)}) async-start(), calls=%async_computation.16 | async-start | bytes 786432 | tf_op jit(solution)/shard_map/reduce_scatter | solution.py:74
  179.8 189.2 %reduce-scatter.22.cloned.1.call-start = ((), (), s32[]{:S(2)}) async-start(), calls=%async_computation.17 | async-start | bytes 786432 | tf_op jit(solution)/shard_map/reduce_scatter | solution.py:74
  194.0 15.4 collective-permute-start.3
  231.4 14.0 collective-permute-start.4
  247.1 26.0 %collective-permute-start.5 = (bf16[2,512,512]{2,1,0:T(8,128)(2,1)S(1)}, bf16[2,512,512]{2,1,0:T(8,128)(2,1)S(1)}, u32[]{:S(2)}, u32[]{:S(2)}) collective-permute-start(bf16[2,512,512]{2,1,0:T(8,128)(2,1)S(1)} %maximum_select_fusion.7), channel_id=1, source_target_pairs={{0,2},{1,3},{2,0},{3,1},{4,6},{5,7},{6,4},{7,5},{8,10},{9,11},{10,... | collective-permute-start | bytes 3145736 | tf_op jit(solution)/shard_map/ppermute | solution.py:18
  273.6 47.5 %collective-permute-start.6 = (bf16[2,1024,512]{2,1,0:T(8,128)(2,1)S(1)}, bf16[2,1024,512]{2,1,0:T(8,128)(2,1)S(1)}, u32[]{:S(2)}, u32[]{:S(2)}) collective-permute-start(bf16[2,1024,512]{2,1,0:T(8,128)(2,1)S(1)} %maximum_select_fusion.4), channel_id=1, source_target_pairs={{0,4},{1,5},{2,6},{3,7},{4,0},{5,1},{6,2},{7,3},{8,12},{9,13},{10,... | collective-permute-start | bytes 6291464 | tf_op jit(solution)/shard_map/ppermute | solution.py:18
  352.7 46.1 %reduce-scatter.30.cloned.1.call-start = ((), (), s32[]{:S(2)}) async-start(), calls=%async_computation.21 | async-start | bytes 786432 | tf_op jit(solution)/shard_map/reduce_scatter | solution.py:85
  386.3 196.5 %reduce-scatter.24.cloned.1.call-start = ((), (), s32[]{:S(2)}) async-start(), calls=%async_computation.18 | async-start | bytes 786432 | tf_op jit(solution)/shard_map/reduce_scatter | solution.py:74
  469.1 49.7 %collective-permute-start.11 = (bf16[2,1024,512]{2,1,0:T(8,128)(2,1)S(1)}, bf16[2,1024,512]{2,1,0:T(8,128)(2,1)S(1)}, u32[]{:S(2)}, u32[]{:S(2)}) collective-permute-start(bf16[2,1024,512]{2,1,0:T(8,128)(2,1)S(1)} %select_convert_fusion.2), channel_id=1, source_target_pairs={{0,4},{1,5},{2,6},{3,7},{4,0},{5,1},{6,2},{7,3},{8,12},{9,13},{10,... | collective-permute-start | bytes 6291464 | tf_op jit(solution)/shard_map/ppermute | solution.py:18
  523.4 26.4 %collective-permute-start.12 = (bf16[2,512,512]{2,1,0:T(8,128)(2,1)}, bf16[2,512,512]{2,1,0:T(8,128)(2,1)}, u32[]{:S(2)}, u32[]{:S(2)}) collective-permute-start(bf16[2,512,512]{2,1,0:T(8,128)(2,1)} %select_convert_fusion.5), channel_id=1, source_target_pairs={{0,2},{1,3},{2,0},{3,1},{4,6},{5,7},{6,4},{7,5},{8,10},{9,11},{10,... | collective-permute-start | bytes 3145736 | tf_op jit(solution)/shard_map/ppermute | solution.py:18
  534.9 67.1 %reduce-scatter.32.cloned.1.call-start = ((), (), s32[]{:S(2)}) async-start(), calls=%async_computation.22 | async-start | bytes 786432 | tf_op jit(solution)/shard_map/reduce_scatter | solution.py:85
  582.7 197.7 %reduce-scatter.26.cloned.1.call-start = ((), (), s32[]{:S(2)}) async-start(), calls=%async_computation.19 | async-start | bytes 786432 | tf_op jit(solution)/shard_map/reduce_scatter | solution.py:74
  637.8 26.4 %collective-permute-start.9 = (bf16[2,512,512]{2,1,0:T(8,128)(2,1)S(1)}, bf16[2,512,512]{2,1,0:T(8,128)(2,1)S(1)}, u32[]{:S(2)}, u32[]{:S(2)}) collective-permute-start(bf16[2,512,512]{2,1,0:T(8,128)(2,1)S(1)} %maximum_select_fusion.8), channel_id=1, source_target_pairs={{0,2},{1,3},{2,0},{3,1},{4,6},{5,7},{6,4},{7,5},{8,10},{9,11},{10,... | collective-permute-start | bytes 3145736 | tf_op jit(solution)/shard_map/ppermute | solution.py:18
  666.1 63.6 %collective-permute-start.10 = (bf16[2,1024,512]{2,1,0:T(8,128)(2,1)}, bf16[2,1024,512]{2,1,0:T(8,128)(2,1)}, u32[]{:S(2)}, u32[]{:S(2)}) collective-permute-start(bf16[2,1024,512]{2,1,0:T(8,128)(2,1)} %maximum_select_fusion.5), channel_id=1, source_target_pairs={{0,4},{1,5},{2,6},{3,7},{4,0},{5,1},{6,2},{7,3},{8,12},{9,13},{10,... | collective-permute-start | bytes 6291464 | tf_op jit(solution)/shard_map/ppermute | solution.py:18
  671.8 54.4 %collective-permute-start.14 = (bf16[2,128,1024]{2,1,0:T(8,128)(2,1)S(1)}, bf16[2,128,1024]{2,1,0:T(8,128)(2,1)S(1)}, u32[]{:S(2)}, u32[]{:S(2)}) collective-permute-start(bf16[2,128,1024]{2,1,0:T(8,128)(2,1)S(1)} %pad_maximum_fusion.20), channel_id=1, source_target_pairs={{64,0},{65,1},{66,2},{67,3},{68,4},{69,5},{70,6},{71,7},{72,8},{73... | collective-permute-start | bytes 1572872 | tf_op jit(solution)/shard_map/ppermute | solution.py:24
  767.6 46.0 %reduce-scatter.34.cloned.1.call-start = ((), (), s32[]{:S(2)}) async-start(), calls=%async_computation.23 | async-start | bytes 786432 | tf_op jit(solution)/shard_map/reduce_scatter | solution.py:85
  801.8 202.6 %reduce-scatter.36.cloned.1.call-start = ((), (), s32[]{:S(2)}) async-start(), calls=%async_computation.24 | async-start | bytes 786432 | tf_op jit(solution)/shard_map/reduce_scatter | solution.py:85
  882.4 49.3 %collective-permute-start.15 = (bf16[2,1024,512]{2,1,0:T(8,128)(2,1)S(1)}, bf16[2,1024,512]{2,1,0:T(8,128)(2,1)S(1)}, u32[]{:S(2)}, u32[]{:S(2)}) collective-permute-start(bf16[2,1024,512]{2,1,0:T(8,128)(2,1)S(1)} %select_convert_fusion.1), channel_id=1, source_target_pairs={{0,4},{1,5},{2,6},{3,7},{4,0},{5,1},{6,2},{7,3},{8,12},{9,13},{10,... | collective-permute-start | bytes 6291464 | tf_op jit(solution)/shard_map/ppermute | solution.py:18
  936.2 26.7 %collective-permute-start.16 = (bf16[2,512,512]{2,1,0:T(8,128)(2,1)}, bf16[2,512,512]{2,1,0:T(8,128)(2,1)}, u32[]{:S(2)}, u32[]{:S(2)}) collective-permute-start(bf16[2,512,512]{2,1,0:T(8,128)(2,1)} %select_convert_fusion.4), channel_id=1, source_target_pairs={{0,2},{1,3},{2,0},{3,1},{4,6},{5,7},{6,4},{7,5},{8,10},{9,11},{10,... | collective-permute-start | bytes 3145736 | tf_op jit(solution)/shard_map/ppermute | solution.py:18
  992.8 64.0 %reduce-scatter.38.cloned.1.call-start = ((), (), s32[]{:S(2)}) async-start(), calls=%async_computation.25 | async-start | bytes 786432 | tf_op jit(solution)/shard_map/reduce_scatter | solution.py:85
  1009.5 16.2 collective-permute-start.18
  1033.9 251.0 %reduce-scatter.28.cloned.1.call-start = ((), (), s32[]{:S(2)}) async-start(), calls=%async_computation.20 | async-start | bytes 786432 | tf_op jit(solution)/shard_map/reduce_scatter | solution.py:74
  1126.5 49.8 %collective-permute-start.19 = (bf16[2,1024,512]{2,1,0:T(8,128)(2,1)}, bf16[2,1024,512]{2,1,0:T(8,128)(2,1)}, u32[]{:S(2)}, u32[]{:S(2)}) collective-permute-start(bf16[2,1024,512]{2,1,0:T(8,128)(2,1)} %select_convert_fusion), channel_id=1, source_target_pairs={{0,4},{1,5},{2,6},{3,7},{4,0},{5,1},{6,2},{7,3},{8,12},{9,13},{10,... | collective-permute-start | bytes 6291464 | tf_op jit(solution)/shard_map/ppermute | solution.py:18
  1135.7 286.7 %reduce-scatter.44.cloned.1.call-start = ((), (), s32[]{:S(2)}) async-start(), calls=%async_computation.28 | async-start | bytes 1081344 | tf_op jit(solution)/shard_map/reduce_scatter | solution.py:386
  1182.2 26.6 %collective-permute-start.20 = (bf16[2,512,512]{2,1,0:T(8,128)(2,1)}, bf16[2,512,512]{2,1,0:T(8,128)(2,1)}, u32[]{:S(2)}, u32[]{:S(2)}) collective-permute-start(bf16[2,512,512]{2,1,0:T(8,128)(2,1)} %select_convert_fusion.3), channel_id=1, source_target_pairs={{0,2},{1,3},{2,0},{3,1},{4,6},{5,7},{6,4},{7,5},{8,10},{9,11},{10,... | collective-permute-start | bytes 3145736 | tf_op jit(solution)/shard_map/ppermute | solution.py:18
  1195.4 228.4 %reduce-scatter.40.cloned.1.call-start = ((), (), s32[]{:S(2)}) async-start(), calls=%async_computation.26 | async-start | bytes 786432 | tf_op jit(solution)/shard_map/reduce_scatter | solution.py:85
  1237.8 359.6 %reduce-scatter.42.cloned.1.call-start = ((), (), s32[]{:S(2)}) async-start(), calls=%async_computation.27 | async-start | bytes 3244032 | tf_op jit(solution)/shard_map/reduce_scatter | solution.py:383
  1246.1 529.3 %reduce-scatter.46.cloned.1.call-start = ((), (), s32[]{:S(2)}) async-start(), calls=%async_computation.29 | async-start | bytes 5947392 | tf_op jit(solution)/shard_map/reduce_scatter | solution.py:389
  (160 other events, 2506.2 us)
Sparse Core Ops, SparseCore 0:
  154.8 12.1 reduce-scatter.17
  179.9 11.8 reduce-scatter.19
  352.9 12.4 reduce-scatter.21
  386.4 12.4 reduce-scatter.29
  535.1 9.8 reduce-scatter.23
  582.8 11.6 reduce-scatter.31
  767.7 10.4 reduce-scatter.25
  801.9 10.4 reduce-scatter.33
  993.0 11.3 reduce-scatter.35
  1034.0 11.8 reduce-scatter.37
  1135.8 9.1 reduce-scatter.27
  1195.5 184.7 reduce-scatter.43
  1382.6 5.3 reduce-scatter.39
  1390.4 191.8 reduce-scatter.41
  1584.5 190.8 reduce-scatter.45
where the time goes:
time: 1790 us; the launch traced here: 1780 us
  waiting for transfers between devices  684 us (38%)
  blocking collectives  309 us (17%)
  matrix products  296 us (17%)
  other arithmetic  226 us (13%)
  local copies, waits for them, and re-layouts  190 us (11%)
  starting transfers between devices  62.8 us (4%)
    ppermute x18, waiting for transfers between devices, swapped(): return lax.ppermute(value, axis, pairs)  386 us
    reduce_scatter x1, waiting for transfers between devices, per_device(): lax.psum_scatter(weight_sums[2].astype(jnp.bfloat16), 'dp', scatter_dimen...  176 us
    psum x1, blocking collectives, per_device(): gain_total = lax.psum(gain_sums, ('tensor', 'dp'))  168 us
    unnamed x1, blocking collectives  113 us
    ppermute x4, waiting for transfers between devices, passed_along(): lax.ppermute(value, axis, [(source, source + steps) for source in range(f...  87.4 us
    ppermute x18, starting transfers between devices, swapped(): return lax.ppermute(value, axis, pairs)  48.3 us
    dot_general x6, matrix products, score_block(): jnp.einsum('qhd,khd->hqk', queries, keys_all, preferred_element_type=jnp....  43.8 us
    dot_general x3, matrix products, backward_block(): jnp.einsum('qhd,khd->hqk', grad_attended, values_all, preferred_element_t...  42.9 us
  transfers between devices with their start and end apart: 40, of which 27 were waited for; matrix products, arithmetic and copies ran while one was open for 20% of the time, Pallas kernels for 0%

commit v1 on v0

v1 whole, which is shorter than its diff:
```python
import functools

import jax
import jax.numpy as jnp
from jax import lax
from jax.experimental import pallas as pl
from jax.experimental.pallas import tpu as pltpu
from jax.sharding import PartitionSpec as P

HD = 64
LEN = 2048
RING = 4
BLOCK = 128
PAIR = 2 * HD
EPSILON = 1e-06
NEGATIVE = -1e30
KEYS = 256
QUERIES = 512
VMEM = 56 * 1024 * 1024
BF = jnp.bfloat16
F32 = jnp.float32


def along(kind, shift):
    pairs = []
    for index in range(32):
        y, z, x = index // 8, index // 4 % 2, index % 4
        if kind == "x":
            x = (x + shift) % 4
        elif kind == "y":
            y = (y + shift) % 4
        else:
            z = (z + shift) % 2
        pairs.append((index, y * 8 + z * 4 + x))
    return pairs


def moved(value, kind, shift):
    return lax.ppermute(value, "dp", along(kind, shift))


def swapped(value):
    return lax.ppermute(value, "tensor", [(0, 1), (1, 0)])


def rms_scale(hidden):
    return lax.rsqrt(jnp.mean(hidden * hidden, axis=-1, keepdims=True) + EPSILON)


def norm_backward(hidden, grad_normed, gain_row):
    scale_row = rms_scale(hidden)
    unit = hidden * scale_row
    weighted = grad_normed * gain_row
    grad_hidden = scale_row * (weighted - unit * jnp.mean(weighted * unit, axis=-1, keepdims=True))
    return (grad_hidden, jnp.sum(grad_normed * unit, axis=0))


def rotary_tables():
    places = jnp.arange(LEN, dtype=jnp.int32).astype(F32)
    half = HD // 2
    freqs = 10000.0 ** (-jnp.arange(half, dtype=F32) / half)
    angles = places[:, None] * freqs[None, :]
    return (jnp.tile(jnp.cos(angles), (1, 4)), jnp.tile(jnp.sin(angles), (1, 4)))


def low_lanes(shape):
    return lax.broadcasted_iota(jnp.int32, shape, 1) % HD < HD // 2


def turned(u, cosine, sine, sign):
    ahead = pltpu.roll(u, PAIR - HD // 2, 1)
    behind = pltpu.roll(u, HD // 2, 1)
    cross = jnp.where(low_lanes(u.shape), -sign * ahead, sign * behind)
    return u * cosine + cross * sine


def place_block(source, part):
    return (source, 4 + source, 15 - source, 11 - source)[part]


def project_kernel(x_ref, mix_ref, h_ref, gain_ref, w_ref, v1_ref, cos_ref, sin_ref,
                   m0, m1, m2, m3, n_ref, v_ref):
    step = pl.program_id(0)

    @pl.when(step == 0)
    def _():
        h = h_ref[...].astype(F32)
        n_ref[...] = (h * rms_scale(h) * gain_ref[...]).astype(BF)

    normed = n_ref[...]
    cosine, sine = cos_ref[...], sin_ref[...]
    query = jnp.dot(normed, w_ref[0], preferred_element_type=F32)
    query = (turned(query, cosine, sine, 1.0) * HD ** (-0.5)).astype(BF)
    key = jnp.dot(normed, w_ref[1], preferred_element_type=F32)
    key = turned(key, cosine, sine, 1.0).astype(BF)
    value = jnp.dot(normed, w_ref[2], preferred_element_type=F32)
    value = (mix_ref[0] * value + mix_ref[1] * v1_ref[0].astype(F32)).astype(BF)
    v_ref[0] = value
    for index, out in enumerate((m0, m1, m2, m3)):
        @pl.when(step == index)
        def _():
            out[0] = query
            out[1] = key
            out[2] = value


def project(x_index, mix, hidden, gain, w_qkv, value_first, cosine, sine):
    rows, width = hidden.shape
    message = jax.ShapeDtypeStruct((3, rows, PAIR), BF)
    whole = lambda *shape: pl.BlockSpec(shape, lambda i, x: (0,) * len(shape))
    return pl.pallas_call(
        project_kernel,
        grid_spec=pltpu.PrefetchScalarGridSpec(
            num_scalar_prefetch=1,
            grid=(RING,),
            in_specs=[
                pl.BlockSpec(memory_space=pltpu.SMEM),
                whole(rows, width),
                whole(1, width),
                pl.BlockSpec((3, width, PAIR), lambda i, x: (0, 0, (i + x[0]) % RING)),
                pl.BlockSpec((1, rows, PAIR), lambda i, x: (i, 0, 0)),
                whole(rows, PAIR),
                whole(rows, PAIR),
            ],
            out_specs=[whole(3, rows, PAIR)] * 4
            + [whole(rows, width), pl.BlockSpec((1, rows, PAIR), lambda i, x: (i, 0, 0))],
        ),
        out_shape=[message] * 4
        + [jax.ShapeDtypeStruct((rows, width), BF), jax.ShapeDtypeStruct((RING, rows, PAIR), BF)],
        compiler_params=pltpu.CompilerParams(vmem_limit_bytes=VMEM),
        cost_estimate=pl.CostEstimate(
            flops=2 * rows * width * 12 * PAIR, bytes_accessed=8 * 1024 * 1024, transcendentals=0
        ),
        name="project",
    )(x_index, mix, hidden, gain, w_qkv, value_first, cosine, sine)


def first_visible(ends_ref, places):
    start = jnp.zeros_like(places)
    for index in range(4):
        start = jnp.where(places >= ends_ref[index], ends_ref[index], start)
    return start


def attend_kernel(x_ref, ends_ref, m0, m1, m2, m3, o0, o1, o2, o3, lse_ref, out_t, keys, query_t,
                  value_t, acc):
    x = x_ref[0]
    lanes = lax.broadcasted_iota(jnp.int32, (BLOCK, PAIR), 1)
    for shift, message in enumerate((m0, m1, m2, m3)):
        source = lax.rem(x + RING - shift, RING)
        for part in range(4):
            at = pl.ds(pl.multiple_of(place_block(source, part) * BLOCK, BLOCK), BLOCK)
            inside = slice(part * BLOCK, (part + 1) * BLOCK)
            block = message[1, inside, :]
            keys[0, at, :] = jnp.where(lanes < HD, block, jnp.zeros_like(block))
            keys[1, at, :] = jnp.where(lanes < HD, jnp.zeros_like(block), block)
            query_t[:, at] = message[0, inside, :].T
            value_t[:, at] = message[2, inside, :].T

    def one_query_block(qi, _):
        q_at = pl.ds(pl.multiple_of(qi * QUERIES, QUERIES), QUERIES)
        places = qi * QUERIES + lax.broadcasted_iota(jnp.int32, (1, QUERIES), 1)
        start = first_visible(ends_ref, places)
        acc[...] = jnp.zeros_like(acc)

        def one_key_block(kj, carry):
            k_at = pl.ds(pl.multiple_of(kj * KEYS, KEYS), KEYS)
            key_places = kj * KEYS + lax.broadcasted_iota(jnp.int32, (KEYS, QUERIES), 0)
            visible = (key_places <= places) & (key_places >= start)
            after = []
            for head in range(2):
                highest, total = carry[head]
                scores = jnp.dot(keys[head, k_at, :], query_t[:, q_at], preferred_element_type=F32)
                scores = jnp.where(visible, scores, NEGATIVE)
                higher = jnp.maximum(highest, jnp.max(scores, axis=0, keepdims=True))
                shrink = jnp.exp(highest - higher)
                weight = jnp.exp(scores - higher)
                total = total * shrink + jnp.sum(weight, axis=0, keepdims=True)
                part = slice(head * HD, (head + 1) * HD)
                acc[part, :] = acc[part, :] * shrink + jnp.dot(
                    value_t[part, k_at], weight.astype(BF), preferred_element_type=F32
                )
                after.append((higher, total))
            return tuple(after)

        begin = (jnp.full((1, QUERIES), NEGATIVE, F32), jnp.zeros((1, QUERIES), F32))
        done = lax.fori_loop(0, (qi + 1) * (QUERIES // KEYS), one_key_block, (begin, begin))
        for head in range(2):
            highest, total = done[head]
            part = slice(head * HD, (head + 1) * HD)
            out_t[part, q_at] = acc[part, :] / total
            lse_ref[head : head + 1, q_at] = highest + jnp.log(total)
        return 0

    lax.fori_loop(0, LEN // QUERIES, one_query_block, 0)
    for shift, out in enumerate((o0, o1, o2, o3)):
        source = lax.rem(x + RING - shift, RING)
        for part in range(4):
            at = pl.ds(pl.multiple_of(place_block(source, part) * BLOCK, BLOCK), BLOCK)
            out[part * BLOCK : (part + 1) * BLOCK, :] = out_t[:, at].T.astype(BF)


def attend(x_index, ends, messages):
    rows = messages[0].shape[1]
    smem = pl.BlockSpec(memory_space=pltpu.SMEM)
    vmem = pl.BlockSpec(memory_space=pltpu.VMEM)
    return pl.pallas_call(
        attend_kernel,
        in_specs=[smem, smem] + [vmem] * 4,
        out_specs=[vmem] * 6,
        out_shape=[jax.ShapeDtypeStruct((rows, PAIR), BF)] * 4
        + [jax.ShapeDtypeStruct((2, LEN), F32), jax.ShapeDtypeStruct((PAIR, LEN), F32)],
        scratch_shapes=[
            pltpu.VMEM((2, LEN, PAIR), BF),
            pltpu.VMEM((PAIR, LEN), BF),
            pltpu.VMEM((PAIR, LEN), BF),
            pltpu.VMEM((PAIR, QUERIES), F32),
        ],
        compiler_params=pltpu.CompilerParams(vmem_limit_bytes=VMEM),
        cost_estimate=pl.CostEstimate(
            flops=8 * LEN * LEN * HD, bytes_accessed=4 * 1024 * 1024, transcendentals=LEN * LEN
        ),
        name="attend",
    )(x_index, ends, *messages)


def attend_back_kernel(x_ref, ends_ref, mix_ref, m0, m1, m2, m3, d0, d1, d2, d3, lse_ref, out_t,
                       dv1_ref, cos_ref, sin_ref, g0, g1, g2, g3, keys, values, queries, grads,
                       key_t, query_t, grad_t, delta, grad_k, grad_v, grad_q_t):
    x = x_ref[0]
    lanes = lax.broadcasted_iota(jnp.int32, (BLOCK, PAIR), 1)
    for shift, (message, arrived) in enumerate(((m0, d0), (m1, d1), (m2, d2), (m3, d3))):
        source = lax.rem(x + RING - shift, RING)
        for part in range(4):
            at = pl.ds(pl.multiple_of(place_block(source, part) * BLOCK, BLOCK), BLOCK)
            inside = slice(part * BLOCK, (part + 1) * BLOCK)
            query, key, value = message[0, inside, :], message[1, inside, :], message[2, inside, :]
            grad = arrived[inside, :]
            zero = jnp.zeros_like(query)
            for both, block in ((keys, key), (values, value), (queries, query), (grads, grad)):
                both[0, at, :] = jnp.where(lanes < HD, block, zero)
                both[1, at, :] = jnp.where(lanes < HD, zero, block)
            key_t[:, at] = key.T
            query_t[:, at] = query.T
            turned_grad = grad.T
            grad_t[:, at] = turned_grad
            product = out_t[:, at] * turned_grad.astype(F32)
            delta[0:1, at] = jnp.sum(product[:HD], axis=0, keepdims=True)
            delta[1:2, at] = jnp.sum(product[HD:], axis=0, keepdims=True)
    grad_k[...] = jnp.zeros_like(grad_k)
    grad_v[...] = jnp.zeros_like(grad_v)
    grad_q_t[...] = jnp.zeros_like(grad_q_t)

    def one_query_block(qi, _):
        q_at = pl.ds(pl.multiple_of(qi * QUERIES, QUERIES), QUERIES)
        places = qi * QUERIES + lax.broadcasted_iota(jnp.int32, (1, QUERIES), 1)
        start = first_visible(ends_ref, places)

        def one_key_block(kj, carry):
            k_at = pl.ds(pl.multiple_of(kj * KEYS, KEYS), KEYS)
            key_places = kj * KEYS + lax.broadcasted_iota(jnp.int32, (KEYS, QUERIES), 0)
            visible = (key_places <= places) & (key_places >= start)
            for head in range(2):
                part = slice(head * HD, (head + 1) * HD)
                scores = jnp.dot(keys[head, k_at, :], query_t[:, q_at], preferred_element_type=F32)
                scores = jnp.where(visible, scores, NEGATIVE)
                weight = jnp.exp(scores - lse_ref[head : head + 1, q_at])
                grad_w = jnp.dot(values[head, k_at, :], grad_t[:, q_at], preferred_element_type=F32)
                grad_s = (weight * (grad_w - delta[head : head + 1, q_at])).astype(BF)
                grad_v[k_at, :] += jnp.dot(
                    weight.astype(BF), grads[head, q_at, :], preferred_element_type=F32
                )
                grad_k[k_at, :] += jnp.dot(grad_s, queries[head, q_at, :], preferred_element_type=F32)
                grad_q_t[part, q_at] += jnp.dot(
                    key_t[part, k_at], grad_s, preferred_element_type=F32
                )
            return carry

        return lax.fori_loop(0, (qi + 1) * (QUERIES // KEYS), one_key_block, 0)

    lax.fori_loop(0, LEN // QUERIES, one_query_block, 0)
    for shift, out in enumerate((g0, g1, g2, g3)):
        source = lax.rem(x + RING - shift, RING)
        for part in range(4):
            at = pl.ds(pl.multiple_of(place_block(source, part) * BLOCK, BLOCK), BLOCK)
            inside = slice(part * BLOCK, (part + 1) * BLOCK)
            cosine, sine = cos_ref[at, :], sin_ref[at, :]
            grad_q = grad_q_t[:, at].T * HD ** (-0.5)
            out[0, inside, :] = turned(grad_q, cosine, sine, -1.0).astype(BF)
            out[1, inside, :] = turned(grad_k[at, :], cosine, sine, -1.0).astype(BF)
            out[2, inside, :] = (
                mix_ref[0] * grad_v[at, :] + mix_ref[1] * dv1_ref[shift, inside, :].astype(F32)
            ).astype(BF)


def attend_back(x_index, ends, mix, messages, arrived, lse, out_t, dv1, cosine, sine):
    rows = messages[0].shape[1]
    smem = pl.BlockSpec(memory_space=pltpu.SMEM)
    vmem = pl.BlockSpec(memory_space=pltpu.VMEM)
    return pl.pallas_call(
        attend_back_kernel,
        in_specs=[smem] * 3 + [vmem] * 13,
        out_specs=[vmem] * 4,
        out_shape=[jax.ShapeDtypeStruct((3, rows, PAIR), BF)] * 4,
        scratch_shapes=[pltpu.VMEM((2, LEN, PAIR), BF)] * 4
        + [pltpu.VMEM((PAIR, LEN), BF)] * 3
        + [
            pltpu.VMEM((2, LEN), F32),
            pltpu.VMEM((LEN, PAIR), F32),
            pltpu.VMEM((LEN, PAIR), F32),
            pltpu.VMEM((PAIR, LEN), F32),
        ],
        compiler_params=pltpu.CompilerParams(vmem_limit_bytes=VMEM),
        cost_estimate=pl.CostEstimate(
            flops=20 * LEN * LEN * HD, bytes_accessed=8 * 1024 * 1024, transcendentals=LEN * LEN
        ),
        name="attend_back",
    )(x_index, ends, mix, *messages, *arrived, lse, out_t, dv1, cosine, sine)


def out_and_back(values, sign):
    return [values[0]] + [moved(values[shift], "x", sign * shift) for shift in range(1, RING)]


def per_device(tokens, cotangent, doc_lengths, gains, wqkv, wo, wgu, wd):
    first = lax.axis_index("section") == 0
    tensor = lax.axis_index("tensor")
    position = lax.axis_index("dp")
    y, z, x = position // 8, position // 4 % 2, position % 4
    x_index = x.astype(jnp.int32).reshape(1)
    width = tokens.shape[2]

    def held_and_got(pair):
        keep = lax.dynamic_index_in_dim(pair, z, 0, keepdims=False)
        send = lax.dynamic_index_in_dim(pair, 1 - z, 0, keepdims=False)
        got = moved(send.astype(BF), "z", 1).astype(pair.dtype)
        return jnp.where(z == 0, jnp.stack([keep, got]), jnp.stack([got, keep]))

    def both_cores(rows):
        other = swapped(rows)
        return jnp.where(
            tensor == 0, jnp.concatenate([rows, other]), jnp.concatenate([other, rows])
        )

    def own_half(full):
        half = full.shape[0] // 2
        return lax.dynamic_slice_in_dim(full, tensor * half, half, 0)

    lens = lax.dynamic_slice(doc_lengths, (z, y, 0), (1, 1, 4))
    ends = jnp.cumsum(lens.reshape(4), dtype=jnp.int32)
    cosine, sine = rotary_tables()
    blocks = [place_block(x, part) for part in range(4)]
    own_cos, own_sin = [
        jnp.concatenate([lax.dynamic_slice_in_dim(table, b * BLOCK, BLOCK, 0) for b in blocks])
        for table in (cosine, sine)
    ]
    w_qkv = jnp.transpose(wqkv[0], (1, 0, 2))
    w_out = jnp.concatenate(
        [lax.dynamic_slice_in_dim(wo[0], (x + k) % 4 * PAIR, PAIR, 0) for k in range(RING)]
    )
    w_gate, w_up = wgu[0, :, 0], wgu[0, :, 1]
    w_down = wd[0]
    gain_one, gain_two = gains[0, 0:1], gains[0, 1:2]
    mix = jnp.where(first, jnp.array([1.0, 0.0], F32), jnp.array([0.5, 0.5], F32))
    mix_back = jnp.where(first, jnp.array([1.0, 1.0], F32), jnp.array([0.5, 0.0], F32))

    def forward(hidden, value_first):
        *messages, normed, value = project(
            x_index, mix, hidden, gain_one, w_qkv, value_first, own_cos, own_sin
        )
        messages = out_and_back(messages, 1)
        *outs, lse, out_t = attend(x_index, ends, messages)
        attended = jnp.concatenate(out_and_back(outs, -1), axis=1)
        branch = jnp.dot(attended, w_out, preferred_element_type=F32).astype(BF)
        middle = hidden.astype(F32) + (branch.astype(F32) + swapped(branch).astype(F32))
        normed_two = (middle * rms_scale(middle) * gain_two).astype(BF)
        gate = jnp.dot(normed_two, w_gate, preferred_element_type=F32)
        up = jnp.dot(normed_two, w_up, preferred_element_type=F32)
        activated = (jax.nn.silu(gate) * up).astype(BF)
        feed = jnp.dot(activated, w_down, preferred_element_type=F32).astype(BF)
        result = middle + (feed.astype(F32) + swapped(feed).astype(F32))
        saved = (hidden, normed, messages, lse, out_t, attended, middle, normed_two, gate, up, activated)
        return (result.astype(BF), value, saved)

    def backward(grad_out, grad_value_first, saved):
        hidden, normed, messages, lse, out_t, attended, middle, normed_two, gate, up, activated = saved
        hidden = hidden.astype(F32)
        grad_feed = grad_out.astype(BF)
        grad_act = jnp.einsum("td,fd->tf", grad_feed, w_down, preferred_element_type=F32)
        sigma = jax.nn.sigmoid(gate)
        grad_gate = (grad_act * up * sigma * (1.0 + gate * (1.0 - sigma))).astype(BF)
        grad_up = (grad_act * gate * sigma).astype(BF)
        part = (
            jnp.einsum("tf,df->td", grad_gate, w_gate, preferred_element_type=F32)
            + jnp.einsum("tf,df->td", grad_up, w_up, preferred_element_type=F32)
        ).astype(BF)
        grad_normed_two = part.astype(F32) + swapped(part).astype(F32)
        grad_mid, gain_grad_two = norm_backward(middle, grad_normed_two, gain_two)
        grad_middle = grad_out.astype(F32) + grad_mid
        grad_branch = grad_middle.astype(BF)
        grad_attended = jnp.einsum("td,fd->tf", grad_branch, w_out, preferred_element_type=F32)
        grad_attended = grad_attended.astype(BF)
        arrived = out_and_back([grad_attended[:, k * PAIR : (k + 1) * PAIR] for k in range(RING)], 1)
        grads = attend_back(
            x_index, ends, mix_back, messages, arrived, lse, out_t, grad_value_first, cosine, sine
        )
        grad_value_send = jnp.stack([grad[2] for grad in grads])
        grads = out_and_back(grads, -1)
        grad_proj = [
            jnp.concatenate([grads[k][c] for k in range(RING)], axis=1) for c in range(3)
        ]
        w_rel = [
            jnp.concatenate(
                [
                    lax.dynamic_slice_in_dim(w_qkv[c], (x + k) % 4 * PAIR, PAIR, 1)
                    for k in range(RING)
                ],
                axis=1,
            )
            for c in range(3)
        ]
        part = sum(
            jnp.einsum("tf,df->td", grad_proj[c], w_rel[c], preferred_element_type=F32)
            for c in range(3)
        ).astype(BF)
        grad_normed = part.astype(F32) + swapped(part).astype(F32)
        grad_in, gain_grad_one = norm_backward(hidden, grad_normed, gain_one)
        grad_hidden = grad_middle + grad_in
        terms = (grad_feed, grad_gate, grad_up, grad_branch, grad_proj)
        return (grad_hidden, grad_value_send, terms, jnp.stack([gain_grad_one, gain_grad_two]))

    def summed(part, order):
        axes = ["y", "z", "x"]
        place = {"y": y, "z": z, "x": x}
        size = {"y": 4, "z": 2, "x": 4}
        current = part
        for kind in order:
            at = axes.index(kind)
            axes.remove(kind)
            n = size[kind]
            pick = lambda s: lax.dynamic_index_in_dim(
                current, (place[kind] + s) % n, at, keepdims=False
            )
            total = pick(0).astype(F32)
            for s in range(1, n):
                total = total + moved(pick(s), kind, s).astype(F32)
            current = total.astype(BF) if axes else total
        return current

    def summed_gains(total):
        for kind, n in (("x", 4), ("y", 4), ("z", 2)):
            total = sum([total] + [moved(total, kind, s) for s in range(1, n)])
        return total

    own_rows = both_cores(held_and_got(tokens).reshape(2 * BLOCK, width))
    top_grad = both_cores(held_and_got(cotangent).reshape(2 * BLOCK, width))
    no_value = jnp.zeros((RING, 4 * BLOCK, PAIR), BF)

    def handed(value, pairs):
        return lax.ppermute(value, "section", pairs)

    result, value, _ = forward(own_rows, no_value)
    h_in = both_cores(handed(own_half(result), [(0, 1)]))
    v_in = handed(value, [(0, 1)])
    hidden = jnp.where(first, own_rows, h_in)
    result, _, saved = forward(hidden, v_in)
    acts = held_and_got(own_half(result).reshape(2, BLOCK, width))[None]

    grad_hidden, grad_value, _, _ = backward(top_grad, no_value, saved)
    g_in = both_cores(handed(own_half(grad_hidden).astype(BF), [(1, 0)]))
    gv_in = handed(grad_value, [(1, 0)])
    grad_out = jnp.where(first, g_in, top_grad)
    grad_hidden, _, terms, gain_terms = backward(grad_out, gv_in, saved)
    dins = held_and_got(own_half(grad_hidden).reshape(2, BLOCK, width))[None]

    normed, attended, normed_two, activated = saved[1], saved[5], saved[7], saved[10]
    grad_feed, grad_gate, grad_up, grad_branch, grad_proj = terms

    def term(left, right):
        return jnp.einsum("tf,td->fd", left, right, preferred_element_type=F32).astype(BF)

    def cut(whole):
        return whole.reshape(4, 2, 4, whole.shape[0] // 32, whole.shape[1])

    def unrolled(blocks_rel, axis):
        return jnp.concatenate(
            [
                lax.dynamic_index_in_dim(blocks_rel, (b - x) % 4, 0, keepdims=False)
                for b in range(RING)
            ],
            axis=axis,
        )

    down = summed(cut(term(activated, grad_feed)), "yzx")
    gate_share = summed(cut(term(normed_two, grad_gate)), "yxz")
    up_share = summed(cut(term(normed_two, grad_up)), "xyz")
    out_rel = term(attended, grad_branch).reshape(RING, PAIR, width)
    out_share = summed(cut(unrolled(out_rel, 0)), "yxz")
    qkv_shares = []
    for c in range(3):
        full = term(normed, grad_proj[c])
        rel = jnp.stack([full[:, k * PAIR : (k + 1) * PAIR] for k in range(RING)])
        qkv_shares.append(summed(cut(unrolled(rel, 1)), ("yxz", "xyz", "xyz")[c]))
    gain_total = summed_gains(gain_terms)
    return (
        acts,
        dins,
        jnp.stack(qkv_shares, axis=1)[None],
        out_share[None],
        jnp.stack([gate_share, up_share], axis=1)[None],
        down[None],
        gain_total[None],
    )


def solution(mesh):
    placed = (
        P(None, ("tensor", "dp"), None),
        P(None, ("tensor", "dp"), None),
        P(),
        P("section", None, None),
        P("section", None, None, "tensor"),
        P("section", "tensor", None),
        P("section", None, None, "tensor"),
        P("section", "tensor", None),
    )
    return jax.shard_map(
        per_device,
        mesh=mesh,
        in_specs=placed,
        out_specs=(
            P("section", None, ("tensor", "dp"), None),
            P("section", None, ("tensor", "dp"), None),
            P("section", "dp", None, "tensor"),
            P("section", ("tensor", "dp"), None),
            P("section", "dp", None, "tensor"),
            P("section", ("tensor", "dp"), None),
            P("section", None, None),
        ),
        check_vma=False,
    )
```

time: 1790 us -> 665 us (0.37)
  waiting for transfers between devices: 684 us -> 266 us
  blocking collectives: 309 us -> 0 us
  matrix products: 296 us -> 57.3 us
  other arithmetic: 226 us -> 30.2 us
  local copies, waits for them, and re-layouts: 190 us -> 64.8 us
  Pallas kernels: 0 us -> 102 us
  starting transfers between devices: 62.8 us -> 134 us
    dot_general x57 -> x28, matrix products: 296 us -> 57.3 us  [the longest x7 13.2 us: term(): jnp.einsum('tf,td->fd', left, right, preferred_element_type=F32).astype(BF)]
    reduce_scatter x15 -> x0, waiting for transfers between devices: 208 us -> none  [the longest x1 176 us: per_device(): lax.psum_scatter(weight_sums[2].astype(jnp.bfloat16), 'dp', scatter_dimen...]
    ppermute x22 -> x100, waiting for transfers between devices: 474 us -> 266 us  [the longest x84 221 us: moved(): return lax.ppermute(value, 'dp', along(kind, shift))]
    psum x1 -> x0, blocking collectives: 168 us -> none  [per_device(): gain_total = lax.psum(gain_sums, ('tensor', 'dp'))]
    unnamed x1 -> x0, blocking collectives: 113 us -> none
    pallas_call x0 -> x6, Pallas kernels: none -> 102 us  [the longest x2 46.2 us: attend_back(): pl.pallas_call(attend_back_kernel, in_specs=[smem] * 3 + [vmem] * 13, out...]
    ppermute x22 -> x100, starting transfers between devices: 58.1 us -> 134 us  [the longest x84 121 us: moved(): return lax.ppermute(value, 'dp', along(kind, shift))]
    slice x32 -> x9, local copies, waits for them, and re-layouts: 89.4 us -> 15.4 us  [the longest x1 9.29 us: per_device(): w_gate, w_up = (wgu[0, :, 0], wgu[0, :, 1])]
  transfers between devices with their start and end apart: 40 -> 100, of which waited for: 27 -> 48; matrix products, arithmetic and copies ran while one was open for 20% -> 10% of each run, Pallas kernels for 0% -> 4%
where the time goes in v1:
time: 665 us; the launch traced here: 658 us
  waiting for transfers between devices  266 us (40%)
  starting transfers between devices  134 us (20%)
  Pallas kernels  102 us (15%)
  local copies, waits for them, and re-layouts  64.8 us (10%)
  matrix products  57.3 us (9%)
  other arithmetic  30.2 us (5%)
    ppermute x84, waiting for transfers between devices, moved(): return lax.ppermute(value, 'dp', along(kind, shift))  221 us
    ppermute x84, starting transfers between devices, moved(): return lax.ppermute(value, 'dp', along(kind, shift))  121 us
    pallas_call x2, Pallas kernels, attend_back(): pl.pallas_call(attend_back_kernel, in_specs=[smem] * 3 + [vmem] * 13, out...  46.2 us
    pallas_call x2, Pallas kernels, attend(): pl.pallas_call(attend_kernel, in_specs=[smem, smem] + [vmem] * 4, out_spe...  39.7 us
    ppermute x4, waiting for transfers between devices, handed(): return lax.ppermute(value, 'section', pairs)  36.6 us
    pallas_call x2, Pallas kernels, project(): pl.pallas_call(project_kernel, grid_spec=pltpu.PrefetchScalarGridSpec(num...  16.4 us
    unnamed x198, local copies, waits for them, and re-layouts  15 us
  transfers between devices with their start and end apart: 100, of which 48 were waited for; matrix products, arithmetic and copies ran while one was open for 10% of the time, Pallas kernels for 4%

profile of v1, /device:TPU:0, one launch (start us, length us, event | category | flops | bytes accessed | tf_op | source)
XLA Modules:
  0.0 657.7 jit_solution(11025309172382676187)
XLA Ops:
  22.4 8.2 %project.2 = (bf16[3,512,128]{2,1,0:T(8,128)(2,1)}, bf16[3,512,128]{2,1,0:T(8,128)(2,1)}, bf16[3,512,128]{2,1,0:T(8,128)(2,1)}, bf16[3,512,128]{2,1,0:T(8,128)(2...) custom-call(s32[1]{0:T(128)} %bitcast.3.x_ref, f32[2]{0:T(128)} %broadcast_select_fusion.1.mix_ref, ...), custom_call_target="tpu_custom_call" | custom-call | flops 1610612736 | bytes 8388608 | tf_op jit(solution)/shard_map/project/pallas_call | solution.py:111
  37.7 5.9 collective-permute-done.2.m1
  43.6 9.5 %collective-permute-done.3.m2 = bf16[3,512,128]{2,1,0:T(8,128)(2,1)} collective-permute-done((bf16[3,512,128]{2,1,0:T(8,128)(2,1)}, bf16[3,512,128]{2,1,0:T(8,128)(2,1)}, u32[]{:S(2)}, u32[]{:S(2)}) %collective-permute-start.3) | collective-permute-done | bytes 393248 | tf_op jit(solution)/shard_map/ppermute | solution.py:39
  53.1 19.9 %attend.2 = (bf16[512,128]{1,0:T(8,128)(2,1)}, bf16[512,128]{1,0:T(8,128)(2,1)}, bf16[512,128]{1,0:T(8,128)(2,1)}, bf16[512,128]{1,0:T(8,128)(2,1)}, f32[2,2048]{1,0:T(2,128)}, /*index=5*/f32[128,2048]{1,0:T(8,128)}) custom-call(s32[1]{0:T(128)} %bitcast.3.x_ref, s32[4]{0:T(128)} %bitcast.474, bf16[3,512,128]{2,1,0:T(8,128)(2,1)} %get-tuple-element.35.m0, ...), custom_call_target="tpu_custom_call" | custom-call | flops 2147483648 | bytes 4194304 | tf_op jit(solution)/shard_map/attend/pallas_call | solution.py:207
  85.9 9.3 %fusion.137 = (bf16[1,1024,1,1408]{3,2,1,0:T(2,128)(2,1)}, bf16[1,1024,1,1408]{3,2,1,0:T(2,128)(2,1)}) fusion(bf16[1,1024,2,1408]{3,2,1,0:T(2,128)(2,1)S(1)} %bitcast.419), kind=kLoop, calls=%fused_computation.397 | loop fusion | bytes 11534336 | tf_op jit(solution)/shard_map/slice | solution.py:361
  95.2 6.9 %copy_bitcast_fusion = (bf16[1024,1408]{1,0:T(8,128)(2,1)}, bf16[1024,1408]{1,0:T(8,128)(2,1)S(1)}) fusion(bf16[1,1024,1,1408]{3,2,1,0:T(2,128)(2,1)} %get-tuple-element.101, bf16[1,1024,1,1408]{3,2,1,0:T(2,128)(2,1)} %get-tuple-element.100), kind=kLoop, calls=%fused_computation.8 | loop fusion | bytes 11534336 | tf_op jit(solution)/shard_map/squeeze | solution.py:361
  107.2 7.8 %fusion.15 = bf16[512,1024]{1,0:T(8,128)(2,1)} fusion(bf16[1,1408,1024]{2,1,0:T(8,128)(2,1)S(1)} %copy-done, bf16[1024,1408]{1,0:T(8,128)(2,1)} %get-tuple-element.253, f32[512,1408]{1,0:T(8,128)} %fusion.132, f32[512,1024]{1,0:T(8,128)} %copy-done.9, f32[1024]{0:T(1024)S(1)} %bitcast.462, f32[512]{0:T(512)S(1)} %add_rsqrt_fusion.2), kind=kOutput, calls=%fused_computation.53 | convolution fusion | flops 2959212544 | bytes 11802624 | tf_op jit(solution)/shard_map/dot_general | solution.py:380
  122.8 11.7 %collective-permute-done.10 = bf16[256,1024]{1,0:T(8,128)(2,1)S(1)} collective-permute-done((bf16[256,1024]{1,0:T(8,128)(2,1)S(1)}, bf16[256,1024]{1,0:T(8,128)(2,1)S(1)}, u32[]{:S(2)}, u32[]{:S(2)}) %collective-permute-start.10) | collective-permute-done | bytes 524320 | tf_op jit(solution)/shard_map/ppermute | solution.py:460
  140.4 10.3 %collective-permute-done.12.v1_ref = bf16[4,512,128]{2,1,0:T(8,128)(2,1)S(1)} collective-permute-done((bf16[4,512,128]{2,1,0:T(8,128)(2,1)S(1)}, bf16[4,512,128]{2,1,0:T(8,128)(2,1)S(1)}, u32[]{:S(2)}, u32[]{:S(2)}) %collective-permute-start.12) | collective-permute-done | bytes 524320 | tf_op jit(solution)/shard_map/ppermute | solution.py:460
  151.5 8.2 %project.3 = (bf16[3,512,128]{2,1,0:T(8,128)(2,1)}, bf16[3,512,128]{2,1,0:T(8,128)(2,1)}, bf16[3,512,128]{2,1,0:T(8,128)(2,1)}, bf16[3,512,128]{2,1,0:T(8,128)(2...) custom-call(s32[1]{0:T(128)} %bitcast.3.x_ref, f32[2]{0:T(128)} %broadcast_select_fusion.1.mix_ref, ...), custom_call_target="tpu_custom_call" | custom-call | flops 1610612736 | bytes 8388608 | tf_op jit(solution)/shard_map/project/pallas_call | solution.py:111
  163.0 17.4 %collective-permute-done.13.m1 = bf16[3,512,128]{2,1,0:T(8,128)(2,1)S(1)} collective-permute-done((bf16[3,512,128]{2,1,0:T(8,128)(2,1)}, bf16[3,512,128]{2,1,0:T(8,128)(2,1)S(1)}, u32[]{:S(2)}, u32[]{:S(2)}) %collective-permute-start.13) | collective-permute-done | bytes 393248 | tf_op jit(solution)/shard_map/ppermute | solution.py:39
  181.8 19.8 %attend.3 = (bf16[512,128]{1,0:T(8,128)(2,1)}, bf16[512,128]{1,0:T(8,128)(2,1)}, bf16[512,128]{1,0:T(8,128)(2,1)}, bf16[512,128]{1,0:T(8,128)(2,1)}, f32[2,2048]{1,0:T(2,128)}, /*index=5*/f32[128,2048]{1,0:T(8,128)}) custom-call(s32[1]{0:T(128)} %bitcast.3.x_ref, s32[4]{0:T(128)} %bitcast.475, bf16[3,512,128]{2,1,0:T(8,128)(2,1)} %get-tuple-element.44.m0, ...), custom_call_target="tpu_custom_call" | custom-call | flops 2147483648 | bytes 4194304 | tf_op jit(solution)/shard_map/attend/pallas_call | solution.py:207
  244.0 4.9 collective-permute-done.25.d1
  250.2 23.1 %attend_back.2 = (bf16[3,512,128]{2,1,0:T(8,128)(2,1)}, bf16[3,512,128]{2,1,0:T(8,128)(2,1)}, bf16[3,512,128]{2,1,0:T(8,128)(2,1)}, bf16[3,512,128]{2,1,0:T(8,128)(2,1)}) custom-call(s32[1]{0:T(128)} %bitcast.3.x_ref, s32[4]{0:T(128)} %bitcast.476, f32[2]{0:T(128)} %broadcast_select_fusion.mix_ref, bf16[3,512,128]{2,1,0:T(8,128)(2,1)} %get-tuple-element.44.m0, ...), custom_call_target="tpu_custom_call" | custom-call | flops 5368709120 | bytes 8388608 | tf_op jit(solution)/shard_map/attend_back/pallas_call | solution.py:300
  278.4 14.3 %collective-permute-done.28 = bf16[3,512,128]{2,1,0:T(8,128)(2,1)S(1)} collective-permute-done((bf16[3,512,128]{2,1,0:T(8,128)(2,1)}, bf16[3,512,128]{2,1,0:T(8,128)(2,1)S(1)}, u32[]{:S(2)}, u32[]{:S(2)}) %collective-permute-start.28) | collective-permute-done | bytes 393248 | tf_op jit(solution)/shard_map/ppermute | solution.py:39
  292.7 4.8 collective-permute-done.30
  306.7 14.7 %collective-permute-done.32 = bf16[256,1024]{1,0:T(8,128)(2,1)} collective-permute-done((bf16[256,1024]{1,0:T(8,128)(2,1)S(1)}, bf16[256,1024]{1,0:T(8,128)(2,1)}, u32[]{:S(2)}, u32[]{:S(2)}) %collective-permute-start.32) | collective-permute-done | bytes 524320 | tf_op jit(solution)/shard_map/ppermute | solution.py:460
  325.4 7.7 %multiply_convert_fusion = (bf16[512,1408]{1,0:T(8,128)(2,1)}, bf16[512,1408]{1,0:T(8,128)(2,1)S(1)}, bf16[512,1408]{1,0:T(8,128)(2,1)S(1)}) fusion(f32[512,1408]{1,0:T(8,128)} %copy-done.91, f32[512,1408]{1,0:T(8,128)} %copy-done.90, bf16[1,1408,1024]{2,1,0:T(8,128)(2,1)S(1)} %copy-done, bf16[256,1024]{1,0:T(8,128)(2,1)} %collective-permute-done.33, ...), kind=kOutput, calls=%fused_computation.18 | convolution fusion | flops 1497890816 | bytes 15073282 | tf_op jit(solution)/shard_map/td,fd->tf/dot_general | solution.py:389
  342.6 4.8 convolution_convert_fusion
  347.5 5.2 reshape.397
  370.7 4.8 collective-permute-done.86
  377.1 28.5 %collective-permute-done.72 = bf16[2,4,32,1408]{3,2,0,1:T(8,128)(2,1)S(1)} collective-permute-done((bf16[2,4,32,1408]{3,2,0,1:T(8,128)(2,1)S(1)}, bf16[2,4,32,1408]{3,2,0,1:T(8,128)(2,1)S(1)}, u32[]{:S(2)}, u32[]{:S(2)}) %collective-permute-start.72) | collective-permute-done | bytes 720928 | tf_op jit(solution)/shard_map/ppermute | solution.py:39
  405.6 16.7 %collective-permute-done.73 = bf16[2,4,32,1408]{3,2,0,1:T(8,128)(2,1)S(1)} collective-permute-done((bf16[2,4,32,1408]{3,2,0,1:T(8,128)(2,1)S(1)}, bf16[2,4,32,1408]{3,2,0,1:T(8,128)(2,1)S(1)}, u32[]{:S(2)}, u32[]{:S(2)}) %collective-permute-start.73) | collective-permute-done | bytes 720928 | tf_op jit(solution)/shard_map/ppermute | solution.py:39
  429.2 13.7 %collective-permute-done.80 = bf16[4,2,32,1408]{3,2,1,0:T(8,128)(2,1)S(1)} collective-permute-done((bf16[4,2,32,1408]{3,2,1,0:T(8,128)(2,1)S(1)}, bf16[4,2,32,1408]{3,2,1,0:T(8,128)(2,1)S(1)}, u32[]{:S(2)}, u32[]{:S(2)}) %collective-permute-start.80) | collective-permute-done | bytes 720928 | tf_op jit(solution)/shard_map/ppermute | solution.py:39
  443.4 13.1 %collective-permute-done.81 = bf16[4,2,32,1408]{3,2,1,0:T(8,128)(2,1)S(1)} collective-permute-done((bf16[4,2,32,1408]{3,2,1,0:T(8,128)(2,1)S(1)}, bf16[4,2,32,1408]{3,2,1,0:T(8,128)(2,1)S(1)}, u32[]{:S(2)}, u32[]{:S(2)}) %collective-permute-start.81) | collective-permute-done | bytes 720928 | tf_op jit(solution)/shard_map/ppermute | solution.py:39
  463.1 7.7 %collective-permute-done.82 = bf16[2,32,1408]{2,1,0:T(8,128)(2,1)S(1)} collective-permute-done((bf16[2,32,1408]{2,1,0:T(8,128)(2,1)S(1)}, bf16[2,32,1408]{2,1,0:T(8,128)(2,1)S(1)}, u32[]{:S(2)}, u32[]{:S(2)}) %collective-permute-start.82) | collective-permute-done | bytes 180256 | tf_op jit(solution)/shard_map/ppermute | solution.py:39
  474.6 11.2 %collective-permute-done.78 = bf16[32,1408]{1,0:T(8,128)(2,1)S(1)} collective-permute-done((bf16[32,1408]{1,0:T(8,128)(2,1)S(1)}, bf16[32,1408]{1,0:T(8,128)(2,1)S(1)}, u32[]{:S(2)}, u32[]{:S(2)}) %collective-permute-start.78) | collective-permute-done | bytes 90144 | tf_op jit(solution)/shard_map/ppermute | solution.py:39
  500.1 4.5 collective-permute-start.91
  518.4 23.1 %attend_back.3 = (bf16[3,512,128]{2,1,0:T(8,128)(2,1)}, bf16[3,512,128]{2,1,0:T(8,128)(2,1)}, bf16[3,512,128]{2,1,0:T(8,128)(2,1)}, bf16[3,512,128]{2,1,0:T(8,128)(2,1)}) custom-call(s32[1]{0:T(128)} %bitcast.3.x_ref, s32[4]{0:T(128)} %bitcast.477, f32[2]{0:T(128)} %broadcast_select_fusion.mix_ref, bf16[3,512,128]{2,1,0:T(8,128)(2,1)} %get-tuple-element.44.m0, ...), custom_call_target="tpu_custom_call" | custom-call | flops 5368709120 | bytes 8388608 | tf_op jit(solution)/shard_map/attend_back/pallas_call | solution.py:300
  549.1 5.5 collective-permute-done.68
  581.3 8.9 %collective-permute-done.44 = bf16[2,4,32,512]{3,2,1,0:T(8,128)(2,1)S(1)} collective-permute-done((bf16[2,4,32,512]{3,2,1,0:T(8,128)(2,1)S(1)}, bf16[2,4,32,512]{3,2,1,0:T(8,128)(2,1)S(1)}, u32[]{:S(2)}, u32[]{:S(2)}) %collective-permute-start.44) | collective-permute-done | bytes 262176 | tf_op jit(solution)/shard_map/ppermute | solution.py:39
  596.0 5.0 collective-permute-done.52
  (544 shorter events, 297.4 us)
Async XLA Ops:
  32.1 21.0 %collective-permute-start.3 = (bf16[3,512,128]{2,1,0:T(8,128)(2,1)}, bf16[3,512,128]{2,1,0:T(8,128)(2,1)}, u32[]{:S(2)}, u32[]{:S(2)}) collective-permute-start(bf16[3,512,128]{2,1,0:T(8,128)(2,1)} %get-tuple-element.37), channel_id=1, source_target_pairs={{0,2},{1,3},{2,0},{3,1},{4,6},{5,7},{6,4},{7,5},{8,10},{9,11},{10,... | collective-permute-start | bytes 1179656 | tf_op jit(solution)/shard_map/ppermute | solution.py:39
  34.8 18.2 %collective-permute-start.4 = (bf16[3,512,128]{2,1,0:T(8,128)(2,1)}, bf16[3,512,128]{2,1,0:T(8,128)(2,1)}, u32[]{:S(2)}, u32[]{:S(2)}) collective-permute-start(bf16[3,512,128]{2,1,0:T(8,128)(2,1)} %get-tuple-element.38), channel_id=1, source_target_pairs={{0,3},{1,0},{2,1},{3,2},{4,7},{5,4},{6,5},{7,6},{8,11},{9,8},{10,9... | collective-permute-start | bytes 1179656 | tf_op jit(solution)/shard_map/ppermute | solution.py:39
  85.6 16.5 %collective-permute-start.8 = (bf16[512,1024]{1,0:T(8,128)(2,1)S(1)}, bf16[512,1024]{1,0:T(8,128)(2,1)S(1)}, u32[]{:S(2)}, u32[]{:S(2)}) collective-permute-start(bf16[512,1024]{1,0:T(8,128)(2,1)S(1)} %convolution_convert_fusion.8), channel_id=1, source_target_pairs={{0,32},{32,0},{1,33},{33,1},{2,34},{34,2},{3,35},{35,3},{4,36},{36... | collective-permute-start | bytes 3145736 | tf_op jit(solution)/shard_map/ppermute | solution.py:43
  134.5 16.2 %collective-permute-start.12 = (bf16[4,512,128]{2,1,0:T(8,128)(2,1)S(1)}, bf16[4,512,128]{2,1,0:T(8,128)(2,1)S(1)}, u32[]{:S(2)}, u32[]{:S(2)}) collective-permute-start(bf16[4,512,128]{2,1,0:T(8,128)(2,1)S(1)} %copy-done.72), channel_id=1, source_target_pairs={{0,64},{1,65},{2,66},{3,67},{4,68},{5,69},{6,70},{7,71},{8,72},{9,... | collective-permute-start | bytes 1572872 | tf_op jit(solution)/shard_map/ppermute | solution.py:460
  159.8 20.6 %collective-permute-start.13 = (bf16[3,512,128]{2,1,0:T(8,128)(2,1)}, bf16[3,512,128]{2,1,0:T(8,128)(2,1)S(1)}, u32[]{:S(2)}, u32[]{:S(2)}) collective-permute-start(bf16[3,512,128]{2,1,0:T(8,128)(2,1)} %get-tuple-element.45), channel_id=1, source_target_pairs={{0,1},{1,2},{2,3},{3,0},{4,5},{5,6},{6,7},{7,4},{8,9},{9,10},{10,1... | collective-permute-start | bytes 1179656 | tf_op jit(solution)/shard_map/ppermute | solution.py:39
  159.8 20.6 %collective-permute-start.14 = (bf16[3,512,128]{2,1,0:T(8,128)(2,1)}, bf16[3,512,128]{2,1,0:T(8,128)(2,1)S(1)}, u32[]{:S(2)}, u32[]{:S(2)}) collective-permute-start(bf16[3,512,128]{2,1,0:T(8,128)(2,1)} %get-tuple-element.46), channel_id=1, source_target_pairs={{0,2},{1,3},{2,0},{3,1},{4,6},{5,7},{6,4},{7,5},{8,10},{9,11},{10,... | collective-permute-start | bytes 1179656 | tf_op jit(solution)/shard_map/ppermute | solution.py:39
  162.0 19.0 %collective-permute-start.15 = (bf16[3,512,128]{2,1,0:T(8,128)(2,1)}, bf16[3,512,128]{2,1,0:T(8,128)(2,1)S(1)}, u32[]{:S(2)}, u32[]{:S(2)}) collective-permute-start(bf16[3,512,128]{2,1,0:T(8,128)(2,1)} %get-tuple-element.47), channel_id=1, source_target_pairs={{0,3},{1,0},{2,1},{3,2},{4,7},{5,4},{6,5},{7,6},{8,11},{9,8},{10,9... | collective-permute-start | bytes 1179656 | tf_op jit(solution)/shard_map/ppermute | solution.py:39
  273.3 19.3 %collective-permute-start.28 = (bf16[3,512,128]{2,1,0:T(8,128)(2,1)}, bf16[3,512,128]{2,1,0:T(8,128)(2,1)S(1)}, u32[]{:S(2)}, u32[]{:S(2)}) collective-permute-start(bf16[3,512,128]{2,1,0:T(8,128)(2,1)} %get-tuple-element.55), channel_id=1, source_target_pairs={{0,3},{1,0},{2,1},{3,2},{4,7},{5,4},{6,5},{7,6},{8,11},{9,8},{10,9... | collective-permute-start | bytes 1179656 | tf_op jit(solution)/shard_map/ppermute | solution.py:39
  277.4 20.1 %collective-permute-start.30 = (bf16[3,512,128]{2,1,0:T(8,128)(2,1)S(1)}, bf16[3,512,128]{2,1,0:T(8,128)(2,1)S(1)}, u32[]{:S(2)}, u32[]{:S(2)}) collective-permute-start(bf16[3,512,128]{2,1,0:T(8,128)(2,1)S(1)} %copy-done.67), channel_id=1, source_target_pairs={{0,1},{1,2},{2,3},{3,0},{4,5},{5,6},{6,7},{7,4},{8,9},{9,10},{10,1... | collective-permute-start | bytes 1179656 | tf_op jit(solution)/shard_map/ppermute | solution.py:39
  355.1 20.4 %collective-permute-start.86 = (bf16[2,4,44,1024]{3,1,2,0:T(4,128)(2,1)S(1)}, bf16[2,4,44,1024]{3,1,2,0:T(4,128)(2,1)S(1)}, u32[]{:S(2)}, u32[]{:S(2)}) collective-permute-start(bf16[2,4,44,1024]{3,1,2,0:T(4,128)(2,1)S(1)} %bitcast.456), channel_id=1, source_target_pairs={{0,8},{1,9},{2,10},{3,11},{4,12},{5,13},{6,14},{7,15},{8,16},{9,17... | collective-permute-start | bytes 2162696 | tf_op jit(solution)/shard_map/ppermute | solution.py:39
  357.3 67.1 %collective-permute-start.87 = (bf16[2,4,44,1024]{3,1,2,0:T(4,128)(2,1)S(1)}, bf16[2,4,44,1024]{3,1,2,0:T(4,128)(2,1)S(1)}, u32[]{:S(2)}, u32[]{:S(2)}) collective-permute-start(bf16[2,4,44,1024]{3,1,2,0:T(4,128)(2,1)S(1)} %bitcast.455), channel_id=1, source_target_pairs={{0,16},{1,17},{2,18},{3,19},{4,20},{5,21},{6,22},{7,23},{8,24},{9,... | collective-permute-start | bytes 2162696 | tf_op jit(solution)/shard_map/ppermute | solution.py:39
  361.2 44.4 %collective-permute-start.72 = (bf16[2,4,32,1408]{3,2,0,1:T(8,128)(2,1)S(1)}, bf16[2,4,32,1408]{3,2,0,1:T(8,128)(2,1)S(1)}, u32[]{:S(2)}, u32[]{:S(2)}) collective-permute-start(bf16[2,4,32,1408]{3,2,0,1:T(8,128)(2,1)S(1)} %bitcast.459), channel_id=1, source_target_pairs={{0,8},{1,9},{2,10},{3,11},{4,12},{5,13},{6,14},{7,15},{8,16},{9,17... | collective-permute-start | bytes 2162696 | tf_op jit(solution)/shard_map/ppermute | solution.py:39
  361.7 60.6 %collective-permute-start.73 = (bf16[2,4,32,1408]{3,2,0,1:T(8,128)(2,1)S(1)}, bf16[2,4,32,1408]{3,2,0,1:T(8,128)(2,1)S(1)}, u32[]{:S(2)}, u32[]{:S(2)}) collective-permute-start(bf16[2,4,32,1408]{3,2,0,1:T(8,128)(2,1)S(1)} %bitcast.458), channel_id=1, source_target_pairs={{0,16},{1,17},{2,18},{3,19},{4,20},{5,21},{6,22},{7,23},{8,24},{9,... | collective-permute-start | bytes 2162696 | tf_op jit(solution)/shard_map/ppermute | solution.py:39
  364.7 58.1 %collective-permute-start.74 = (bf16[2,4,32,1408]{3,2,0,1:T(8,128)(2,1)S(1)}, bf16[2,4,32,1408]{3,2,0,1:T(8,128)(2,1)S(1)}, u32[]{:S(2)}, u32[]{:S(2)}) collective-permute-start(bf16[2,4,32,1408]{3,2,0,1:T(8,128)(2,1)S(1)} %bitcast.457), channel_id=1, source_target_pairs={{0,24},{1,25},{2,26},{3,27},{4,28},{5,29},{6,30},{7,31},{8,0},{9,1... | collective-permute-start | bytes 2162696 | tf_op jit(solution)/shard_map/ppermute | solution.py:39
  375.5 50.8 %collective-permute-start.88 = (bf16[2,4,44,1024]{3,1,2,0:T(4,128)(2,1)S(1)}, bf16[2,4,44,1024]{3,1,2,0:T(4,128)(2,1)S(1)}, u32[]{:S(2)}, u32[]{:S(2)}) collective-permute-start(bf16[2,4,44,1024]{3,1,2,0:T(4,128)(2,1)S(1)} %bitcast.454), channel_id=1, source_target_pairs={{0,24},{1,25},{2,26},{3,27},{4,28},{5,29},{6,30},{7,31},{8,0},{9,1... | collective-permute-start | bytes 2162696 | tf_op jit(solution)/shard_map/ppermute | solution.py:39
  405.6 22.7 %collective-permute-start.79 = (bf16[4,2,32,1408]{3,2,1,0:T(8,128)(2,1)S(1)}, bf16[4,2,32,1408]{3,2,1,0:T(8,128)(2,1)S(1)}, u32[]{:S(2)}, u32[]{:S(2)}) collective-permute-start(bf16[4,2,32,1408]{3,2,1,0:T(8,128)(2,1)S(1)} %get-tuple-element.112), channel_id=1, source_target_pairs={{0,1},{1,2},{2,3},{3,0},{4,5},{5,6},{6,7},{7,4},{8,9},{9,10},{10,1... | collective-permute-start | bytes 2162696 | tf_op jit(solution)/shard_map/ppermute | solution.py:39
  422.3 20.6 %collective-permute-start.80 = (bf16[4,2,32,1408]{3,2,1,0:T(8,128)(2,1)S(1)}, bf16[4,2,32,1408]{3,2,1,0:T(8,128)(2,1)S(1)}, u32[]{:S(2)}, u32[]{:S(2)}) collective-permute-start(bf16[4,2,32,1408]{3,2,1,0:T(8,128)(2,1)S(1)} %get-tuple-element.114), channel_id=1, source_target_pairs={{0,2},{1,3},{2,0},{3,1},{4,6},{5,7},{6,4},{7,5},{8,10},{9,11},{10,... | collective-permute-start | bytes 2162696 | tf_op jit(solution)/shard_map/ppermute | solution.py:39
  422.8 33.7 %collective-permute-start.81 = (bf16[4,2,32,1408]{3,2,1,0:T(8,128)(2,1)S(1)}, bf16[4,2,32,1408]{3,2,1,0:T(8,128)(2,1)S(1)}, u32[]{:S(2)}, u32[]{:S(2)}) collective-permute-start(bf16[4,2,32,1408]{3,2,1,0:T(8,128)(2,1)S(1)} %get-tuple-element.113), channel_id=1, source_target_pairs={{0,3},{1,0},{2,1},{3,2},{4,7},{5,4},{6,5},{7,6},{8,11},{9,8},{10,9... | collective-permute-start | bytes 2162696 | tf_op jit(solution)/shard_map/ppermute | solution.py:39
  425.0 86.3 %collective-permute-start.38 = (bf16[4,512,128]{2,1,0:T(8,128)(2,1)S(1)}, bf16[4,512,128]{2,1,0:T(8,128)(2,1)S(1)}, u32[]{:S(2)}, u32[]{:S(2)}) collective-permute-start(bf16[4,512,128]{2,1,0:T(8,128)(2,1)S(1)} %copy-done.28), channel_id=1, source_target_pairs={{64,0},{65,1},{66,2},{67,3},{68,4},{69,5},{70,6},{71,7},{72,8},{73... | collective-permute-start | bytes 1572872 | tf_op jit(solution)/shard_map/ppermute | solution.py:460
  426.3 66.9 %collective-permute-start.34 = (bf16[512,1024]{1,0:T(8,128)(2,1)S(1)}, bf16[512,1024]{1,0:T(8,128)(2,1)S(1)}, u32[]{:S(2)}, u32[]{:S(2)}) collective-permute-start(bf16[512,1024]{1,0:T(8,128)(2,1)S(1)} %add_convert_fusion.1), channel_id=1, source_target_pairs={{0,32},{32,0},{1,33},{33,1},{2,34},{34,2},{3,35},{35,3},{4,36},{36... | collective-permute-start | bytes 3145736 | tf_op jit(solution)/shard_map/ppermute | solution.py:43
  428.3 31.2 %collective-permute-start.75 = (bf16[2,32,1408]{2,1,0:T(8,128)(2,1)S(1)}, bf16[2,32,1408]{2,1,0:T(8,128)(2,1)S(1)}, u32[]{:S(2)}, u32[]{:S(2)}) collective-permute-start(bf16[2,32,1408]{2,1,0:T(8,128)(2,1)S(1)} %get-tuple-element.180), channel_id=1, source_target_pairs={{0,1},{1,2},{2,3},{3,0},{4,5},{5,6},{6,7},{7,4},{8,9},{9,10},{10,1... | collective-permute-start | bytes 540680 | tf_op jit(solution)/shard_map/ppermute | solution.py:39
  442.9 16.8 %collective-permute-start.76 = (bf16[2,32,1408]{2,1,0:T(8,128)(2,1)S(1)}, bf16[2,32,1408]{2,1,0:T(8,128)(2,1)S(1)}, u32[]{:S(2)}, u32[]{:S(2)}) collective-permute-start(bf16[2,32,1408]{2,1,0:T(8,128)(2,1)S(1)} %get-tuple-element.182), channel_id=1, source_target_pairs={{0,2},{1,3},{2,0},{3,1},{4,6},{5,7},{6,4},{7,5},{8,10},{9,11},{10,... | collective-permute-start | bytes 540680 | tf_op jit(solution)/shard_map/ppermute | solution.py:39
  470.8 28.4 %collective-permute-start.20 = (bf16[512,1024]{1,0:T(8,128)(2,1)S(1)}, bf16[512,1024]{1,0:T(8,128)(2,1)S(1)}, u32[]{:S(2)}, u32[]{:S(2)}) collective-permute-start(bf16[512,1024]{1,0:T(8,128)(2,1)S(1)} %copy-done.50), channel_id=1, source_target_pairs={{0,32},{32,0},{1,33},{33,1},{2,34},{34,2},{3,35},{35,3},{4,36},{36... | collective-permute-start | bytes 3145736 | tf_op jit(solution)/shard_map/ppermute | solution.py:43
  470.8 28.8 %collective-permute-start.89 = (bf16[4,44,1024]{2,1,0:T(8,128)(2,1)S(1)}, bf16[4,44,1024]{2,1,0:T(8,128)(2,1)S(1)}, u32[]{:S(2)}, u32[]{:S(2)}) collective-permute-start(bf16[4,44,1024]{2,1,0:T(8,128)(2,1)S(1)} %dynamic-slice_bitcast_fusion.4), channel_id=1, source_target_pairs={{0,4},{1,5},{2,6},{3,7},{4,0},{5,1},{6,2},{7,3},{8,12},{9,13},{10,... | collective-permute-start | bytes 1081352 | tf_op jit(solution)/shard_map/ppermute | solution.py:39
  510.4 33.9 %collective-permute-start.65 = (bf16[2,4,16,1024]{3,2,1,0:T(8,128)(2,1)S(1)}, bf16[2,4,16,1024]{3,2,1,0:T(8,128)(2,1)S(1)}, u32[]{:S(2)}, u32[]{:S(2)}) collective-permute-start(bf16[2,4,16,1024]{3,2,1,0:T(8,128)(2,1)S(1)} %get-tuple-element.116), channel_id=1, source_target_pairs={{0,8},{1,9},{2,10},{3,11},{4,12},{5,13},{6,14},{7,15},{8,16},{9,17... | collective-permute-start | bytes 786440 | tf_op jit(solution)/shard_map/ppermute | solution.py:39
  511.3 32.9 %collective-permute-start.66 = (bf16[2,4,16,1024]{3,2,1,0:T(8,128)(2,1)S(1)}, bf16[2,4,16,1024]{3,2,1,0:T(8,128)(2,1)S(1)}, u32[]{:S(2)}, u32[]{:S(2)}) collective-permute-start(bf16[2,4,16,1024]{3,2,1,0:T(8,128)(2,1)S(1)} %get-tuple-element.118), channel_id=1, source_target_pairs={{0,16},{1,17},{2,18},{3,19},{4,20},{5,21},{6,22},{7,23},{8,24},{9,... | collective-permute-start | bytes 786440 | tf_op jit(solution)/shard_map/ppermute | solution.py:39
  512.2 32.0 %collective-permute-start.67 = (bf16[2,4,16,1024]{3,2,1,0:T(8,128)(2,1)S(1)}, bf16[2,4,16,1024]{3,2,1,0:T(8,128)(2,1)S(1)}, u32[]{:S(2)}, u32[]{:S(2)}) collective-permute-start(bf16[2,4,16,1024]{3,2,1,0:T(8,128)(2,1)S(1)} %get-tuple-element.117), channel_id=1, source_target_pairs={{0,24},{1,25},{2,26},{3,27},{4,28},{5,29},{6,30},{7,31},{8,0},{9,1... | collective-permute-start | bytes 786440 | tf_op jit(solution)/shard_map/ppermute | solution.py:39
  514.7 42.4 %collective-permute-start.21 = (bf16[128,1024]{1,0:T(8,128)(2,1)S(1)}, bf16[128,1024]{1,0:T(8,128)(2,1)}, u32[]{:S(2)}, u32[]{:S(2)}) collective-permute-start(bf16[128,1024]{1,0:T(8,128)(2,1)S(1)} %get-tuple-element.197), channel_id=1, source_target_pairs={{0,4},{1,5},{2,6},{3,7},{4,0},{5,1},{6,2},{7,3},{8,12},{9,13},{10,... | collective-permute-start | bytes 786440 | tf_op jit(solution)/shard_map/ppermute | solution.py:39
  541.5 20.7 %collective-permute-start.39 = (bf16[3,512,128]{2,1,0:T(8,128)(2,1)}, bf16[3,512,128]{2,1,0:T(8,128)(2,1)S(1)}, u32[]{:S(2)}, u32[]{:S(2)}) collective-permute-start(bf16[3,512,128]{2,1,0:T(8,128)(2,1)} %get-tuple-element.59), channel_id=1, source_target_pairs={{0,3},{1,0},{2,1},{3,2},{4,7},{5,4},{6,5},{7,6},{8,11},{9,8},{10,9... | collective-permute-start | bytes 1179656 | tf_op jit(solution)/shard_map/ppermute | solution.py:39
  573.8 60.4 %collective-permute-start.42 = (bf16[512,1024]{1,0:T(8,128)(2,1)S(1)}, bf16[512,1024]{1,0:T(8,128)(2,1)S(1)}, u32[]{:S(2)}, u32[]{:S(2)}) collective-permute-start(bf16[512,1024]{1,0:T(8,128)(2,1)S(1)} %add_convert_fusion), channel_id=1, source_target_pairs={{0,32},{32,0},{1,33},{33,1},{2,34},{34,2},{3,35},{35,3},{4,36},{36... | collective-permute-start | bytes 3145736 | tf_op jit(solution)/shard_map/ppermute | solution.py:43
  591.6 18.0 %collective-permute-start.58 = (bf16[4,2,32,512]{3,2,1,0:T(8,128)(2,1)S(1)}, bf16[4,2,32,512]{3,2,1,0:T(8,128)(2,1)S(1)}, u32[]{:S(2)}, u32[]{:S(2)}) collective-permute-start(bf16[4,2,32,512]{3,2,1,0:T(8,128)(2,1)S(1)} %get-tuple-element.145), channel_id=1, source_target_pairs={{0,1},{1,2},{2,3},{3,0},{4,5},{5,6},{6,7},{7,4},{8,9},{9,10},{10,1... | collective-permute-start | bytes 786440 | tf_op jit(solution)/shard_map/ppermute | solution.py:39
  592.6 17.0 %collective-permute-start.59 = (bf16[4,2,32,512]{3,2,1,0:T(8,128)(2,1)S(1)}, bf16[4,2,32,512]{3,2,1,0:T(8,128)(2,1)S(1)}, u32[]{:S(2)}, u32[]{:S(2)}) collective-permute-start(bf16[4,2,32,512]{3,2,1,0:T(8,128)(2,1)S(1)} %get-tuple-element.146), channel_id=1, source_target_pairs={{0,2},{1,3},{2,0},{3,1},{4,6},{5,7},{6,4},{7,5},{8,10},{9,11},{10,... | collective-permute-start | bytes 786440 | tf_op jit(solution)/shard_map/ppermute | solution.py:39
  (165 other events, 1692.2 us)

commit v2 on v1

v2 whole, which is shorter than its diff:
```python
import jax
import jax.numpy as jnp
import numpy as np
from jax import lax
from jax.experimental import pallas as pl
from jax.experimental.pallas import tpu as pltpu
from jax.sharding import PartitionSpec as P

HD = 64
LEN = 2048
RING = 4
BLOCK = 128
PAIR = 2 * HD
EPSILON = 1e-06
NEGATIVE = -1e30
KEYS = 512
QUERIES = 1024
BACK_KEYS = 256
BACK_QUERIES = 512
BF = jnp.bfloat16
F32 = jnp.float32


def along(kind, shift):
    pairs = []
    for index in range(32):
        y, z, x = index // 8, index // 4 % 2, index % 4
        if kind == "x":
            x = (x + shift) % 4
        elif kind == "y":
            y = (y + shift) % 4
        else:
            z = (z + shift) % 2
        pairs.append((index, y * 8 + z * 4 + x))
    return pairs


def moved(value, kind, shift):
    return lax.ppermute(value, "dp", along(kind, shift))


def swapped(value):
    return lax.ppermute(value, "tensor", [(0, 1), (1, 0)])


def rms_scale(hidden):
    return lax.rsqrt(jnp.mean(hidden * hidden, axis=-1, keepdims=True) + EPSILON)


def rotary_tables():
    half = HD // 2
    freqs = np.float32(10000.0) ** (-np.arange(half, dtype=np.float32) / np.float32(half))
    angles = np.arange(LEN, dtype=np.float32)[:, None] * freqs[None, :]
    return [jnp.asarray(np.tile(f(angles).astype(np.float32), (1, 4))) for f in (np.cos, np.sin)]


def low_lanes(shape):
    return lax.broadcasted_iota(jnp.int32, shape, 1) % HD < HD // 2


def turned(u, cosine, sine, sign):
    ahead = pltpu.roll(u, PAIR - HD // 2, 1)
    behind = pltpu.roll(u, HD // 2, 1)
    cross = jnp.where(low_lanes(u.shape), -sign * ahead, sign * behind)
    return u * cosine + cross * sine


def place_block(source, part):
    return (source, 4 + source, 15 - source, 11 - source)[part]


def on_core(kernel, ins, outs, *, scratch=(), smem=0, far=0, waits=(), limit=24, name):
    spots = [pl.BlockSpec(memory_space=pltpu.SMEM)] * smem
    spots += [pl.BlockSpec(memory_space=pltpu.VMEM)] * (len(ins) - smem - far)
    spots += [pl.BlockSpec(memory_space=pltpu.HBM)] * far
    spots += [pl.BlockSpec(memory_space=pl.ANY)] * len(waits)
    taken, given = len(ins), len(outs)

    def body(*refs):
        kernel(*refs[:taken], *refs[taken + len(waits) :])

    return pl.pallas_call(
        body,
        in_specs=spots,
        out_specs=[pl.BlockSpec(memory_space=pltpu.VMEM)] * given,
        out_shape=list(outs),
        scratch_shapes=list(scratch),
        compiler_params=pltpu.CompilerParams(vmem_limit_bytes=limit * 2**20),
        cost_estimate=pl.CostEstimate(flops=1, bytes_accessed=1, transcendentals=0),
        name=name,
    )(*ins, *waits)


def seen(value):
    return value[(0,) * (value.ndim - 2)][:8, :PAIR]


def shaped(*shape, dtype=BF):
    return jax.ShapeDtypeStruct(shape, dtype)


def heads_at(x_ref, shift):
    return pl.ds(pl.multiple_of(lax.rem(x_ref[0] + shift, RING) * PAIR, PAIR), PAIR)


def halves(rows):
    return [slice(0, rows // 2), slice(rows // 2, rows)]


def across(left, right):
    return lax.dot_general(left, right, (((1,), (1,)), ((), ())), preferred_element_type=F32)


def down_rows(left, right):
    return lax.dot_general(left, right, (((0,), (0,)), ((), ())), preferred_element_type=F32)


def own_half(t_ref, rows):
    return pl.ds(pl.multiple_of(t_ref[0] * (rows // 2), rows // 2), rows // 2)


def far_half(t_ref, rows):
    return pl.ds(pl.multiple_of((1 - t_ref[0]) * (rows // 2), rows // 2), rows // 2)


def own_tables(x_ref, table, half):
    blocks = [place_block(x_ref[0], 2 * half + part) for part in range(2)]
    return jnp.concatenate(
        [table[pl.ds(pl.multiple_of(b * BLOCK, BLOCK), BLOCK), :] for b in blocks]
    )


def project_kernel(x_ref, t_ref, mix_ref, own_ref, other_ref, gain_ref, w_ref, v1_ref, cos_ref, sin_ref,
                   m0, m1, m2, m3, n_ref, v_ref, h_ref):
    rows = h_ref.shape[0]
    h_ref[own_half(t_ref, rows), :] = own_ref[...]
    h_ref[far_half(t_ref, rows), :] = other_ref[...]
    for part in halves(rows):
        h = h_ref[part].astype(F32)
        n_ref[part] = (h * rms_scale(h) * gain_ref[...]).astype(BF)
    outs = (m0, m1, m2, m3)
    for pair in ((0, 1), (2, 3)):
        weight = jnp.concatenate(
            [w_ref[c, :, heads_at(x_ref, k)] for k in pair for c in range(3)], axis=1
        )
        for which, part in enumerate(halves(rows)):
            both = jnp.dot(n_ref[part], weight, preferred_element_type=F32)
            cosine, sine = own_tables(x_ref, cos_ref, which), own_tables(x_ref, sin_ref, which)
            for index, k in enumerate(pair):
                query, key, value = [
                    both[:, (3 * index + c) * PAIR : (3 * index + c + 1) * PAIR] for c in range(3)
                ]
                outs[k][0, part] = (turned(query, cosine, sine, 1.0) * HD ** (-0.5)).astype(BF)
                outs[k][1, part] = turned(key, cosine, sine, 1.0).astype(BF)
                value = mix_ref[0] * value + mix_ref[1] * v1_ref[k, part].astype(F32)
                outs[k][2, part] = value.astype(BF)
                v_ref[k, part] = value.astype(BF)


def project(x_index, t_index, mix, own, other, gain, w_qkv, value_first, cosine, sine, waits=()):
    rows, width = 2 * own.shape[0], own.shape[1]
    return on_core(
        project_kernel,
        (x_index, t_index, mix, own, other, gain, w_qkv, value_first, cosine, sine),
        [shaped(3, rows, PAIR)] * 4
        + [shaped(rows, width), shaped(RING, rows, PAIR), shaped(rows, width)],
        smem=3, waits=waits, limit=20, name="project",
    )


def pick_kernel(z_ref, pair_ref, keep_ref, send_ref):
    keep_ref[...] = pair_ref[z_ref[0]]
    send_ref[...] = pair_ref[1 - z_ref[0]]


def pick(z_index, pair, waits=()):
    return on_core(
        pick_kernel, (z_index, pair), [shaped(*pair.shape[1:])] * 2, smem=1, waits=waits, limit=4, name="pick"
    )


def branch_kernel(x_ref, o0, o1, o2, o3, w_ref, v_ref, o_ref, part_ref, copy_ref):
    for k, arrived in enumerate((o0, o1, o2, o3)):
        o_ref[:, heads_at(x_ref, k)] = arrived[...]
    for part in halves(o_ref.shape[0]):
        part_ref[part] = jnp.dot(o_ref[part], w_ref[...], preferred_element_type=F32).astype(BF)
    copy_ref[...] = v_ref[...]


def branch(x_index, arrived, w_out, value, waits=()):
    rows, width = arrived[0].shape[0], w_out.shape[1]
    return on_core(
        branch_kernel,
        (x_index, *arrived, w_out, value),
        [shaped(rows, RING * PAIR), shaped(rows, width), jax.ShapeDtypeStruct(value.shape, BF)],
        smem=1, waits=waits, limit=14, name="branch",
    )


def put_halves(t_ref, which, keep_ref, send_ref, value):
    @pl.when(t_ref[0] == which)
    def _():
        keep_ref[...] = value

    @pl.when(t_ref[0] != which)
    def _():
        send_ref[...] = value


def pieces(units):
    cut = (units // PAIR + 1) // 2 * PAIR
    return [(0, cut), (cut, units)]


def weight_copies(wgu_ref, wd_ref, gu_buf, d_buf, sems):
    copies = []
    for index, (low, high) in enumerate(pieces(wd_ref.shape[0])):
        at = pl.ds(low, high - low)
        copies.append(
            [
                pltpu.make_async_copy(wgu_ref.at[:, :, at], gu_buf.at[:, :, at], sems.at[index, 0]),
                pltpu.make_async_copy(wd_ref.at[at, :], d_buf.at[at, :], sems.at[index, 1]),
            ]
        )
    return copies


def weight_scratch(width, units):
    return [
        pltpu.VMEM((2, width, units), BF),
        pltpu.VMEM((units, width), BF),
        pltpu.SemaphoreType.DMA((2, 2)),
    ]


def feed_kernel(t_ref, h_ref, p_ref, q_ref, gain_ref, wgu_ref, wd_ref,
                m_ref, mine_ref, n_ref, gate_ref, up_ref, act_ref, keep_ref, send_ref,
                gu_buf, d_buf, sems, acc):
    copies = weight_copies(wgu_ref, wd_ref, gu_buf, d_buf, sems)
    for pair in copies:
        for copy in pair:
            copy.start()
    rows = halves(h_ref.shape[0])
    for part in rows:
        middle = h_ref[part].astype(F32) + (p_ref[part].astype(F32) + q_ref[part].astype(F32))
        m_ref[part] = middle
        n_ref[part] = (middle * rms_scale(middle) * gain_ref[...]).astype(BF)
    mine_ref[...] = m_ref[own_half(t_ref, h_ref.shape[0]), :]
    for index, (low, high) in enumerate(pieces(d_buf.shape[0])):
        at = slice(low, high)
        for copy in copies[index]:
            copy.wait()
        for which, part in enumerate(rows):
            gate = jnp.dot(n_ref[part], gu_buf[0, :, at], preferred_element_type=F32)
            up = jnp.dot(n_ref[part], gu_buf[1, :, at], preferred_element_type=F32)
            gate_ref[part, at] = gate.astype(BF)
            up_ref[part, at] = up.astype(BF)
            act = (gate / (1.0 + jnp.exp(-gate)) * up).astype(BF)
            act_ref[part, at] = act
            total = jnp.dot(act, d_buf[at, :], preferred_element_type=F32)
            if index == 0:
                acc[part] = total
            else:
                put_halves(t_ref, which, keep_ref, send_ref, (acc[part] + total).astype(BF))


def feed(t_index, hidden, own, other, gain, w_gu, w_down, waits=()):
    rows, width = hidden.shape
    units = w_down.shape[0]
    wide = shaped(rows, units)
    return on_core(
        feed_kernel,
        (t_index, hidden, own, other, gain, w_gu, w_down),
        [shaped(rows, width, dtype=F32), shaped(rows // 2, width, dtype=F32), shaped(rows, width)]
        + [wide, wide, wide, shaped(rows // 2, width), shaped(rows // 2, width)],
        scratch=weight_scratch(width, units) + [pltpu.VMEM((rows, width), F32)],
        smem=1, far=2, waits=waits, limit=30, name="feed",
    )


def feed_back_kernel(t_ref, own_ref, other_ref, gate_ref, up_ref, wgu_ref, wd_ref,
                     dgate_ref, dup_ref, part_ref, g_ref, gu_buf, d_buf, sems, acc):
    copies = weight_copies(wgu_ref, wd_ref, gu_buf, d_buf, sems)
    for which in (1, 0):
        for pair in copies:
            pair[which].start()
    g_ref[own_half(t_ref, g_ref.shape[0]), :] = own_ref[...]
    g_ref[far_half(t_ref, g_ref.shape[0]), :] = other_ref[...]
    for index, (low, high) in enumerate(pieces(d_buf.shape[0])):
        at = slice(low, high)
        copies[index][1].wait()
        for part in halves(g_ref.shape[0]):
            grad = across(g_ref[part], d_buf[at, :])
            gate = gate_ref[part, at].astype(F32)
            sigma = 1.0 / (1.0 + jnp.exp(-gate))
            up = up_ref[part, at].astype(F32)
            dgate_ref[part, at] = (grad * up * sigma * (1.0 + gate * (1.0 - sigma))).astype(BF)
            dup_ref[part, at] = (grad * gate * sigma).astype(BF)
        copies[index][0].wait()
        for part in halves(g_ref.shape[0]):
            total = across(dgate_ref[part, at], gu_buf[0, :, at]) + across(
                dup_ref[part, at], gu_buf[1, :, at]
            )
            if index == 0:
                acc[part] = total
            else:
                part_ref[part] = (acc[part] + total).astype(BF)


def feed_back(t_index, own, other, w_gu, w_down, gate, up, waits=()):
    rows, width = 2 * own.shape[0], own.shape[1]
    units = w_down.shape[0]
    wide = shaped(rows, units)
    return on_core(
        feed_back_kernel,
        (t_index, own, other, gate, up, w_gu, w_down),
        [wide, wide, shaped(rows, width), shaped(rows, width)],
        scratch=weight_scratch(width, units) + [pltpu.VMEM((rows, width), F32)],
        smem=1, far=2, waits=waits, limit=26, name="feed_back",
    )


def feed_terms_kernel(y_ref, n_ref, g_ref, u_ref, t0, t1, t2, t3):
    size = n_ref.shape[1] // 4
    rows = size // 8
    for k, out in enumerate((t0, t1, t2, t3)):
        at = pl.multiple_of(lax.rem(y_ref[0] + k, 4) * size, size)
        left = n_ref[:, pl.ds(at, size)]
        for spot, right in enumerate((g_ref, u_ref)):
            term = down_rows(left, right[...]).astype(BF)
            for index in range(8):
                out[index, spot * rows : (spot + 1) * rows, :] = term[index * rows : (index + 1) * rows]


def feed_terms(y_index, normed, dgate, dup):
    width, units = normed.shape[1], dgate.shape[1]
    return on_core(
        feed_terms_kernel, (y_index, normed, dgate, dup), [shaped(8, width // 16, units)] * 4,
        smem=1, limit=16, name="feed_terms",
    )


def sum_kernel(*refs):
    total = refs[0][...].astype(F32)
    for ref in refs[1:-1]:
        total += ref[...].astype(F32)
    refs[-1][...] = total.astype(BF)


def summed(values, waits=()):
    shape = values[0].shape
    piece = pl.BlockSpec((shape[0] // 4, *shape[1:]), lambda i: (i, 0, 0))

    def body(*refs):
        sum_kernel(*refs[: len(values)], refs[-1])

    return pl.pallas_call(
        body,
        grid=(4,),
        in_specs=[piece] * len(values) + [pl.BlockSpec(memory_space=pl.ANY)] * len(waits),
        out_specs=piece,
        out_shape=shaped(*shape),
        compiler_params=pltpu.CompilerParams(vmem_limit_bytes=8 * 2**20),
        cost_estimate=pl.CostEstimate(flops=1, bytes_accessed=1, transcendentals=0),
        name="summed",
    )(*values, *waits)


def middle_back_kernel(x_ref, t_ref, g_ref, m_ref, p_ref, q_ref, gain_ref, w_ref,
                       dm_ref, gm_ref, d0, d1, d2, d3, sum_ref, do_ref):
    rows = g_ref.shape[0]
    for which, part in enumerate(halves(rows)):
        grad = p_ref[part].astype(F32) + q_ref[part].astype(F32)
        inner, scale, unit = norm_back(m_ref[part], grad, gain_ref[...])
        middle = g_ref[part].astype(F32) + inner

        @pl.when(t_ref[0] == which)
        def _():
            dm_ref[...] = middle
            sum_ref[...] = jnp.sum(grad * unit, axis=0, keepdims=True)

        gm_ref[part] = middle.astype(BF)
        do_ref[part] = across(gm_ref[part], w_ref[...]).astype(BF)
    for k, out in enumerate((d0, d1, d2, d3)):
        out[...] = do_ref[:, heads_at(x_ref, k)]


def norm_back(hidden, grad, gain):
    scale = rms_scale(hidden)
    unit = hidden * scale
    weighted = grad * gain
    inner = scale * (weighted - unit * jnp.mean(weighted * unit, axis=-1, keepdims=True))
    return inner, scale, unit


def middle_back(x_index, t_index, grad, middle, own, other, gain, w_out, waits=()):
    rows, width = grad.shape
    return on_core(
        middle_back_kernel,
        (x_index, t_index, grad, middle, own, other, gain, w_out),
        [shaped(rows // 2, width, dtype=F32), shaped(rows, width)]
        + [shaped(rows, PAIR)] * 4
        + [shaped(1, width, dtype=F32)],
        scratch=[pltpu.VMEM((rows, RING * PAIR), BF)],
        smem=2, waits=waits, limit=20, name="middle_back",
    )


def project_back_kernel(x_ref, t_ref, g0, g1, g2, g3, w_ref, n_ref, keep_ref, send_ref, half_ref, d_ref):
    for k, grad in enumerate((g0, g1, g2, g3)):
        for c in range(3):
            d_ref[c, :, heads_at(x_ref, k)] = grad[c]
    for which, part in enumerate(halves(d_ref.shape[1])):
        total = sum(across(d_ref[c, part], w_ref[c]) for c in range(3)).astype(BF)
        put_halves(t_ref, which, keep_ref, send_ref, total)
    half_ref[...] = n_ref[own_half(t_ref, n_ref.shape[0]), :]


def project_back(x_index, t_index, grads, w_qkv, normed, waits=()):
    rows, width = normed.shape
    return on_core(
        project_back_kernel,
        (x_index, t_index, *grads, w_qkv, normed),
        [shaped(rows // 2, width)] * 3,
        scratch=[pltpu.VMEM((3, rows, RING * PAIR), BF)],
        smem=2, waits=waits, limit=16, name="project_back",
    )


def input_back_kernel(h_ref, dm_ref, p_ref, q_ref, gain_ref, dh_ref, low_ref):
    grad = p_ref[...].astype(F32) + q_ref[...].astype(F32)
    total = dm_ref[...] + norm_back(h_ref[...].astype(F32), grad, gain_ref[...])[0]
    dh_ref[...] = total
    low_ref[...] = total.astype(BF)


def input_back(hidden, grad_middle, own, other, gain):
    return on_core(
        input_back_kernel, (hidden, grad_middle, own, other, gain),
        [shaped(*hidden.shape, dtype=F32), shaped(*hidden.shape)], limit=10, name="input_back",
    )


def close_kernel(m_ref, p_ref, q_ref, out_ref):
    out_ref[...] = (m_ref[...] + (p_ref[...].astype(F32) + q_ref[...].astype(F32))).astype(BF)


def close(middle, own, other, waits=()):
    return on_core(
        close_kernel, (middle, own, other), [shaped(*own.shape)], waits=waits, limit=6, name="close"
    )[0]


DOWN_ROWS, OUT_AT, QKV_AT = 44, 48, 64


def put_by_z(z_ref, keep_ref, send_ref, device, rows, lanes, value):
    spot = device // 8 * 4 + device % 4
    put_halves(z_ref, device // 4 % 2, keep_ref.at[spot, rows, lanes], send_ref.at[spot, rows, lanes], value)


def early_terms_kernel(z_ref, act_ref, go_ref, o_ref, gm_ref, keep_ref, send_ref, down):
    width = go_ref.shape[1]
    units = act_ref.shape[1]
    for low in range(0, units, 256):
        high = min(low + 256, units)
        down[low:high, :] = down_rows(act_ref[:, low:high], go_ref[...])
    blank = jnp.zeros((OUT_AT - DOWN_ROWS, width), F32)
    everywhere = slice(0, width)
    for at in range(32):
        block = jnp.concatenate([down[at * DOWN_ROWS : (at + 1) * DOWN_ROWS, :], blank])
        put_by_z(z_ref, keep_ref, send_ref, at, slice(0, OUT_AT), everywhere, block.astype(BF))
    rows = o_ref.shape[1] // 32
    for low in range(0, o_ref.shape[1], 256):
        term = down_rows(o_ref[:, low : low + 256], gm_ref[...]).astype(BF)
        for index in range(256 // rows):
            put_by_z(
                z_ref, keep_ref, send_ref, low // rows + index, slice(OUT_AT, QKV_AT), everywhere,
                term[index * rows : (index + 1) * rows],
            )


def early_terms(z_index, act, grad_out, attended, grad_branch):
    width = grad_out.shape[1]
    return on_core(
        early_terms_kernel,
        (z_index, act, grad_out, attended, grad_branch),
        [shaped(16, QKV_AT, width)] * 2,
        scratch=[pltpu.VMEM((act.shape[1], width), F32)],
        smem=1, limit=18, name="early_terms",
    )


def qkv_terms_kernel(x_ref, t_ref, z_ref, n_ref, near_ref, far_ref, g0, g1, g2, g3,
                     w_ref, gain_ref, two_ref, keep_ref, send_ref, sum_ref, acc):
    half = near_ref.shape[1]
    rows, wide = n_ref.shape[1] // 32, 3 * PAIR

    def joined(grad, at):
        return jnp.concatenate([grad[c, at, :] for c in range(3)], axis=1)

    acc[...] = down_rows(joined(g0, slice(None)), n_ref[...])
    for index, grad in enumerate((g1, g2, g3)):
        acc[...] += down_rows(joined(grad, own_half(t_ref, 2 * half)), near_ref[index]) + down_rows(
            joined(grad, far_half(t_ref, 2 * half)), far_ref[index]
        )
    for low in range(0, acc.shape[1], 256):
        term = acc[:, low : low + 256].T.astype(BF)
        for index in range(256 // rows):
            at = low // rows + index
            block = term[index * rows : (index + 1) * rows]
            both = jnp.concatenate([block[: rows // 2], block[rows // 2 :]], axis=1)
            put_by_z(z_ref, keep_ref, send_ref, at, slice(0, rows // 2), slice(0, 2 * wide), both)
        total = jnp.zeros((1, 256), F32)
        for c in range(3):
            weight = w_ref[c, low : low + 256, heads_at(x_ref, 0)].astype(F32).T
            total += jnp.sum(weight * acc[c * PAIR : (c + 1) * PAIR, low : low + 256], axis=0, keepdims=True)
        sum_ref[0:1, low : low + 256] = total / gain_ref[:, low : low + 256]
    sum_ref[1:2, :] = two_ref[...]


def qkv_terms(x_index, t_index, z_index, normed, near, far, grads, w_qkv, gain, gain_sum):
    width = normed.shape[1]
    return on_core(
        qkv_terms_kernel,
        (x_index, t_index, z_index, normed, near, far, *grads, w_qkv, gain, gain_sum),
        [shaped(16, width // 64, 6 * PAIR)] * 2 + [shaped(2, width, dtype=F32)],
        scratch=[pltpu.VMEM((3 * PAIR, width), F32)],
        smem=3, limit=18, name="qkv_terms",
    )


def rest_kernel(a_ref, b_ref, c_ref, d_ref, out_ref):
    wide = c_ref.shape[2]
    out_ref[:, :QKV_AT, :] = (a_ref[...].astype(F32) + b_ref[...].astype(F32)).astype(BF)
    out_ref[:, QKV_AT:, :wide] = (c_ref[...].astype(F32) + d_ref[...].astype(F32)).astype(BF)
    out_ref[:, QKV_AT:, wide:] = jnp.zeros((out_ref.shape[0], out_ref.shape[1] - QKV_AT, out_ref.shape[2] - wide), BF)


def rest_sum(early, early_got, late, late_got, waits=()):
    count, _, width = early.shape
    first = pl.BlockSpec((count // 4, QKV_AT, width), lambda i: (i, 0, 0))
    second = pl.BlockSpec((count // 4, *late.shape[1:]), lambda i: (i, 0, 0))
    total = QKV_AT + late.shape[1]

    def body(*refs):
        rest_kernel(*refs[:4], refs[-1])

    return pl.pallas_call(
        body,
        grid=(4,),
        in_specs=[first, first, second, second] + [pl.BlockSpec(memory_space=pl.ANY)] * len(waits),
        out_specs=pl.BlockSpec((count // 4, total, width), lambda i: (i, 0, 0)),
        out_shape=shaped(count, total, width),
        compiler_params=pltpu.CompilerParams(vmem_limit_bytes=8 * 2**20),
        cost_estimate=pl.CostEstimate(flops=1, bytes_accessed=1, transcendentals=0),
        name="rest_sum",
    )(early, early_got, late, late_got, *waits)


def first_visible(ends_ref, places):
    start = jnp.zeros_like(places)
    for index in range(4):
        start = jnp.where(places >= ends_ref[index], ends_ref[index], start)
    return start


def attend_kernel(x_ref, ends_ref, m0, m1, m2, m3, o0, o1, o2, o3, lse_ref, out_t, keys, query_t,
                  value_t, acc):
    x = x_ref[0]
    lanes = lax.broadcasted_iota(jnp.int32, (BLOCK, PAIR), 1)
    for shift, message in enumerate((m0, m1, m2, m3)):
        source = lax.rem(x + RING - shift, RING)
        for part in range(4):
            at = pl.ds(pl.multiple_of(place_block(source, part) * BLOCK, BLOCK), BLOCK)
            inside = slice(part * BLOCK, (part + 1) * BLOCK)
            block = message[1, inside, :]
            keys[0, at, :] = jnp.where(lanes < HD, block, jnp.zeros_like(block))
            keys[1, at, :] = jnp.where(lanes < HD, jnp.zeros_like(block), block)
            query_t[:, at] = message[0, inside, :].T
            value_t[:, at] = message[2, inside, :].T

    def one_query_block(qi, _):
        q_at = pl.ds(pl.multiple_of(qi * QUERIES, QUERIES), QUERIES)
        places = qi * QUERIES + lax.broadcasted_iota(jnp.int32, (1, QUERIES), 1)
        start = first_visible(ends_ref, places)
        acc[...] = jnp.zeros_like(acc)

        def one_key_block(kj, carry, diagonal):
            k_at = pl.ds(pl.multiple_of(kj * KEYS, KEYS), KEYS)
            key_places = kj * KEYS + lax.broadcasted_iota(jnp.int32, (KEYS, QUERIES), 0)
            visible = key_places >= start
            if diagonal:
                visible = visible & (key_places <= places)
            after = []
            for head in range(2):
                highest, total = carry[head]
                scores = jnp.dot(keys[head, k_at, :], query_t[:, q_at], preferred_element_type=F32)
                scores = jnp.where(visible, scores, NEGATIVE)
                higher = jnp.maximum(highest, jnp.max(scores, axis=0, keepdims=True))
                shrink = jnp.exp(highest - higher)
                weight = jnp.exp(scores - higher)
                total = total * shrink + jnp.sum(weight, axis=0, keepdims=True)
                part = slice(head * HD, (head + 1) * HD)
                acc[part, :] = acc[part, :] * shrink + jnp.dot(
                    value_t[part, k_at], weight.astype(BF), preferred_element_type=F32
                )
                after.append((higher, total))
            return tuple(after)

        begin = (jnp.full((1, QUERIES), NEGATIVE, F32), jnp.zeros((1, QUERIES), F32))
        ratio = QUERIES // KEYS
        done = lax.fori_loop(
            0, qi * ratio, lambda kj, carry: one_key_block(kj, carry, False), (begin, begin)
        )
        for step in range(ratio):
            done = one_key_block(qi * ratio + step, done, True)
        for head in range(2):
            highest, total = done[head]
            part = slice(head * HD, (head + 1) * HD)
            out_t[part, q_at] = acc[part, :] / total
            lse_ref[head : head + 1, q_at] = highest + jnp.log(total)
        return 0

    lax.fori_loop(0, LEN // QUERIES, one_query_block, 0)
    for shift, out in enumerate((o0, o1, o2, o3)):
        source = lax.rem(x + RING - shift, RING)
        for part in range(4):
            at = pl.ds(pl.multiple_of(place_block(source, part) * BLOCK, BLOCK), BLOCK)
            out[part * BLOCK : (part + 1) * BLOCK, :] = out_t[:, at].T.astype(BF)


def attend(x_index, ends, messages, waits=()):
    rows = messages[0].shape[1]
    return on_core(
        attend_kernel,
        (x_index, ends, *messages),
        [shaped(rows, PAIR)] * 4 + [shaped(2, LEN, dtype=F32), shaped(PAIR, LEN, dtype=F32)],
        scratch=[
            pltpu.VMEM((2, LEN, PAIR), BF),
            pltpu.VMEM((PAIR, LEN), BF),
            pltpu.VMEM((PAIR, LEN), BF),
            pltpu.VMEM((PAIR, QUERIES), F32),
        ],
        smem=2, waits=waits, limit=16, name="attend",
    )


def attend_back_kernel(x_ref, ends_ref, mix_ref, m0, m1, m2, m3, d0, d1, d2, d3, lse_ref, out_t,
                       dv1_ref, cos_ref, sin_ref, g0, g1, g2, g3, keys, values, queries, grads,
                       key_t, query_t, grad_t, delta, grad_k, grad_v, grad_q_t):
    x = x_ref[0]
    lanes = lax.broadcasted_iota(jnp.int32, (BLOCK, PAIR), 1)
    for shift, (message, arrived) in enumerate(((m0, d0), (m1, d1), (m2, d2), (m3, d3))):
        source = lax.rem(x + RING - shift, RING)
        for part in range(4):
            at = pl.ds(pl.multiple_of(place_block(source, part) * BLOCK, BLOCK), BLOCK)
            inside = slice(part * BLOCK, (part + 1) * BLOCK)
            query, key, value = message[0, inside, :], message[1, inside, :], message[2, inside, :]
            grad = arrived[inside, :]
            zero = jnp.zeros_like(query)
            for both, block in ((keys, key), (values, value), (queries, query), (grads, grad)):
                both[0, at, :] = jnp.where(lanes < HD, block, zero)
                both[1, at, :] = jnp.where(lanes < HD, zero, block)
            key_t[:, at] = key.T
            query_t[:, at] = query.T
            turned_grad = grad.T
            grad_t[:, at] = turned_grad
            product = out_t[:, at] * turned_grad.astype(F32)
            delta[0:1, at] = jnp.sum(product[:HD], axis=0, keepdims=True)
            delta[1:2, at] = jnp.sum(product[HD:], axis=0, keepdims=True)
    grad_k[...] = jnp.zeros_like(grad_k)
    grad_v[...] = jnp.zeros_like(grad_v)
    grad_q_t[...] = jnp.zeros_like(grad_q_t)

    def one_query_block(qi, _):
        q_at = pl.ds(pl.multiple_of(qi * BACK_QUERIES, BACK_QUERIES), BACK_QUERIES)
        places = qi * BACK_QUERIES + lax.broadcasted_iota(jnp.int32, (1, BACK_QUERIES), 1)
        start = first_visible(ends_ref, places)

        def one_key_block(kj, carry):
            k_at = pl.ds(pl.multiple_of(kj * BACK_KEYS, BACK_KEYS), BACK_KEYS)
            key_places = kj * BACK_KEYS + lax.broadcasted_iota(jnp.int32, (BACK_KEYS, BACK_QUERIES), 0)
            visible = (key_places <= places) & (key_places >= start)
            for head in range(2):
                part = slice(head * HD, (head + 1) * HD)
                scores = jnp.dot(keys[head, k_at, :], query_t[:, q_at], preferred_element_type=F32)
                scores = jnp.where(visible, scores, NEGATIVE)
                weight = jnp.exp(scores - lse_ref[head : head + 1, q_at])
                grad_w = jnp.dot(values[head, k_at, :], grad_t[:, q_at], preferred_element_type=F32)
                grad_s = (weight * (grad_w - delta[head : head + 1, q_at])).astype(BF)
                grad_v[k_at, :] += jnp.dot(
                    weight.astype(BF), grads[head, q_at, :], preferred_element_type=F32
                )
                grad_k[k_at, :] += jnp.dot(grad_s, queries[head, q_at, :], preferred_element_type=F32)
                grad_q_t[part, q_at] += jnp.dot(
                    key_t[part, k_at], grad_s, preferred_element_type=F32
                )
            return carry

        return lax.fori_loop(0, (qi + 1) * (BACK_QUERIES // BACK_KEYS), one_key_block, 0)

    lax.fori_loop(0, LEN // BACK_QUERIES, one_query_block, 0)
    for shift, out in enumerate((g0, g1, g2, g3)):
        source = lax.rem(x + RING - shift, RING)
        for part in range(4):
            at = pl.ds(pl.multiple_of(place_block(source, part) * BLOCK, BLOCK), BLOCK)
            inside = slice(part * BLOCK, (part + 1) * BLOCK)
            cosine, sine = cos_ref[at, :], sin_ref[at, :]
            grad_q = grad_q_t[:, at].T * HD ** (-0.5)
            out[0, inside, :] = turned(grad_q, cosine, sine, -1.0).astype(BF)
            out[1, inside, :] = turned(grad_k[at, :], cosine, sine, -1.0).astype(BF)
            out[2, inside, :] = (
                mix_ref[0] * grad_v[at, :] + mix_ref[1] * dv1_ref[shift, inside, :].astype(F32)
            ).astype(BF)


def attend_back(x_index, ends, mix, messages, arrived, lse, out_t, dv1, cosine, sine, waits=()):
    rows = messages[0].shape[1]
    return on_core(
        attend_back_kernel,
        (x_index, ends, mix, *messages, *arrived, lse, out_t, dv1, cosine, sine),
        [shaped(3, rows, PAIR)] * 4,
        scratch=[pltpu.VMEM((2, LEN, PAIR), BF)] * 4
        + [pltpu.VMEM((PAIR, LEN), BF)] * 3
        + [
            pltpu.VMEM((2, LEN), F32),
            pltpu.VMEM((LEN, PAIR), F32),
            pltpu.VMEM((LEN, PAIR), F32),
            pltpu.VMEM((PAIR, LEN), F32),
        ],
        smem=3, waits=waits, limit=24, name="attend_back",
    )


def out_and_back(values, sign):
    return [values[0]] + [moved(values[shift], "x", sign * shift) for shift in range(1, RING)]


def all_to_all(value, kinds):
    groups = {}
    for index in range(32):
        place = {"y": index // 8, "z": index // 4 % 2, "x": index % 4}
        groups.setdefault(tuple(place[k] for k in "yzx" if k not in kinds), []).append(index)
    return lax.all_to_all(value, "dp", 0, 0, axis_index_groups=list(groups.values()))


def per_device(tokens, cotangent, doc_lengths, gains, wqkv, wo, wgu, wd):
    first = lax.axis_index("section") == 0
    tensor = lax.axis_index("tensor")
    position = lax.axis_index("dp")
    y, z, x = position // 8, position // 4 % 2, position % 4
    x_index, y_index, z_index, t_index = [
        v.astype(jnp.int32).reshape(1) for v in (x, y, z, tensor)
    ]
    width = tokens.shape[2]

    def in_order(keep, got):
        got = got.astype(keep.dtype)
        return jnp.where(z == 0, jnp.stack([keep, got]), jnp.stack([got, keep]))

    def regrouped(pair):
        keep = lax.dynamic_index_in_dim(pair, z, 0, keepdims=False)
        send = lax.dynamic_index_in_dim(pair, 1 - z, 0, keepdims=False)
        return in_order(keep, moved(send.astype(BF), "z", 1))

    lens = lax.dynamic_slice(doc_lengths, (z, y, 0), (1, 1, 4))
    ends = jnp.cumsum(lens.reshape(4), dtype=jnp.int32)
    cosine, sine = rotary_tables()
    w_qkv = jnp.transpose(wqkv[0], (1, 0, 2))
    w_gu = jnp.transpose(wgu[0], (1, 0, 2))
    w_out, w_down = wo[0], wd[0]
    gain_one, gain_two = gains[0, 0:1], gains[0, 1:2]
    mix = jnp.where(first, jnp.array([1.0, 0.0], F32), jnp.array([0.5, 0.5], F32))
    mix_back = jnp.where(first, jnp.array([1.0, 1.0], F32), jnp.array([0.5, 0.0], F32))

    def handed(value, pairs):
        return lax.ppermute(value, "section", pairs)

    def first_half(own, value_first):
        *messages, normed, value, hidden = project(
            x_index, t_index, mix, own, swapped(own), gain_one, w_qkv, value_first, cosine, sine
        )
        return out_and_back(messages, 1), normed, value, hidden

    def second_half(hidden, outs, value, waits=()):
        attended, part, value = branch(x_index, out_and_back(outs, -1), w_out, value, waits=waits)
        middle, mine, normed_two, gate, up, act, keep, send = feed(
            t_index, hidden, part, swapped(part), gain_two, w_gu, w_down
        )
        return mine, keep, swapped(send), value, (attended, middle, normed_two, gate, up, act)

    own_rows = regrouped(tokens).reshape(2 * BLOCK, width)
    no_value = jnp.zeros((RING, 4 * BLOCK, PAIR), BF)

    messages, _, value, hidden = first_half(own_rows, no_value)
    *outs, _, _ = attend(x_index, ends, messages, waits=(seen(w_gu),))
    cot_keep, cot_send = pick(z_index, cotangent, waits=(seen(outs[0]),))
    top_grad = in_order(cot_keep, moved(cot_send, "z", 1)).reshape(2 * BLOCK, width)
    mine, keep, got, value, _ = second_half(hidden, outs, value)
    v_in = handed(value, [(0, 1)])
    result = close(mine, keep, got, waits=(seen(v_in),))
    own = jnp.where(first, own_rows, handed(result, [(0, 1)]))

    messages, normed, value, hidden = first_half(own, v_in)
    *outs, lse, out_t = attend(x_index, ends, messages)
    mine, keep, got, _, saved = second_half(hidden, outs, value, waits=(seen(top_grad),))
    attended, middle, normed_two, gate, up, act = saved
    acts = regrouped(close(mine, keep, got).reshape(2, BLOCK, width))[None]

    def first_back(own_grad, waits=()):
        return feed_back(t_index, own_grad, swapped(own_grad), w_gu, w_down, gate, up, waits=waits)

    def second_back(grad, part, waits=()):
        grad_middle, grad_branch, *sends, gain_sum = middle_back(
            x_index, t_index, grad, middle, part, swapped(part), gain_two, w_out, waits=waits
        )
        return grad_middle, grad_branch, out_and_back(sends, 1), gain_sum

    def third_back(arrived, grad_value, waits=()):
        return attend_back(
            x_index, ends, mix_back, messages, arrived, lse, out_t, grad_value, cosine, sine, waits=waits
        )

    def fourth_back(grads, grad_middle, waits=()):
        keep, send, half = project_back(
            x_index, t_index, out_and_back(grads, -1), w_qkv, normed, waits=waits
        )
        return *input_back(own, grad_middle, keep, swapped(send), gain_one), half, keep

    _, _, part, grad = first_back(top_grad)
    grad_middle, _, arrived, _ = second_back(grad, part)
    grads = third_back(arrived, no_value, waits=(seen(acts[0]),))
    gv_in = handed(jnp.stack([grad[2] for grad in grads]), [(1, 0)])
    _, grad_hidden, half, _ = fourth_back(grads, grad_middle, waits=(seen(gv_in),))
    near = [moved(half, "x", k) for k in range(1, RING)]
    own_grad = jnp.where(first, handed(grad_hidden, [(1, 0)]), top_grad)

    dgate, dup, part, grad_out = first_back(own_grad, waits=[seen(rows) for rows in near])
    feed_term = feed_terms(y_index, normed_two, dgate, dup)
    feed_got = [moved(feed_term[k], "y", k) for k in range(1, 4)]
    grad_middle, grad_branch, arrived, gain_sum = second_back(grad_out, part, waits=(seen(feed_term[0]),))
    early, early_send = early_terms(z_index, act, grad_out, attended, grad_branch)
    early_got = moved(early_send, "z", 1)
    near = jnp.stack(near)
    far = swapped(near)
    grads = third_back(arrived, gv_in, waits=(seen(far), seen(early)))
    late, late_send, gain_total = qkv_terms(
        x_index, t_index, z_index, normed, near, far, grads, w_qkv, gain_one, gain_sum
    )
    late_got = moved(late_send, "z", 1)
    grad_hidden, _, _, last = fourth_back(grads, grad_middle, waits=(seen(late),))
    dins = regrouped(grad_hidden.reshape(2, BLOCK, width))[None]

    rows = width // 32
    feed_sum = summed([feed_term[0], *feed_got], waits=(seen(last),))
    feed_share = jnp.sum(all_to_all(feed_sum, "zx").astype(F32), axis=0).reshape(2, rows, -1)
    rest = rest_sum(early, early_got, late, late_got, waits=(seen(feed_sum),))
    rest = all_to_all(rest, "yx").astype(F32)
    down_share = jnp.sum(rest[:, :DOWN_ROWS], axis=0)
    out_share = jnp.sum(rest[:, OUT_AT:QKV_AT], axis=0)
    qkv_share = jnp.sum(
        rest[:, QKV_AT:, : 6 * PAIR].reshape(4, RING, rows // 2, 2, 3, PAIR), axis=0
    )
    qkv_share = jnp.transpose(qkv_share, (2, 1, 3, 0, 4)).reshape(rows, 3, RING * PAIR)

    gain_total = gain_total + swapped(gain_total)
    gain_total = jnp.sum(
        lax.all_to_all(jnp.broadcast_to(gain_total, (32, *gain_total.shape)), "dp", 0, 0), axis=0
    )
    return (
        acts,
        dins,
        qkv_share[None],
        out_share[None],
        jnp.transpose(feed_share, (1, 0, 2))[None],
        down_share[None],
        gain_total[None],
    )


def solution(mesh):
    placed = (
        P(None, ("tensor", "dp"), None),
        P(None, ("tensor", "dp"), None),
        P(),
        P("section", None, None),
        P("section", None, None, "tensor"),
        P("section", "tensor", None),
        P("section", None, None, "tensor"),
        P("section", "tensor", None),
    )
    return jax.shard_map(
        per_device,
        mesh=mesh,
        in_specs=placed,
        out_specs=(
            P("section", None, ("tensor", "dp"), None),
            P("section", None, ("tensor", "dp"), None),
            P("section", "dp", None, "tensor"),
            P("section", ("tensor", "dp"), None),
            P("section", "dp", None, "tensor"),
            P("section", ("tensor", "dp"), None),
            P("section", None, None),
        ),
        check_vma=False,
    )
```

time: 665 us -> 498 us (0.75)
  matrix products: 57.3 us -> 0 us
  waiting for transfers between devices: 266 us -> 212 us
  starting transfers between devices: 134 us -> 81.5 us
  Pallas kernels: 102 us -> 147 us
  local copies, waits for them, and re-layouts: 64.8 us -> 34.5 us
  other arithmetic: 30.2 us -> 11.4 us
    ppermute x84 -> x36, waiting for transfers between devices: 221 us -> 132 us  [moved(): return lax.ppermute(value, 'dp', along(kind, shift))]
    ppermute x84 -> x36, starting transfers between devices: 121 us -> 54.2 us  [moved(): return lax.ppermute(value, 'dp', along(kind, shift))]
    dot_general x28 -> x0, matrix products: 57.3 us -> none  [the longest x7 13.2 us: term(): jnp.einsum('tf,td->fd', left, right, preferred_element_type=F32).astype(BF)]
    pallas_call x6 -> x26, Pallas kernels: 102 us -> 147 us  [the longest x24 139 us: on_core(): pl.pallas_call(body, in_specs=spots, out_specs=[pl.BlockSpec(memory_space...]
    all_to_all x0 -> x3, waiting for transfers between devices: none -> 33.6 us  [the longest x2 23.2 us: all_to_all(): lax.all_to_all(value, 'dp', 0, 0, axis_index_groups=list(groups.values()))]
    all_to_all x0 -> x3, starting transfers between devices: none -> 14.9 us  [the longest x2 8.94 us: all_to_all(): lax.all_to_all(value, 'dp', 0, 0, axis_index_groups=list(groups.values()))]
    slice x9 -> x20, local copies, waits for them, and re-layouts: 15.4 us -> 1.15 us  [the longest x1 1.07 us: per_device(): rest[:, QKV_AT:, :6 * PAIR].reshape(4, RING, rows // 2, 2, 3, PAIR)]
    unnamed x198 -> x124, local copies, waits for them, and re-layouts: 15 us -> 28 us
  transfers between devices with their start and end apart: 100 -> 57, of which waited for: 48 -> 38; matrix products, arithmetic and copies ran while one was open for 10% -> 3% of each run, Pallas kernels for 4% -> 19%
where the time goes in v2:
time: 498 us; the launch traced here: 489 us
  waiting for transfers between devices  212 us (43%)
  Pallas kernels  147 us (30%)
  starting transfers between devices  81.5 us (16%)
  local copies, waits for them, and re-layouts  34.5 us (7%)
  other arithmetic  11.4 us (2%)
    pallas_call x24, Pallas kernels, on_core(): pl.pallas_call(body, in_specs=spots, out_specs=[pl.BlockSpec(memory_space...  139 us
    ppermute x36, waiting for transfers between devices, moved(): return lax.ppermute(value, 'dp', along(kind, shift))  132 us
    ppermute x36, starting transfers between devices, moved(): return lax.ppermute(value, 'dp', along(kind, shift))  54.2 us
    ppermute x4, waiting for transfers between devices, handed(): return lax.ppermute(value, 'section', pairs)  34.6 us
    unnamed x124, local copies, waits for them, and re-layouts  28 us
    all_to_all x2, waiting for transfers between devices, all_to_all(): lax.all_to_all(value, 'dp', 0, 0, axis_index_groups=list(groups.values()))  23.2 us
    ppermute x14, waiting for transfers between devices, swapped(): return lax.ppermute(value, 'tensor', [(0, 1), (1, 0)])  12 us
    all_to_all x1, waiting for transfers between devices, per_device(): lax.all_to_all(jnp.broadcast_to(gain_total, (32, *gain_total.shape)), 'dp...  10.3 us
  transfers between devices with their start and end apart: 57, of which 38 were waited for; matrix products, arithmetic and copies ran while one was open for 3% of the time, Pallas kernels for 19%

profile of v2, /device:TPU:0, one launch (start us, length us, event | category | flops | bytes accessed | tf_op | source)
XLA Modules:
  0.0 488.8 jit_solution(14146657596383822859)
XLA Ops:
  5.8 6.3 %collective-permute-done = bf16[128,1024]{1,0:T(8,128)(2,1)S(1)} collective-permute-done((bf16[128,1024]{1,0:T(8,128)(2,1)S(1)}, bf16[128,1024]{1,0:T(8,128)(2,1)S(1)}, u32[]{:S(2)}, u32[]{:S(2)}) %collective-permute-start) | collective-permute-done | bytes 262176 | tf_op jit(solution)/shard_map/ppermute | solution.py:39
  13.2 5.9 %copy.38 = bf16[1,1024,2,1408]{3,1,2,0:T(8,128)(2,1)} copy(bf16[1,1024,2,1408]{3,2,1,0:T(2,128)(2,1)} %param.20) | data formatting | bytes 11534336 | tf_op args[6]
  21.7 4.7 project.2
  32.2 6.9 %collective-permute-done.2.refs_3_ = bf16[3,512,128]{2,1,0:T(8,128)(2,1)S(1)} collective-permute-done((bf16[3,512,128]{2,1,0:T(8,128)(2,1)S(1)}, bf16[3,512,128]{2,1,0:T(8,128)(2,1)S(1)}, u32[]{:S(2)}, u32[]{:S(2)}) %collective-permute-start.2) | collective-permute-done | bytes 393248 | tf_op jit(solution)/shard_map/ppermute | solution.py:39
  39.1 9.4 %collective-permute-done.3.refs_4_ = bf16[3,512,128]{2,1,0:T(8,128)(2,1)S(1)} collective-permute-done((bf16[3,512,128]{2,1,0:T(8,128)(2,1)S(1)}, bf16[3,512,128]{2,1,0:T(8,128)(2,1)S(1)}, u32[]{:S(2)}, u32[]{:S(2)}) %collective-permute-start.3) | collective-permute-done | bytes 393248 | tf_op jit(solution)/shard_map/ppermute | solution.py:39
  48.5 13.7 %attend.2 = (bf16[512,128]{1,0:T(8,128)(2,1)S(1)}, bf16[512,128]{1,0:T(8,128)(2,1)S(1)}, bf16[512,128]{1,0:T(8,128)(2,1)S(1)}, bf16[512,128]{1,0:T(8,128)(2,1)S(...) custom-call(s32[1]{0:T(128)} %bitcast.1.refs_0_, s32[4]{0:T(128)S(1)} %bitcast.100, ...), custom_call_target="tpu_custom_call" | custom-call | flops 1 | bytes 1 | tf_op jit(solution)/shard_map/attend/pallas_call | solution.py:82
  78.7 10.0 %feed.2 = (f32[512,1024]{1,0:T(8,128)}, f32[256,1024]{1,0:T(8,128)S(1)}, bf16[512,1024]{1,0:T(8,128)(2,1)}, bf16[512,1408]{1,0:T(8,128)(2,1)}, bf16[512,1408]{1,...) custom-call(s32[1]{0:T(128)} %bitcast.refs_1_.refs_0_, ...), custom_call_target="tpu_custom_call" | custom-call | flops 1 | bytes 1 | tf_op jit(solution)/shard_map/feed/pallas_call | solution.py:82
  95.3 11.0 %collective-permute-done.11 = bf16[256,1024]{1,0:T(8,128)(2,1)S(1)} collective-permute-done((bf16[256,1024]{1,0:T(8,128)(2,1)S(1)}, bf16[256,1024]{1,0:T(8,128)(2,1)S(1)}, u32[]{:S(2)}, u32[]{:S(2)}) %collective-permute-start.11) | collective-permute-done | bytes 524320 | tf_op jit(solution)/shard_map/ppermute | solution.py:778
  119.6 13.7 %collective-permute-done.13.refs_3_.refs_4_ = bf16[3,512,128]{2,1,0:T(8,128)(2,1)S(1)} collective-permute-done((bf16[3,512,128]{2,1,0:T(8,128)(2,1)S(1)}, bf16[3,512,128]{2,1,0:T(8,128)(2,1)S(1)}, u32[]{:S(2)}, u32[]{:S(2)}) %collective-permute-start.13) | collective-permute-done | bytes 393248 | tf_op jit(solution)/shard_map/ppermute | solution.py:39
  133.9 12.8 %attend.3 = (bf16[512,128]{1,0:T(8,128)(2,1)S(1)}, bf16[512,128]{1,0:T(8,128)(2,1)S(1)}, bf16[512,128]{1,0:T(8,128)(2,1)S(1)}, bf16[512,128]{1,0:T(8,128)(2,1)S(...) custom-call(s32[1]{0:T(128)} %bitcast.1.refs_0_, s32[4]{0:T(128)S(1)} %bitcast.101, ...), custom_call_target="tpu_custom_call" | custom-call | flops 1 | bytes 1 | tf_op jit(solution)/shard_map/attend/pallas_call | solution.py:82
  150.2 4.4 collective-permute-done.16.refs_2_
  163.1 7.0 %feed.3 = (f32[512,1024]{1,0:T(8,128)S(1)}, f32[256,1024]{1,0:T(8,128)S(1)}, bf16[512,1024]{1,0:T(8,128)(2,1)S(1)}, bf16[512,1408]{1,0:T(8,128)(2,1)S(1)}, bf16[...) custom-call(s32[1]{0:T(128)} %bitcast.refs_1_.refs_0_, ...), custom_call_target="tpu_custom_call" | custom-call | flops 1 | bytes 1 | tf_op jit(solution)/shard_map/feed/pallas_call | solution.py:82
  175.7 7.4 %feed_back.2 = (bf16[512,1408]{1,0:T(8,128)(2,1)}, bf16[512,1408]{1,0:T(8,128)(2,1)}, bf16[512,1024]{1,0:T(8,128)(2,1)S(1)}, bf16[512,1024]{1,0:T(8,128)(2,1)S(1)}) custom-call(s32[1]{0:T(128)} %bitcast.refs_1_.refs_0_, bf16[256,1024]{1,0:T(8,128)(2,1)S(1)} %bitcast.95, bf16[256,1024]{1,0:T(8,128)(2,1)S(1)} %copy-done.42, ...), custom_call_target="tpu_custom_call" | custom-call | flops 1 | bytes 1 | tf_op jit(solution)/shard_map/feed_back/pallas_call | solution.py:82
  197.6 5.5 %collective-permute-done.25.refs_8_ = bf16[512,128]{1,0:T(8,128)(2,1)S(1)} collective-permute-done((bf16[512,128]{1,0:T(8,128)(2,1)S(1)}, bf16[512,128]{1,0:T(8,128)(2,1)S(1)}, u32[]{:S(2)}, u32[]{:S(2)}) %collective-permute-start.25) | collective-permute-done | bytes 131104 | tf_op jit(solution)/shard_map/ppermute | solution.py:39
  203.7 20.0 %attend_back.2 = (bf16[3,512,128]{2,1,0:T(8,128)(2,1)S(1)}, bf16[3,512,128]{2,1,0:T(8,128)(2,1)S(1)}, bf16[3,512,128]{2,1,0:T(8,128)(2,1)S(1)}, bf16[3,512,128]{2,1,0:T(8,128)(2,1)S(1)}) custom-call(s32[1]{0:T(128)} %bitcast.1.refs_0_, s32[4]{0:T(128)S(1)} %bitcast.102, f32[2]{0:T(128)S(1)} %broadcast_select_fusion.2.refs_2_, ...), custom_call_target="tpu_custom_call" | custom-call | flops 1 | bytes 1 | tf_op jit(solution)/shard_map/attend_back/pallas_call | solution.py:82
  228.7 9.8 %collective-permute-done.31.refs_13_ = bf16[4,512,128]{2,1,0:T(8,128)(2,1)S(1)} collective-permute-done((bf16[4,512,128]{2,1,0:T(8,128)(2,1)S(1)}, bf16[4,512,128]{2,1,0:T(8,128)(2,1)S(1)}, u32[]{:S(2)}, u32[]{:S(2)}) %collective-permute-start.31) | collective-permute-done | bytes 524320 | tf_op jit(solution)/shard_map/ppermute | solution.py:778
  238.5 5.9 %collective-permute-done.28.refs_3_ = bf16[3,512,128]{2,1,0:T(8,128)(2,1)S(1)} collective-permute-done((bf16[3,512,128]{2,1,0:T(8,128)(2,1)S(1)}, bf16[3,512,128]{2,1,0:T(8,128)(2,1)S(1)}, u32[]{:S(2)}, u32[]{:S(2)}) %collective-permute-start.28) | collective-permute-done | bytes 393248 | tf_op jit(solution)/shard_map/ppermute | solution.py:39
  257.4 12.3 %collective-permute-done.33 = bf16[256,1024]{1,0:T(8,128)(2,1)S(1)} collective-permute-done((bf16[256,1024]{1,0:T(8,128)(2,1)S(1)}, bf16[256,1024]{1,0:T(8,128)(2,1)S(1)}, u32[]{:S(2)}, u32[]{:S(2)}) %collective-permute-start.33) | collective-permute-done | bytes 524320 | tf_op jit(solution)/shard_map/ppermute | solution.py:778
  272.4 10.1 %collective-permute-done.35 = bf16[256,1024]{1,0:T(8,128)(2,1)S(1)} collective-permute-done((bf16[256,1024]{1,0:T(8,128)(2,1)S(1)}, bf16[256,1024]{1,0:T(8,128)(2,1)S(1)}, u32[]{:S(2)}, u32[]{:S(2)}) %collective-permute-start.35) | collective-permute-done | bytes 524320 | tf_op jit(solution)/shard_map/ppermute | solution.py:39
  284.3 7.4 %feed_back.3 = (bf16[512,1408]{1,0:T(8,128)(2,1)S(1)}, bf16[512,1408]{1,0:T(8,128)(2,1)S(1)}, bf16[512,1024]{1,0:T(8,128)(2,1)S(1)}, bf16[512,1024]{1,0:T(8,128)(2,1)S(1)}) custom-call(s32[1]{0:T(128)} %bitcast.refs_1_.refs_0_, bf16[256,1024]{1,0:T(8,128)(2,1)S(1)} %broadcast_select_fusion.refs_1_, bf16[256,1024]{1,0:T(8,128)(2,1)S(1)} %collective-permute-done.34.refs_2_, ...), custom_call_target="tpu_custom_call" | custom-call | flops 1 | bytes 1 | tf_op jit(solution)/shard_map/feed_back/pallas_call | solution.py:82
  291.8 4.9 feed_terms.1
  308.4 5.2 %early_terms.1 = (bf16[16,64,1024]{2,1,0:T(8,128)(2,1)S(1)}, bf16[16,64,1024]{2,1,0:T(8,128)(2,1)}) custom-call(s32[1]{0:T(128)} %bitcast.17.refs_0_.refs_2_, bf16[512,1408]{1,0:T(8,128)(2,1)S(1)} %copy-done.32, bf16[512,1024]{1,0:T(8,128)(2,1)S(1)} %get-tuple-element.141.refs_2_, bf16[512,512]{1,0:T(8,128)(2,1)S(1)} %copy-done.40, ...), custom_call_target="tpu_custom_call" | custom-call | flops 1 | bytes 1 | tf_op jit(solution)/shard_map/early_terms/pallas_call | solution.py:82
  320.2 20.8 %attend_back.3 = (bf16[3,512,128]{2,1,0:T(8,128)(2,1)S(1)}, bf16[3,512,128]{2,1,0:T(8,128)(2,1)S(1)}, bf16[3,512,128]{2,1,0:T(8,128)(2,1)S(1)}, bf16[3,512,128]{2,1,0:T(8,128)(2,1)}) custom-call(s32[1]{0:T(128)} %bitcast.1.refs_0_, s32[4]{0:T(128)S(1)} %bitcast.103, f32[2]{0:T(128)S(1)} %broadcast_select_fusion.2.refs_2_, ...), custom_call_target="tpu_custom_call" | custom-call | flops 1 | bytes 1 | tf_op jit(solution)/shard_map/attend_back/pallas_call | solution.py:82
  352.5 10.4 %collective-permute-done.44.refs_4_ = bf16[3,512,128]{2,1,0:T(8,128)(2,1)S(1)} collective-permute-done((bf16[3,512,128]{2,1,0:T(8,128)(2,1)S(1)}, bf16[3,512,128]{2,1,0:T(8,128)(2,1)S(1)}, u32[]{:S(2)}, u32[]{:S(2)}) %collective-permute-start.44) | collective-permute-done | bytes 393248 | tf_op jit(solution)/shard_map/ppermute | solution.py:39
  365.2 6.0 %all-to-all-start.2 = ((f32[32,2,1024]{2,1,0:T(2,128)}), f32[32,2,1024]{2,1,0:T(2,128)}, u32[]{:S(2)}, u32[]{:S(2)}) async-start(f32[32,2,1024]{2,1,0:T(2,128)} %broadcast_in_dim.24), calls=%async_computation.2 | async-start | bytes 524288 | tf_op jit(solution)/shard_map/all_to_all | solution.py:869
  371.2 4.6 collective-permute-done.45.refs_5_
  385.9 4.4 summed.1
  390.3 10.3 %all-to-all-done.2 = f32[32,2,1024]{2,1,0:T(2,128)} async-done(((f32[32,2,1024]{2,1,0:T(2,128)}), f32[32,2,1024]{2,1,0:T(2,128)}, u32[]{:S(2)}, u32[]{:S(2)}) %all-to-all-start.2) | async-done | bytes 262176 | tf_op jit(solution)/shard_map/all_to_all | solution.py:869
  409.3 23.0 %collective-permute-done.49.refs_3_ = bf16[16,16,768]{2,1,0:T(8,128)(2,1)S(1)} collective-permute-done((bf16[16,16,768]{2,1,0:T(8,128)(2,1)S(1)}, bf16[16,16,768]{2,1,0:T(8,128)(2,1)S(1)}, u32[]{:S(2)}, u32[]{:S(2)}) %collective-permute-start.49) | collective-permute-done | bytes 393248 | tf_op jit(solution)/shard_map/ppermute | solution.py:39
  436.6 4.6 all-to-all-start
  447.7 6.9 %collective-permute-done.47 = bf16[128,1024]{1,0:T(8,128)(2,1)S(1)} collective-permute-done((bf16[128,1024]{1,0:T(8,128)(2,1)S(1)}, bf16[128,1024]{1,0:T(8,128)(2,1)S(1)}, u32[]{:S(2)}, u32[]{:S(2)}) %collective-permute-start.47) | collective-permute-done | bytes 262176 | tf_op jit(solution)/shard_map/ppermute | solution.py:39
  458.3 23.2 %all-to-all-done = bf16[16,80,1024]{2,1,0:T(8,128)(2,1)} async-done(((bf16[16,80,1024]{2,1,0:T(8,128)(2,1)}), bf16[16,80,1024]{2,1,0:T(8,128)(2,1)}, u32[]{:S(2)}, u32[]{:S(2)}) %all-to-all-start) | async-done | bytes 2621472 | tf_op jit(solution)/shard_map/all_to_all | solution.py:745
  (290 shorter events, 178.3 us)
Async XLA Ops:
  26.4 12.7 %collective-permute-start.2 = (bf16[3,512,128]{2,1,0:T(8,128)(2,1)S(1)}, bf16[3,512,128]{2,1,0:T(8,128)(2,1)S(1)}, u32[]{:S(2)}, u32[]{:S(2)}) collective-permute-start(bf16[3,512,128]{2,1,0:T(8,128)(2,1)S(1)} %get-tuple-element.91), channel_id=1, source_target_pairs={{0,1},{1,2},{2,3},{3,0},{4,5},{5,6},{6,7},{7,4},{8,9},{9,10},{10,1... | collective-permute-start | bytes 1179656 | tf_op jit(solution)/shard_map/ppermute | solution.py:39
  27.8 20.7 %collective-permute-start.3 = (bf16[3,512,128]{2,1,0:T(8,128)(2,1)S(1)}, bf16[3,512,128]{2,1,0:T(8,128)(2,1)S(1)}, u32[]{:S(2)}, u32[]{:S(2)}) collective-permute-start(bf16[3,512,128]{2,1,0:T(8,128)(2,1)S(1)} %get-tuple-element.92), channel_id=1, source_target_pairs={{0,2},{1,3},{2,0},{3,1},{4,6},{5,7},{6,4},{7,5},{8,10},{9,11},{10,... | collective-permute-start | bytes 1179656 | tf_op jit(solution)/shard_map/ppermute | solution.py:39
  30.5 17.9 %collective-permute-start.4 = (bf16[3,512,128]{2,1,0:T(8,128)(2,1)S(1)}, bf16[3,512,128]{2,1,0:T(8,128)(2,1)S(1)}, u32[]{:S(2)}, u32[]{:S(2)}) collective-permute-start(bf16[3,512,128]{2,1,0:T(8,128)(2,1)S(1)} %get-tuple-element.93), channel_id=1, source_target_pairs={{0,3},{1,0},{2,1},{3,2},{4,7},{5,4},{6,5},{7,6},{8,11},{9,8},{10,9... | collective-permute-start | bytes 1179656 | tf_op jit(solution)/shard_map/ppermute | solution.py:39
  75.5 15.0 %collective-permute-start.10 = (bf16[4,512,128]{2,1,0:T(8,128)(2,1)S(1)}, bf16[4,512,128]{2,1,0:T(8,128)(2,1)S(1)}, u32[]{:S(2)}, u32[]{:S(2)}) collective-permute-start(bf16[4,512,128]{2,1,0:T(8,128)(2,1)S(1)} %get-tuple-element.103), channel_id=1, source_target_pairs={{0,64},{1,65},{2,66},{3,67},{4,68},{5,69},{6,70},{7,71},{8,72},{9,... | collective-permute-start | bytes 1572872 | tf_op jit(solution)/shard_map/ppermute | solution.py:778
  90.9 15.4 %collective-permute-start.11 = (bf16[256,1024]{1,0:T(8,128)(2,1)S(1)}, bf16[256,1024]{1,0:T(8,128)(2,1)S(1)}, u32[]{:S(2)}, u32[]{:S(2)}) collective-permute-start(bf16[256,1024]{1,0:T(8,128)(2,1)S(1)} %close.2), channel_id=1, source_target_pairs={{0,64},{1,65},{2,66},{3,67},{4,68},{5,69},{6,70},{7,71},{8,72},{9,... | collective-permute-start | bytes 1572872 | tf_op jit(solution)/shard_map/ppermute | solution.py:778
  112.4 20.9 %collective-permute-start.13 = (bf16[3,512,128]{2,1,0:T(8,128)(2,1)S(1)}, bf16[3,512,128]{2,1,0:T(8,128)(2,1)S(1)}, u32[]{:S(2)}, u32[]{:S(2)}) collective-permute-start(bf16[3,512,128]{2,1,0:T(8,128)(2,1)S(1)} %get-tuple-element.106), channel_id=1, source_target_pairs={{0,1},{1,2},{2,3},{3,0},{4,5},{5,6},{6,7},{7,4},{8,9},{9,10},{10,1... | collective-permute-start | bytes 1179656 | tf_op jit(solution)/shard_map/ppermute | solution.py:39
  112.5 20.8 %collective-permute-start.14 = (bf16[3,512,128]{2,1,0:T(8,128)(2,1)S(1)}, bf16[3,512,128]{2,1,0:T(8,128)(2,1)S(1)}, u32[]{:S(2)}, u32[]{:S(2)}) collective-permute-start(bf16[3,512,128]{2,1,0:T(8,128)(2,1)S(1)} %get-tuple-element.107), channel_id=1, source_target_pairs={{0,2},{1,3},{2,0},{3,1},{4,6},{5,7},{6,4},{7,5},{8,10},{9,11},{10,... | collective-permute-start | bytes 1179656 | tf_op jit(solution)/shard_map/ppermute | solution.py:39
  114.6 19.3 %collective-permute-start.15 = (bf16[3,512,128]{2,1,0:T(8,128)(2,1)S(1)}, bf16[3,512,128]{2,1,0:T(8,128)(2,1)S(1)}, u32[]{:S(2)}, u32[]{:S(2)}) collective-permute-start(bf16[3,512,128]{2,1,0:T(8,128)(2,1)S(1)} %get-tuple-element.108), channel_id=1, source_target_pairs={{0,3},{1,0},{2,1},{3,2},{4,7},{5,4},{6,5},{7,6},{8,11},{9,8},{10,9... | collective-permute-start | bytes 1179656 | tf_op jit(solution)/shard_map/ppermute | solution.py:39
  115.8 34.3 %collective-permute-start.19 = (bf16[128,1024]{1,0:T(8,128)(2,1)S(1)}, bf16[128,1024]{1,0:T(8,128)(2,1)S(1)}, u32[]{:S(2)}, u32[]{:S(2)}) collective-permute-start(bf16[128,1024]{1,0:T(8,128)(2,1)S(1)} %get-tuple-element.115), channel_id=1, source_target_pairs={{0,4},{1,5},{2,6},{3,7},{4,0},{5,1},{6,2},{7,3},{8,12},{9,13},{10,... | collective-permute-start | bytes 786440 | tf_op jit(solution)/shard_map/ppermute | solution.py:39
  160.4 11.8 %collective-permute-start.23 = (bf16[256,1024]{1,0:T(8,128)(2,1)S(1)}, bf16[256,1024]{1,0:T(8,128)(2,1)S(1)}, u32[]{:S(2)}, u32[]{:S(2)}) collective-permute-start(bf16[256,1024]{1,0:T(8,128)(2,1)S(1)} %bitcast.94), channel_id=1, source_target_pairs={{0,32},{32,0},{1,33},{33,1},{2,34},{34,2},{3,35},{35,3},{4,36},{36... | collective-permute-start | bytes 1572872 | tf_op jit(solution)/shard_map/ppermute | solution.py:43
  186.9 10.7 %collective-permute-start.22 = (bf16[128,1024]{1,0:T(8,128)(2,1)S(1)}, bf16[128,1024]{1,0:T(8,128)(2,1)S(1)}, u32[]{:S(2)}, u32[]{:S(2)}) collective-permute-start(bf16[128,1024]{1,0:T(8,128)(2,1)S(1)} %get-tuple-element.207), channel_id=1, source_target_pairs={{0,4},{1,5},{2,6},{3,7},{4,0},{5,1},{6,2},{7,3},{8,12},{9,13},{10,... | collective-permute-start | bytes 786440 | tf_op jit(solution)/shard_map/ppermute | solution.py:39
  223.9 14.6 %collective-permute-start.31 = (bf16[4,512,128]{2,1,0:T(8,128)(2,1)S(1)}, bf16[4,512,128]{2,1,0:T(8,128)(2,1)S(1)}, u32[]{:S(2)}, u32[]{:S(2)}) collective-permute-start(bf16[4,512,128]{2,1,0:T(8,128)(2,1)S(1)} %pad_maximum_fusion.1), channel_id=1, source_target_pairs={{64,0},{65,1},{66,2},{67,3},{68,4},{69,5},{70,6},{71,7},{72,8},{73... | collective-permute-start | bytes 1572872 | tf_op jit(solution)/shard_map/ppermute | solution.py:778
  225.4 19.0 %collective-permute-start.28 = (bf16[3,512,128]{2,1,0:T(8,128)(2,1)S(1)}, bf16[3,512,128]{2,1,0:T(8,128)(2,1)S(1)}, u32[]{:S(2)}, u32[]{:S(2)}) collective-permute-start(bf16[3,512,128]{2,1,0:T(8,128)(2,1)S(1)} %get-tuple-element.133), channel_id=1, source_target_pairs={{0,3},{1,0},{2,1},{3,2},{4,7},{5,4},{6,5},{7,6},{8,11},{9,8},{10,9... | collective-permute-start | bytes 1179656 | tf_op jit(solution)/shard_map/ppermute | solution.py:39
  227.8 16.6 %collective-permute-start.29 = (bf16[3,512,128]{2,1,0:T(8,128)(2,1)S(1)}, bf16[3,512,128]{2,1,0:T(8,128)(2,1)S(1)}, u32[]{:S(2)}, u32[]{:S(2)}) collective-permute-start(bf16[3,512,128]{2,1,0:T(8,128)(2,1)S(1)} %get-tuple-element.134), channel_id=1, source_target_pairs={{0,2},{1,3},{2,0},{3,1},{4,6},{5,7},{6,4},{7,5},{8,10},{9,11},{10,... | collective-permute-start | bytes 1179656 | tf_op jit(solution)/shard_map/ppermute | solution.py:39
  227.8 20.0 %collective-permute-start.30 = (bf16[3,512,128]{2,1,0:T(8,128)(2,1)S(1)}, bf16[3,512,128]{2,1,0:T(8,128)(2,1)S(1)}, u32[]{:S(2)}, u32[]{:S(2)}) collective-permute-start(bf16[3,512,128]{2,1,0:T(8,128)(2,1)S(1)} %get-tuple-element.135), channel_id=1, source_target_pairs={{0,1},{1,2},{2,3},{3,0},{4,5},{5,6},{6,7},{7,4},{8,9},{9,10},{10,1... | collective-permute-start | bytes 1179656 | tf_op jit(solution)/shard_map/ppermute | solution.py:39
  253.8 15.9 %collective-permute-start.33 = (bf16[256,1024]{1,0:T(8,128)(2,1)S(1)}, bf16[256,1024]{1,0:T(8,128)(2,1)S(1)}, u32[]{:S(2)}, u32[]{:S(2)}) collective-permute-start(bf16[256,1024]{1,0:T(8,128)(2,1)S(1)} %get-tuple-element.139), channel_id=1, source_target_pairs={{64,0},{65,1},{66,2},{67,3},{68,4},{69,5},{70,6},{71,7},{72,8},{73... | collective-permute-start | bytes 1572872 | tf_op jit(solution)/shard_map/ppermute | solution.py:778
  255.1 14.8 %collective-permute-start.37 = (bf16[256,1024]{1,0:T(8,128)(2,1)S(1)}, bf16[256,1024]{1,0:T(8,128)(2,1)S(1)}, u32[]{:S(2)}, u32[]{:S(2)}) collective-permute-start(bf16[256,1024]{1,0:T(8,128)(2,1)S(1)} %get-tuple-element.140), channel_id=1, source_target_pairs={{0,3},{1,0},{2,1},{3,2},{4,7},{5,4},{6,5},{7,6},{8,11},{9,8},{10,9... | collective-permute-start | bytes 1572872 | tf_op jit(solution)/shard_map/ppermute | solution.py:39
  256.1 16.4 %collective-permute-start.36 = (bf16[256,1024]{1,0:T(8,128)(2,1)S(1)}, bf16[256,1024]{1,0:T(8,128)(2,1)S(1)}, u32[]{:S(2)}, u32[]{:S(2)}) collective-permute-start(bf16[256,1024]{1,0:T(8,128)(2,1)S(1)} %get-tuple-element.140), channel_id=1, source_target_pairs={{0,2},{1,3},{2,0},{3,1},{4,6},{5,7},{6,4},{7,5},{8,10},{9,11},{10,... | collective-permute-start | bytes 1572872 | tf_op jit(solution)/shard_map/ppermute | solution.py:39
  256.4 26.1 %collective-permute-start.35 = (bf16[256,1024]{1,0:T(8,128)(2,1)S(1)}, bf16[256,1024]{1,0:T(8,128)(2,1)S(1)}, u32[]{:S(2)}, u32[]{:S(2)}) collective-permute-start(bf16[256,1024]{1,0:T(8,128)(2,1)S(1)} %get-tuple-element.140), channel_id=1, source_target_pairs={{0,1},{1,2},{2,3},{3,0},{4,5},{5,6},{6,7},{7,4},{8,9},{9,10},{10,1... | collective-permute-start | bytes 1572872 | tf_op jit(solution)/shard_map/ppermute | solution.py:39
  269.8 13.0 %collective-permute-start.34 = (bf16[256,1024]{1,0:T(8,128)(2,1)S(1)}, bf16[256,1024]{1,0:T(8,128)(2,1)S(1)}, u32[]{:S(2)}, u32[]{:S(2)}) collective-permute-start(bf16[256,1024]{1,0:T(8,128)(2,1)S(1)} %broadcast_select_fusion.refs_1_), channel_id=1, source_target_pairs={{0,32},{32,0},{1,33},{33,1},{2,34},{34,2},{3,35},{35,3},{4,36},{36... | collective-permute-start | bytes 1572872 | tf_op jit(solution)/shard_map/ppermute | solution.py:43
  282.7 23.5 %collective-permute-start.42 = (bf16[3,256,1024]{2,1,0:T(8,128)(2,1)S(1)}, bf16[3,256,1024]{2,1,0:T(8,128)(2,1)S(1)}, u32[]{:S(2)}, u32[]{:S(2)}) collective-permute-start(bf16[3,256,1024]{2,1,0:T(8,128)(2,1)S(1)} %pad_maximum_fusion.refs_4_), channel_id=1, source_target_pairs={{0,32},{32,0},{1,33},{33,1},{2,34},{34,2},{3,35},{35,3},{4,36},{36... | collective-permute-start | bytes 4718600 | tf_op jit(solution)/shard_map/ppermute | solution.py:43
  291.7 11.9 %collective-permute-start.38 = (bf16[512,1024]{1,0:T(8,128)(2,1)S(1)}, bf16[512,1024]{1,0:T(8,128)(2,1)S(1)}, u32[]{:S(2)}, u32[]{:S(2)}) collective-permute-start(bf16[512,1024]{1,0:T(8,128)(2,1)S(1)} %get-tuple-element.142.refs_4_), channel_id=1, source_target_pairs={{0,32},{32,0},{1,33},{33,1},{2,34},{34,2},{3,35},{35,3},{4,36},{36... | collective-permute-start | bytes 3145736 | tf_op jit(solution)/shard_map/ppermute | solution.py:43
  297.8 88.1 %collective-permute-start.50 = (bf16[8,64,1408]{2,1,0:T(8,128)(2,1)}, bf16[8,64,1408]{2,1,0:T(8,128)(2,1)}, u32[]{:S(2)}, u32[]{:S(2)}) collective-permute-start(bf16[8,64,1408]{2,1,0:T(8,128)(2,1)} %get-tuple-element.167), channel_id=1, source_target_pairs={{0,8},{1,9},{2,10},{3,11},{4,12},{5,13},{6,14},{7,15},{8,16},{9,17... | collective-permute-start | bytes 4325384 | tf_op jit(solution)/shard_map/ppermute | solution.py:39
  299.4 86.5 %collective-permute-start.51 = (bf16[8,64,1408]{2,1,0:T(8,128)(2,1)}, bf16[8,64,1408]{2,1,0:T(8,128)(2,1)}, u32[]{:S(2)}, u32[]{:S(2)}) collective-permute-start(bf16[8,64,1408]{2,1,0:T(8,128)(2,1)} %get-tuple-element.168), channel_id=1, source_target_pairs={{0,16},{1,17},{2,18},{3,19},{4,20},{5,21},{6,22},{7,23},{8,24},{9,... | collective-permute-start | bytes 4325384 | tf_op jit(solution)/shard_map/ppermute | solution.py:39
  302.3 83.6 %collective-permute-start.52 = (bf16[8,64,1408]{2,1,0:T(8,128)(2,1)}, bf16[8,64,1408]{2,1,0:T(8,128)(2,1)}, u32[]{:S(2)}, u32[]{:S(2)}) collective-permute-start(bf16[8,64,1408]{2,1,0:T(8,128)(2,1)} %get-tuple-element.169), channel_id=1, source_target_pairs={{0,24},{1,25},{2,26},{3,27},{4,28},{5,29},{6,30},{7,31},{8,0},{9,1... | collective-permute-start | bytes 4325384 | tf_op jit(solution)/shard_map/ppermute | solution.py:39
  348.1 84.3 %collective-permute-start.48 = (bf16[16,64,1024]{2,1,0:T(8,128)(2,1)}, bf16[16,64,1024]{2,1,0:T(8,128)(2,1)}, u32[]{:S(2)}, u32[]{:S(2)}) collective-permute-start(bf16[16,64,1024]{2,1,0:T(8,128)(2,1)} %get-tuple-element.165), channel_id=1, source_target_pairs={{0,4},{1,5},{2,6},{3,7},{4,0},{5,1},{6,2},{7,3},{8,12},{9,13},{10,... | collective-permute-start | bytes 6291464 | tf_op jit(solution)/shard_map/ppermute | solution.py:39
  351.3 11.6 %collective-permute-start.44 = (bf16[3,512,128]{2,1,0:T(8,128)(2,1)S(1)}, bf16[3,512,128]{2,1,0:T(8,128)(2,1)S(1)}, u32[]{:S(2)}, u32[]{:S(2)}) collective-permute-start(bf16[3,512,128]{2,1,0:T(8,128)(2,1)S(1)} %get-tuple-element.158.refs_8_), channel_id=1, source_target_pairs={{0,2},{1,3},{2,0},{3,1},{4,6},{5,7},{6,4},{7,5},{8,10},{9,11},{10,... | collective-permute-start | bytes 1179656 | tf_op jit(solution)/shard_map/ppermute | solution.py:39
  363.6 12.2 %collective-permute-start.45 = (bf16[3,512,128]{2,1,0:T(8,128)(2,1)}, bf16[3,512,128]{2,1,0:T(8,128)(2,1)}, u32[]{:S(2)}, u32[]{:S(2)}) collective-permute-start(bf16[3,512,128]{2,1,0:T(8,128)(2,1)} %get-tuple-element.159.refs_9_), channel_id=1, source_target_pairs={{0,1},{1,2},{2,3},{3,0},{4,5},{5,6},{6,7},{7,4},{8,9},{9,10},{10,1... | collective-permute-start | bytes 1179656 | tf_op jit(solution)/shard_map/ppermute | solution.py:39
  365.2 35.5 %all-to-all-start.2 = ((f32[32,2,1024]{2,1,0:T(2,128)}), f32[32,2,1024]{2,1,0:T(2,128)}, u32[]{:S(2)}, u32[]{:S(2)}) async-start(f32[32,2,1024]{2,1,0:T(2,128)} %broadcast_in_dim.24), calls=%async_computation.2 | async-start | bytes 524288 | tf_op jit(solution)/shard_map/all_to_all | solution.py:869
  400.6 35.9 %all-to-all-start.1 = ((bf16[8,64,1408]{2,1,0:T(8,128)(2,1)}), bf16[8,64,1408]{2,1,0:T(8,128)(2,1)}, u32[]{:S(2)}, u32[]{:S(2)}) async-start(bf16[8,64,1408]{2,1,0:T(8,128)(2,1)} %summed.1), calls=%async_computation.1 | async-start | bytes 2883584 | tf_op jit(solution)/shard_map/all_to_all | solution.py:745
  405.0 27.4 %collective-permute-start.49 = (bf16[16,16,768]{2,1,0:T(8,128)(2,1)S(1)}, bf16[16,16,768]{2,1,0:T(8,128)(2,1)S(1)}, u32[]{:S(2)}, u32[]{:S(2)}) collective-permute-start(bf16[16,16,768]{2,1,0:T(8,128)(2,1)S(1)} %copy-done.53), channel_id=1, source_target_pairs={{0,4},{1,5},{2,6},{3,7},{4,0},{5,1},{6,2},{7,3},{8,12},{9,13},{10,... | collective-permute-start | bytes 1179656 | tf_op jit(solution)/shard_map/ppermute | solution.py:39
  436.6 45.0 %all-to-all-start = ((bf16[16,80,1024]{2,1,0:T(8,128)(2,1)}), bf16[16,80,1024]{2,1,0:T(8,128)(2,1)}, u32[]{:S(2)}, u32[]{:S(2)}) async-start(bf16[16,80,1024]{2,1,0:T(8,128)(2,1)} %rest_sum.1), calls=%async_computation | async-start | bytes 5242880 | tf_op jit(solution)/shard_map/all_to_all | solution.py:745
  (86 other events, 898.7 us)

commit v3 on v2

--- a/solution.py
+++ b/solution.py
@@ -12,6 +12,7 @@
 BLOCK = 128
 PAIR = 2 * HD
 EPSILON = 1e-06
+BRIEF = 0.001
 NEGATIVE = -1e30
 KEYS = 512
 QUERIES = 1024
@@ -69,7 +70,11 @@
     return (source, 4 + source, 15 - source, 11 - source)[part]
 
 
-def on_core(kernel, ins, outs, *, scratch=(), smem=0, far=0, waits=(), limit=24, name):
+def lasting(us):
+    return pl.CostEstimate(flops=int(us * 1.1e9), bytes_accessed=int(us * 3.6e6), transcendentals=0)
+
+
+def on_core(kernel, ins, outs, *, scratch=(), smem=0, far=0, waits=(), limit=24, us, name):
     spots = [pl.BlockSpec(memory_space=pltpu.SMEM)] * smem
     spots += [pl.BlockSpec(memory_space=pltpu.VMEM)] * (len(ins) - smem - far)
     spots += [pl.BlockSpec(memory_space=pltpu.HBM)] * far
@@ -86,7 +91,7 @@
         out_shape=list(outs),
         scratch_shapes=list(scratch),
         compiler_params=pltpu.CompilerParams(vmem_limit_bytes=limit * 2**20),
-        cost_estimate=pl.CostEstimate(flops=1, bytes_accessed=1, transcendentals=0),
+        cost_estimate=lasting(us),
         name=name,
     )(*ins, *waits)
 
@@ -123,29 +128,33 @@
     return pl.ds(pl.multiple_of((1 - t_ref[0]) * (rows // 2), rows // 2), rows // 2)
 
 
-def own_tables(x_ref, table, half):
-    blocks = [place_block(x_ref[0], 2 * half + part) for part in range(2)]
-    return jnp.concatenate(
-        [table[pl.ds(pl.multiple_of(b * BLOCK, BLOCK), BLOCK), :] for b in blocks]
-    )
-
-
 def project_kernel(x_ref, t_ref, mix_ref, own_ref, other_ref, gain_ref, w_ref, v1_ref, cos_ref, sin_ref,
-                   m0, m1, m2, m3, n_ref, v_ref, h_ref):
+                   m0, m1, m2, m3, n_ref, v_ref, h_ref, zero_ref, cos_buf, sin_buf, sems):
+    copies = []
+    for part in range(4):
+        at = pl.ds(pl.multiple_of(place_block(x_ref[0], part) * BLOCK, BLOCK), BLOCK)
+        to = pl.ds(part * BLOCK, BLOCK)
+        copies.append(pltpu.make_async_copy(cos_ref.at[at], cos_buf.at[to], sems.at[part, 0]))
+        copies.append(pltpu.make_async_copy(sin_ref.at[at], sin_buf.at[to], sems.at[part, 1]))
+    for copy in copies:
+        copy.start()
+    zero_ref[...] = jnp.zeros_like(zero_ref)
     rows = h_ref.shape[0]
     h_ref[own_half(t_ref, rows), :] = own_ref[...]
     h_ref[far_half(t_ref, rows), :] = other_ref[...]
     for part in halves(rows):
         h = h_ref[part].astype(F32)
         n_ref[part] = (h * rms_scale(h) * gain_ref[...]).astype(BF)
+    for copy in copies:
+        copy.wait()
     outs = (m0, m1, m2, m3)
     for pair in ((0, 1), (2, 3)):
         weight = jnp.concatenate(
             [w_ref[c, :, heads_at(x_ref, k)] for k in pair for c in range(3)], axis=1
         )
-        for which, part in enumerate(halves(rows)):
+        for part in halves(rows):
             both = jnp.dot(n_ref[part], weight, preferred_element_type=F32)
-            cosine, sine = own_tables(x_ref, cos_ref, which), own_tables(x_ref, sin_ref, which)
+            cosine, sine = cos_buf[part], sin_buf[part]
             for index, k in enumerate(pair):
                 query, key, value = [
                     both[:, (3 * index + c) * PAIR : (3 * index + c + 1) * PAIR] for c in range(3)
@@ -163,8 +172,9 @@
         project_kernel,
         (x_index, t_index, mix, own, other, gain, w_qkv, value_first, cosine, sine),
         [shaped(3, rows, PAIR)] * 4
-        + [shaped(rows, width), shaped(RING, rows, PAIR), shaped(rows, width)],
-        smem=3, waits=waits, limit=20, name="project",
+        + [shaped(rows, width), shaped(RING, rows, PAIR), shaped(rows, width), shaped(8, PAIR)],
+        scratch=[pltpu.VMEM((rows, PAIR), F32)] * 2 + [pltpu.SemaphoreType.DMA((4, 2))],
+        smem=3, far=2, waits=waits, limit=5, us=3, name="project",
     )
 
 
@@ -175,7 +185,7 @@
 
 def pick(z_index, pair, waits=()):
     return on_core(
-        pick_kernel, (z_index, pair), [shaped(*pair.shape[1:])] * 2, smem=1, waits=waits, limit=4, name="pick"
+        pick_kernel, (z_index, pair), [shaped(*pair.shape[1:])] * 2, smem=1, waits=waits, limit=4, us=0.6, name="pick"
     )
 
 
@@ -193,7 +203,7 @@
         branch_kernel,
         (x_index, *arrived, w_out, value),
         [shaped(rows, RING * PAIR), shaped(rows, width), jax.ShapeDtypeStruct(value.shape, BF)],
-        smem=1, waits=waits, limit=14, name="branch",
+        smem=1, waits=waits, limit=4, us=1, name="branch",
     )
 
 
@@ -234,18 +244,23 @@
 
 
 def feed_kernel(t_ref, h_ref, p_ref, q_ref, gain_ref, wgu_ref, wd_ref,
-                m_ref, mine_ref, n_ref, gate_ref, up_ref, act_ref, keep_ref, send_ref,
-                gu_buf, d_buf, sems, acc):
+                mine_ref, keep_ref, send_ref, n_ref, *rest):
+    *saved, gu_buf, d_buf, sems, acc = rest
     copies = weight_copies(wgu_ref, wd_ref, gu_buf, d_buf, sems)
     for pair in copies:
         for copy in pair:
             copy.start()
     rows = halves(h_ref.shape[0])
-    for part in rows:
+    for which, part in enumerate(rows):
         middle = h_ref[part].astype(F32) + (p_ref[part].astype(F32) + q_ref[part].astype(F32))
-        m_ref[part] = middle
+        if saved:
+            saved[0][part] = middle
         n_ref[part] = (middle * rms_scale(middle) * gain_ref[...]).astype(BF)
-    mine_ref[...] = m_ref[own_half(t_ref, h_ref.shape[0]), :]
+
+        @pl.when(t_ref[0] == which)
+        def _():
+            mine_ref[...] = middle
+
     for index, (low, high) in enumerate(pieces(d_buf.shape[0])):
         at = slice(low, high)
         for copy in copies[index]:
@@ -253,10 +268,11 @@
         for which, part in enumerate(rows):
             gate = jnp.dot(n_ref[part], gu_buf[0, :, at], preferred_element_type=F32)
             up = jnp.dot(n_ref[part], gu_buf[1, :, at], preferred_element_type=F32)
-            gate_ref[part, at] = gate.astype(BF)
-            up_ref[part, at] = up.astype(BF)
             act = (gate / (1.0 + jnp.exp(-gate)) * up).astype(BF)
-            act_ref[part, at] = act
+            if saved:
+                saved[1][part, at] = gate.astype(BF)
+                saved[2][part, at] = up.astype(BF)
+                saved[3][part, at] = act
             total = jnp.dot(act, d_buf[at, :], preferred_element_type=F32)
             if index == 0:
                 acc[part] = total
@@ -264,17 +280,19 @@
                 put_halves(t_ref, which, keep_ref, send_ref, (acc[part] + total).astype(BF))
 
 
-def feed(t_index, hidden, own, other, gain, w_gu, w_down, waits=()):
+def feed(t_index, hidden, own, other, gain, w_gu, w_down, save, waits=()):
     rows, width = hidden.shape
     units = w_down.shape[0]
-    wide = shaped(rows, units)
+    wide, half = shaped(rows, units), shaped(rows // 2, width)
+    outs = [shaped(rows // 2, width, dtype=F32), half, half, shaped(rows, width)]
+    if save:
+        outs += [shaped(rows, width, dtype=F32), wide, wide, wide]
     return on_core(
         feed_kernel,
         (t_index, hidden, own, other, gain, w_gu, w_down),
-        [shaped(rows, width, dtype=F32), shaped(rows // 2, width, dtype=F32), shaped(rows, width)]
-        + [wide, wide, wide, shaped(rows // 2, width), shaped(rows // 2, width)],
+        outs,
         scratch=weight_scratch(width, units) + [pltpu.VMEM((rows, width), F32)],
-        smem=1, far=2, waits=waits, limit=30, name="feed",
+        smem=1, far=2, waits=waits, limit=14, us=7, name="feed",
     )
 
 
@@ -307,7 +325,7 @@
                 part_ref[part] = (acc[part] + total).astype(BF)
 
 
-def feed_back(t_index, own, other, w_gu, w_down, gate, up, waits=()):
+def feed_back(t_index, own, other, w_gu, w_down, gate, up, waits=(), us=7):
     rows, width = 2 * own.shape[0], own.shape[1]
     units = w_down.shape[0]
     wide = shaped(rows, units)
@@ -316,28 +334,28 @@
         (t_index, own, other, gate, up, w_gu, w_down),
         [wide, wide, shaped(rows, width), shaped(rows, width)],
         scratch=weight_scratch(width, units) + [pltpu.VMEM((rows, width), F32)],
-        smem=1, far=2, waits=waits, limit=26, name="feed_back",
-    )
-
-
-def feed_terms_kernel(y_ref, n_ref, g_ref, u_ref, t0, t1, t2, t3):
-    size = n_ref.shape[1] // 4
-    rows = size // 8
-    for k, out in enumerate((t0, t1, t2, t3)):
-        at = pl.multiple_of(lax.rem(y_ref[0] + k, 4) * size, size)
-        left = n_ref[:, pl.ds(at, size)]
+        smem=1, far=2, waits=waits, limit=15, us=us, name="feed_back",
+    )
+
+
+def feed_terms_kernel(n_ref, g_ref, u_ref, out_ref):
+    rows = n_ref.shape[1] // 32
+    for low in range(0, n_ref.shape[1], 256):
+        left = n_ref[:, low : low + 256]
         for spot, right in enumerate((g_ref, u_ref)):
             term = down_rows(left, right[...]).astype(BF)
-            for index in range(8):
-                out[index, spot * rows : (spot + 1) * rows, :] = term[index * rows : (index + 1) * rows]
-
-
-def feed_terms(y_index, normed, dgate, dup):
+            for index in range(256 // rows):
+                out_ref[low // rows + index, spot * rows : (spot + 1) * rows, :] = term[
+                    index * rows : (index + 1) * rows
+                ]
+
+
+def feed_terms(normed, dgate, dup, waits=()):
     width, units = normed.shape[1], dgate.shape[1]
     return on_core(
-        feed_terms_kernel, (y_index, normed, dgate, dup), [shaped(8, width // 16, units)] * 4,
-        smem=1, limit=16, name="feed_terms",
-    )
+        feed_terms_kernel, (normed, dgate, dup), [shaped(32, width // 16, units)],
+        waits=waits, limit=8, us=BRIEF, name="feed_terms",
+    )[0]
 
 
 def sum_kernel(*refs):
@@ -361,7 +379,7 @@
         out_specs=piece,
         out_shape=shaped(*shape),
         compiler_params=pltpu.CompilerParams(vmem_limit_bytes=8 * 2**20),
-        cost_estimate=pl.CostEstimate(flops=1, bytes_accessed=1, transcendentals=0),
+        cost_estimate=lasting(BRIEF),
         name="summed",
     )(*values, *waits)
 
@@ -393,7 +411,7 @@
     return inner, scale, unit
 
 
-def middle_back(x_index, t_index, grad, middle, own, other, gain, w_out, waits=()):
+def middle_back(x_index, t_index, grad, middle, own, other, gain, w_out, waits=(), us=2.3):
     rows, width = grad.shape
     return on_core(
         middle_back_kernel,
@@ -402,42 +420,43 @@
         + [shaped(rows, PAIR)] * 4
         + [shaped(1, width, dtype=F32)],
         scratch=[pltpu.VMEM((rows, RING * PAIR), BF)],
-        smem=2, waits=waits, limit=20, name="middle_back",
-    )
-
-
-def project_back_kernel(x_ref, t_ref, g0, g1, g2, g3, w_ref, n_ref, keep_ref, send_ref, half_ref, d_ref):
+        smem=2, waits=waits, limit=8, us=us, name="middle_back",
+    )
+
+
+def project_back_kernel(x_ref, t_ref, g0, g1, g2, g3, w_ref, keep_ref, send_ref, d_ref):
     for k, grad in enumerate((g0, g1, g2, g3)):
         for c in range(3):
             d_ref[c, :, heads_at(x_ref, k)] = grad[c]
     for which, part in enumerate(halves(d_ref.shape[1])):
         total = sum(across(d_ref[c, part], w_ref[c]) for c in range(3)).astype(BF)
         put_halves(t_ref, which, keep_ref, send_ref, total)
-    half_ref[...] = n_ref[own_half(t_ref, n_ref.shape[0]), :]
-
-
-def project_back(x_index, t_index, grads, w_qkv, normed, waits=()):
-    rows, width = normed.shape
+
+
+def project_back(x_index, t_index, grads, w_qkv, waits=(), us=2.2):
+    rows, width = grads[0].shape[1], w_qkv.shape[1]
     return on_core(
         project_back_kernel,
-        (x_index, t_index, *grads, w_qkv, normed),
-        [shaped(rows // 2, width)] * 3,
+        (x_index, t_index, *grads, w_qkv),
+        [shaped(rows // 2, width)] * 2,
         scratch=[pltpu.VMEM((3, rows, RING * PAIR), BF)],
-        smem=2, waits=waits, limit=16, name="project_back",
-    )
-
-
-def input_back_kernel(h_ref, dm_ref, p_ref, q_ref, gain_ref, dh_ref, low_ref):
+        smem=2, waits=waits, limit=5, us=us, name="project_back",
+    )
+
+
+def input_back_kernel(t_ref, h_ref, dm_ref, p_ref, q_ref, gain_ref, n_ref, dh_ref, low_ref, half_ref):
     grad = p_ref[...].astype(F32) + q_ref[...].astype(F32)
     total = dm_ref[...] + norm_back(h_ref[...].astype(F32), grad, gain_ref[...])[0]
     dh_ref[...] = total
     low_ref[...] = total.astype(BF)
-
-
-def input_back(hidden, grad_middle, own, other, gain):
-    return on_core(
-        input_back_kernel, (hidden, grad_middle, own, other, gain),
-        [shaped(*hidden.shape, dtype=F32), shaped(*hidden.shape)], limit=10, name="input_back",
+    half_ref[...] = n_ref[own_half(t_ref, n_ref.shape[0]), :]
+
+
+def input_back(t_index, hidden, grad_middle, own, other, gain, normed, us=1.5):
+    return on_core(
+        input_back_kernel, (t_index, hidden, grad_middle, own, other, gain, normed),
+        [shaped(*hidden.shape, dtype=F32), shaped(*hidden.shape), shaped(*hidden.shape)],
+        smem=1, limit=5, us=us, name="input_back",
     )
 
 
@@ -447,7 +466,7 @@
 
 def close(middle, own, other, waits=()):
     return on_core(
-        close_kernel, (middle, own, other), [shaped(*own.shape)], waits=waits, limit=6, name="close"
+        close_kernel, (middle, own, other), [shaped(*own.shape)], waits=waits, limit=4, us=0.7, name="close"
     )[0]
 
 
@@ -487,12 +506,12 @@
         (z_index, act, grad_out, attended, grad_branch),
         [shaped(16, QKV_AT, width)] * 2,
         scratch=[pltpu.VMEM((act.shape[1], width), F32)],
-        smem=1, limit=18, name="early_terms",
+        smem=1, limit=9, us=BRIEF, name="early_terms",
     )
 
 
 def qkv_terms_kernel(x_ref, t_ref, z_ref, n_ref, near_ref, far_ref, g0, g1, g2, g3,
-                     w_ref, gain_ref, two_ref, keep_ref, send_ref, sum_ref, acc):
+                     w_ref, gain_ref, two_ref, keep_ref, send_ref, acc):
     half = near_ref.shape[1]
     rows, wide = n_ref.shape[1] // 32, 3 * PAIR
 
@@ -500,10 +519,12 @@
         return jnp.concatenate([grad[c, at, :] for c in range(3)], axis=1)
 
     acc[...] = down_rows(joined(g0, slice(None)), n_ref[...])
-    for index, grad in enumerate((g1, g2, g3)):
-        acc[...] += down_rows(joined(grad, own_half(t_ref, 2 * half)), near_ref[index]) + down_rows(
-            joined(grad, far_half(t_ref, 2 * half)), far_ref[index]
+    for shift, grad in ((1, g1), (2, g2), (3, g3)):
+        source = lax.rem(x_ref[0] + RING - shift, RING)
+        acc[...] += down_rows(joined(grad, own_half(t_ref, 2 * half)), near_ref[source]) + down_rows(
+            joined(grad, far_half(t_ref, 2 * half)), far_ref[source]
         )
+    sums = []
     for low in range(0, acc.shape[1], 256):
         term = acc[:, low : low + 256].T.astype(BF)
         for index in range(256 // rows):
@@ -515,8 +536,13 @@
         for c in range(3):
             weight = w_ref[c, low : low + 256, heads_at(x_ref, 0)].astype(F32).T
             total += jnp.sum(weight * acc[c * PAIR : (c + 1) * PAIR, low : low + 256], axis=0, keepdims=True)
-        sum_ref[0:1, low : low + 256] = total / gain_ref[:, low : low + 256]
-    sum_ref[1:2, :] = two_ref[...]
+        sums.append(total / gain_ref[:, low : low + 256])
+    sums += [two_ref[:, low : low + 256] for low in range(0, acc.shape[1], 256)]
+    sums = jnp.concatenate(sums)
+    high = sums.astype(BF)
+    sums = jnp.concatenate([high, (sums - high.astype(F32)).astype(BF)])
+    for out in (keep_ref, send_ref):
+        out[:, :, 2 * wide :] = jnp.broadcast_to(sums[None], (out.shape[0], *sums.shape))
 
 
 def qkv_terms(x_index, t_index, z_index, normed, near, far, grads, w_qkv, gain, gain_sum):
@@ -524,17 +550,67 @@
     return on_core(
         qkv_terms_kernel,
         (x_index, t_index, z_index, normed, near, far, *grads, w_qkv, gain, gain_sum),
-        [shaped(16, width // 64, 6 * PAIR)] * 2 + [shaped(2, width, dtype=F32)],
+        [shaped(16, width // 64, width)] * 2,
         scratch=[pltpu.VMEM((3 * PAIR, width), F32)],
-        smem=3, limit=18, name="qkv_terms",
+        smem=3, limit=6, us=BRIEF, name="qkv_terms",
     )
 
 
 def rest_kernel(a_ref, b_ref, c_ref, d_ref, out_ref):
-    wide = c_ref.shape[2]
+    rows, lanes = c_ref.shape[1] // 2, 6 * PAIR
     out_ref[:, :QKV_AT, :] = (a_ref[...].astype(F32) + b_ref[...].astype(F32)).astype(BF)
-    out_ref[:, QKV_AT:, :wide] = (c_ref[...].astype(F32) + d_ref[...].astype(F32)).astype(BF)
-    out_ref[:, QKV_AT:, wide:] = jnp.zeros((out_ref.shape[0], out_ref.shape[1] - QKV_AT, out_ref.shape[2] - wide), BF)
+    late = c_ref[...].astype(F32) + d_ref[...].astype(F32)
+    out_ref[:, QKV_AT:, :lanes] = late[:, :, :lanes].astype(BF)
+    sums = late[:, :rows, lanes:] + late[:, rows:, lanes:]
+    high = sums.astype(BF)
+    out_ref[:, QKV_AT : QKV_AT + rows, lanes:] = high
+    out_ref[:, QKV_AT + rows :, lanes:] = (sums - high.astype(F32)).astype(BF)
+
+
+def finish_kernel(rest_ref, down_ref, out_ref, qkv_ref, gain_ref):
+    count, total, width = rest_ref.shape
+    wide, rows = 3 * PAIR, total - QKV_AT
+
+    def added(low, high):
+        value = rest_ref[0, low:high, :].astype(F32)
+        for source in range(1, count):
+            value += rest_ref[source, low:high, :].astype(F32)
+        return value
+
+    down_ref[...] = added(0, OUT_AT)[:DOWN_ROWS]
+    out_ref[...] = added(OUT_AT, QKV_AT)
+    gains = jnp.zeros((rows, width - 2 * wide), F32)
+    for x in range(RING):
+        value = rest_ref[x, QKV_AT:, :].astype(F32)
+        for source in range(x + RING, count, RING):
+            value += rest_ref[source, QKV_AT:, :].astype(F32)
+        for half in range(2):
+            for c in range(3):
+                low = half * wide + c * PAIR
+                qkv_ref[c, half * rows : (half + 1) * rows, x * PAIR : (x + 1) * PAIR] = value[
+                    :, low : low + PAIR
+                ]
+        gains += value[:, 2 * wide :]
+    gains = gains[: rows // 2] + gains[rows // 2 :]
+    for index in range(rows // 2):
+        low = index % 4 * 256
+        gain_ref[index // 4 : index // 4 + 1, low : low + 256] = gains[index : index + 1]
+
+
+def finish(rest):
+    width = rest.shape[2]
+    rows = 2 * (rest.shape[1] - QKV_AT)
+    return on_core(
+        finish_kernel,
+        (rest,),
+        [
+            shaped(DOWN_ROWS, width, dtype=F32),
+            shaped(QKV_AT - OUT_AT, width, dtype=F32),
+            shaped(3, rows, RING * PAIR, dtype=F32),
+            shaped(2, width, dtype=F32),
+        ],
+        limit=4, us=BRIEF, name="finish",
+    )
 
 
 def rest_sum(early, early_got, late, late_got, waits=()):
@@ -553,7 +629,7 @@
         out_specs=pl.BlockSpec((count // 4, total, width), lambda i: (i, 0, 0)),
         out_shape=shaped(count, total, width),
         compiler_params=pltpu.CompilerParams(vmem_limit_bytes=8 * 2**20),
-        cost_estimate=pl.CostEstimate(flops=1, bytes_accessed=1, transcendentals=0),
+        cost_estimate=lasting(BRIEF),
         name="rest_sum",
     )(early, early_got, late, late_got, *waits)
 
@@ -642,12 +718,12 @@
             pltpu.VMEM((PAIR, LEN), BF),
             pltpu.VMEM((PAIR, QUERIES), F32),
         ],
-        smem=2, waits=waits, limit=16, name="attend",
+        smem=2, waits=waits, limit=12, us=13, name="attend",
     )
 
 
 def attend_back_kernel(x_ref, ends_ref, mix_ref, m0, m1, m2, m3, d0, d1, d2, d3, lse_ref, out_t,
-                       dv1_ref, cos_ref, sin_ref, g0, g1, g2, g3, keys, values, queries, grads,
+                       dv1_ref, cos_ref, sin_ref, g0, g1, g2, g3, dv_ref, keys, values, queries, grads,
                        key_t, query_t, grad_t, delta, grad_k, grad_v, grad_q_t):
     x = x_ref[0]
     lanes = lax.broadcasted_iota(jnp.int32, (BLOCK, PAIR), 1)
@@ -710,17 +786,17 @@
             grad_q = grad_q_t[:, at].T * HD ** (-0.5)
             out[0, inside, :] = turned(grad_q, cosine, sine, -1.0).astype(BF)
             out[1, inside, :] = turned(grad_k[at, :], cosine, sine, -1.0).astype(BF)
-            out[2, inside, :] = (
-                mix_ref[0] * grad_v[at, :] + mix_ref[1] * dv1_ref[shift, inside, :].astype(F32)
-            ).astype(BF)
-
-
-def attend_back(x_index, ends, mix, messages, arrived, lse, out_t, dv1, cosine, sine, waits=()):
+            grad_value = mix_ref[0] * grad_v[at, :] + mix_ref[1] * dv1_ref[shift, inside, :].astype(F32)
+            out[2, inside, :] = grad_value.astype(BF)
+            dv_ref[shift, inside, :] = grad_value.astype(BF)
+
+
+def attend_back(x_index, ends, mix, messages, arrived, lse, out_t, dv1, cosine, sine, waits=(), us=20):
     rows = messages[0].shape[1]
     return on_core(
         attend_back_kernel,
         (x_index, ends, mix, *messages, *arrived, lse, out_t, dv1, cosine, sine),
-        [shaped(3, rows, PAIR)] * 4,
+        [shaped(3, rows, PAIR)] * 4 + [shaped(RING, rows, PAIR)],
         scratch=[pltpu.VMEM((2, LEN, PAIR), BF)] * 4
         + [pltpu.VMEM((PAIR, LEN), BF)] * 3
         + [
@@ -729,7 +805,7 @@
             pltpu.VMEM((LEN, PAIR), F32),
             pltpu.VMEM((PAIR, LEN), F32),
         ],
-        smem=3, waits=waits, limit=24, name="attend_back",
+        smem=3, waits=waits, limit=13, us=us, name="attend_back",
     )
 
 
@@ -737,12 +813,16 @@
     return [values[0]] + [moved(values[shift], "x", sign * shift) for shift in range(1, RING)]
 
 
-def all_to_all(value, kinds):
-    groups = {}
+def groups(kinds):
+    found = {}
     for index in range(32):
         place = {"y": index // 8, "z": index // 4 % 2, "x": index % 4}
-        groups.setdefault(tuple(place[k] for k in "yzx" if k not in kinds), []).append(index)
-    return lax.all_to_all(value, "dp", 0, 0, axis_index_groups=list(groups.values()))
+        found.setdefault(tuple(place[k] for k in "yzx" if k not in kinds), []).append(index)
+    return list(found.values())
+
+
+def all_to_all(value, kinds):
+    return lax.all_to_all(value, "dp", 0, 0, axis_index_groups=groups(kinds))
 
 
 def per_device(tokens, cotangent, doc_lengths, gains, wqkv, wo, wgu, wd):
@@ -750,9 +830,7 @@
     tensor = lax.axis_index("tensor")
     position = lax.axis_index("dp")
     y, z, x = position // 8, position // 4 % 2, position % 4
-    x_index, y_index, z_index, t_index = [
-        v.astype(jnp.int32).reshape(1) for v in (x, y, z, tensor)
-    ]
+    x_index, z_index, t_index = [v.astype(jnp.int32).reshape(1) for v in (x, z, tensor)]
     width = tokens.shape[2]
 
     def in_order(keep, got):
@@ -768,7 +846,6 @@
     ends = jnp.cumsum(lens.reshape(4), dtype=jnp.int32)
     cosine, sine = rotary_tables()
     w_qkv = jnp.transpose(wqkv[0], (1, 0, 2))
-    w_gu = jnp.transpose(wgu[0], (1, 0, 2))
     w_out, w_down = wo[0], wd[0]
     gain_one, gain_two = gains[0, 0:1], gains[0, 1:2]
     mix = jnp.where(first, jnp.array([1.0, 0.0], F32), jnp.array([0.5, 0.5], F32))
@@ -778,104 +855,98 @@
         return lax.ppermute(value, "section", pairs)
 
     def first_half(own, value_first):
-        *messages, normed, value, hidden = project(
+        *messages, normed, value, hidden, zero = project(
             x_index, t_index, mix, own, swapped(own), gain_one, w_qkv, value_first, cosine, sine
         )
-        return out_and_back(messages, 1), normed, value, hidden
-
-    def second_half(hidden, outs, value, waits=()):
+        return out_and_back(messages, 1), normed, value, hidden, zero
+
+    def second_half(hidden, outs, value, save, waits=()):
         attended, part, value = branch(x_index, out_and_back(outs, -1), w_out, value, waits=waits)
-        middle, mine, normed_two, gate, up, act, keep, send = feed(
-            t_index, hidden, part, swapped(part), gain_two, w_gu, w_down
+        mine, keep, send, normed_two, *more = feed(
+            t_index, hidden, part, swapped(part), gain_two, w_gu, w_down, save
         )
-        return mine, keep, swapped(send), value, (attended, middle, normed_two, gate, up, act)
+        return mine, keep, swapped(send), value, (attended, normed_two, *more)
 
     own_rows = regrouped(tokens).reshape(2 * BLOCK, width)
     no_value = jnp.zeros((RING, 4 * BLOCK, PAIR), BF)
 
-    messages, _, value, hidden = first_half(own_rows, no_value)
+    messages, _, value, hidden, zero = first_half(own_rows, no_value)
+    w_gu = jnp.transpose(wgu[0] + zero[0, 0], (1, 0, 2))
     *outs, _, _ = attend(x_index, ends, messages, waits=(seen(w_gu),))
     cot_keep, cot_send = pick(z_index, cotangent, waits=(seen(outs[0]),))
     top_grad = in_order(cot_keep, moved(cot_send, "z", 1)).reshape(2 * BLOCK, width)
-    mine, keep, got, value, _ = second_half(hidden, outs, value)
+    mine, keep, got, value, _ = second_half(hidden, outs, value, False)
     v_in = handed(value, [(0, 1)])
     result = close(mine, keep, got, waits=(seen(v_in),))
     own = jnp.where(first, own_rows, handed(result, [(0, 1)]))
 
-    messages, normed, value, hidden = first_half(own, v_in)
+    messages, normed, value, hidden, _ = first_half(own, v_in)
     *outs, lse, out_t = attend(x_index, ends, messages)
-    mine, keep, got, _, saved = second_half(hidden, outs, value, waits=(seen(top_grad),))
-    attended, middle, normed_two, gate, up, act = saved
-    acts = regrouped(close(mine, keep, got).reshape(2, BLOCK, width))[None]
-
-    def first_back(own_grad, waits=()):
-        return feed_back(t_index, own_grad, swapped(own_grad), w_gu, w_down, gate, up, waits=waits)
-
-    def second_back(grad, part, waits=()):
+    mine, keep, got, _, saved = second_half(hidden, outs, value, True, waits=(seen(top_grad),))
+    attended, normed_two, middle, gate, up, act = saved
+    def first_back(own_grad, us=7):
+        return feed_back(t_index, own_grad, swapped(own_grad), w_gu, w_down, gate, up, us=us)
+
+    def second_back(grad, part, waits=(), us=2.3):
         grad_middle, grad_branch, *sends, gain_sum = middle_back(
-            x_index, t_index, grad, middle, part, swapped(part), gain_two, w_out, waits=waits
+            x_index, t_index, grad, middle, part, swapped(part), gain_two, w_out, waits=waits, us=us
         )
         return grad_middle, grad_branch, out_and_back(sends, 1), gain_sum
 
-    def third_back(arrived, grad_value, waits=()):
+    def third_back(arrived, grad_value, waits=(), us=20):
         return attend_back(
-            x_index, ends, mix_back, messages, arrived, lse, out_t, grad_value, cosine, sine, waits=waits
+            x_index, ends, mix_back, messages, arrived, lse, out_t, grad_value, cosine, sine, waits=waits, us=us
         )
 
-    def fourth_back(grads, grad_middle, waits=()):
-        keep, send, half = project_back(
-            x_index, t_index, out_and_back(grads, -1), w_qkv, normed, waits=waits
+    def fourth_back(grads, grad_middle, waits=(), us=2):
+        keep, send = project_back(
+            x_index, t_index, out_and_back(grads, -1), w_qkv, waits=waits, us=us
         )
-        return *input_back(own, grad_middle, keep, swapped(send), gain_one), half, keep
+        return *input_back(
+            t_index, own, grad_middle, keep, swapped(send), gain_one, normed, us=us
+        ), keep
 
     _, _, part, grad = first_back(top_grad)
     grad_middle, _, arrived, _ = second_back(grad, part)
-    grads = third_back(arrived, no_value, waits=(seen(acts[0]),))
-    gv_in = handed(jnp.stack([grad[2] for grad in grads]), [(1, 0)])
-    _, grad_hidden, half, _ = fourth_back(grads, grad_middle, waits=(seen(gv_in),))
-    near = [moved(half, "x", k) for k in range(1, RING)]
+    *grads, grad_value = third_back(arrived, no_value)
+    result = close(mine, keep, got, waits=(seen(grad_value),))
+    acts = regrouped(result.reshape(2, BLOCK, width))[None]
+    gv_in = handed(grad_value, [(1, 0)])
+    _, grad_hidden, half, _ = fourth_back(
+        grads, grad_middle, waits=(seen(gv_in), seen(acts[0, 0]))
+    )
+    near = lax.all_gather(half, "dp", axis_index_groups=groups("x"))
     own_grad = jnp.where(first, handed(grad_hidden, [(1, 0)]), top_grad)
 
-    dgate, dup, part, grad_out = first_back(own_grad, waits=[seen(rows) for rows in near])
-    feed_term = feed_terms(y_index, normed_two, dgate, dup)
-    feed_got = [moved(feed_term[k], "y", k) for k in range(1, 4)]
-    grad_middle, grad_branch, arrived, gain_sum = second_back(grad_out, part, waits=(seen(feed_term[0]),))
+    dgate, dup, part, grad_out = first_back(own_grad, us=BRIEF)
+    grad_middle, grad_branch, arrived, gain_sum = second_back(grad_out, part, us=BRIEF)
+    feed_term = feed_terms(normed_two, dgate, dup, waits=(seen(grad_branch),))
+    feed_sum = lax.psum_scatter(
+        feed_term, "dp", scatter_dimension=0, axis_index_groups=groups("y"), tiled=True
+    )
     early, early_send = early_terms(z_index, act, grad_out, attended, grad_branch)
     early_got = moved(early_send, "z", 1)
-    near = jnp.stack(near)
     far = swapped(near)
-    grads = third_back(arrived, gv_in, waits=(seen(far), seen(early)))
-    late, late_send, gain_total = qkv_terms(
+    *grads, _ = third_back(arrived, gv_in, waits=(seen(far), seen(early), seen(feed_term)), us=BRIEF)
+    late, late_send = qkv_terms(
         x_index, t_index, z_index, normed, near, far, grads, w_qkv, gain_one, gain_sum
     )
     late_got = moved(late_send, "z", 1)
-    grad_hidden, _, _, last = fourth_back(grads, grad_middle, waits=(seen(late),))
+    grad_hidden, _, _, last = fourth_back(grads, grad_middle, waits=(seen(late),), us=BRIEF)
+    rest = rest_sum(early, early_got, late, late_got, waits=(seen(last),))
     dins = regrouped(grad_hidden.reshape(2, BLOCK, width))[None]
-
-    rows = width // 32
-    feed_sum = summed([feed_term[0], *feed_got], waits=(seen(last),))
-    feed_share = jnp.sum(all_to_all(feed_sum, "zx").astype(F32), axis=0).reshape(2, rows, -1)
-    rest = rest_sum(early, early_got, late, late_got, waits=(seen(feed_sum),))
-    rest = all_to_all(rest, "yx").astype(F32)
-    down_share = jnp.sum(rest[:, :DOWN_ROWS], axis=0)
-    out_share = jnp.sum(rest[:, OUT_AT:QKV_AT], axis=0)
-    qkv_share = jnp.sum(
-        rest[:, QKV_AT:, : 6 * PAIR].reshape(4, RING, rows // 2, 2, 3, PAIR), axis=0
-    )
-    qkv_share = jnp.transpose(qkv_share, (2, 1, 3, 0, 4)).reshape(rows, 3, RING * PAIR)
-
-    gain_total = gain_total + swapped(gain_total)
-    gain_total = jnp.sum(
-        lax.all_to_all(jnp.broadcast_to(gain_total, (32, *gain_total.shape)), "dp", 0, 0), axis=0
-    )
+    feed_sum = summed([feed_sum], waits=(seen(rest), seen(dins[0, 0])))
+    feed_share = jnp.sum(all_to_all(feed_sum, "zx").astype(F32), axis=0)
+    feed_share = feed_share.reshape(2, width // 32, -1)
+    down_share, out_share, qkv_share, gain_total = finish(all_to_all(rest, "yx"))
     return (
         acts,
         dins,
-        qkv_share[None],
+        jnp.transpose(qkv_share, (1, 0, 2))[None],
         out_share[None],
         jnp.transpose(feed_share, (1, 0, 2))[None],
         down_share[None],
-        gain_total[None],
+        (gain_total + swapped(gain_total))[None],
     )
 
 

time: 498 us -> 468 us (0.940)
  waiting for transfers between devices: 212 us -> 190 us
  between operations: 1.96 us -> 16.8 us
  starting transfers between devices: 81.5 us -> 68.3 us
  Pallas kernels: 147 us -> 135 us
  local copies, waits for them, and re-layouts: 34.5 us -> 45.9 us
  other arithmetic: 11.4 us -> 5.65 us
    ppermute x36 -> x30, waiting for transfers between devices: 132 us -> 96.9 us  [moved(): return lax.ppermute(value, 'dp', along(kind, shift))]
    unnamed x124 -> x162, local copies, waits for them, and re-layouts: 28 us -> 41.9 us
    ppermute x36 -> x30, starting transfers between devices: 54.2 us -> 46.2 us  [moved(): return lax.ppermute(value, 'dp', along(kind, shift))]
    ppermute x4, waiting for transfers between devices: 34.6 us -> 41.5 us  [handed(): return lax.ppermute(value, 'section', pairs)]
    pallas_call x24 -> x25, Pallas kernels: 139 us -> 133 us  [on_core(): pl.pallas_call(body, in_specs=spots, out_specs=[pl.BlockSpec(memory_space...]
    all_to_all x3 -> x2, starting transfers between devices: 14.9 us -> 8.96 us  [all_to_all(): return lax.all_to_all(value, 'dp', 0, 0, axis_index_groups=groups(kinds))]
    all_to_all x3 -> x2, waiting for transfers between devices: 33.6 us -> 35.7 us  [all_to_all(): return lax.all_to_all(value, 'dp', 0, 0, axis_index_groups=groups(kinds))]
  transfers between devices with their start and end apart: 57 -> 52, of which waited for: 38 -> 36; matrix products, arithmetic and copies ran while one was open for 3% -> 2% of each run, Pallas kernels for 19% -> 21%
where the time goes in v3:
time: 468 us; the launch traced here: 462 us
  waiting for transfers between devices  190 us (41%)
  Pallas kernels  135 us (29%)
  starting transfers between devices  68.3 us (15%)
  local copies, waits for them, and re-layouts  45.9 us (10%)
  between operations  16.8 us (4%)
  other arithmetic  5.65 us (1%)
    pallas_call x25, Pallas kernels, on_core(): pl.pallas_call(body, in_specs=spots, out_specs=[pl.BlockSpec(memory_space...  133 us
    ppermute x30, waiting for transfers between devices, moved(): return lax.ppermute(value, 'dp', along(kind, shift))  96.9 us
    ppermute x30, starting transfers between devices, moved(): return lax.ppermute(value, 'dp', along(kind, shift))  46.2 us
    unnamed x162, local copies, waits for them, and re-layouts  41.9 us
    ppermute x4, waiting for transfers between devices, handed(): return lax.ppermute(value, 'section', pairs)  41.5 us
    all_to_all x2, waiting for transfers between devices, all_to_all(): return lax.all_to_all(value, 'dp', 0, 0, axis_index_groups=groups(kinds))  35.7 us
    ppermute x14, waiting for transfers between devices, swapped(): return lax.ppermute(value, 'tensor', [(0, 1), (1, 0)])  16.2 us
    ppermute x4, starting transfers between devices, handed(): return lax.ppermute(value, 'section', pairs)  10.6 us
  transfers between devices with their start and end apart: 52, of which 36 were waited for; matrix products, arithmetic and copies ran while one was open for 2% of the time, Pallas kernels for 21%

profile of v3, /device:TPU:0, one launch (start us, length us, event | category | flops | bytes accessed | tf_op | source)
XLA Modules:
  0.0 462.3 jit_solution(6094321571190577504)
XLA Ops:
  9.2 4.0 collective-permute-start
  13.2 6.3 %collective-permute-done = bf16[128,1024]{1,0:T(8,128)(2,1)S(1)} collective-permute-done((bf16[128,1024]{1,0:T(8,128)(2,1)S(1)}, bf16[128,1024]{1,0:T(8,128)(2,1)S(1)}, u32[]{:S(2)}, u32[]{:S(2)}) %collective-permute-start) | collective-permute-done | bytes 262176 | tf_op jit(solution)/shard_map/ppermute | solution.py:40
  28.9 3.9 project.2
  41.1 4.5 collective-permute-done.2.refs_3_
  45.7 9.4 %collective-permute-done.3.refs_4_ = bf16[3,512,128]{2,1,0:T(8,128)(2,1)S(1)} collective-permute-done((bf16[3,512,128]{2,1,0:T(8,128)(2,1)S(1)}, bf16[3,512,128]{2,1,0:T(8,128)(2,1)S(1)}, u32[]{:S(2)}, u32[]{:S(2)}) %collective-permute-start.3) | collective-permute-done | bytes 393248 | tf_op jit(solution)/shard_map/ppermute | solution.py:40
  55.1 13.6 %attend.2 = (bf16[512,128]{1,0:T(8,128)(2,1)S(1)}, bf16[512,128]{1,0:T(8,128)(2,1)S(1)}, bf16[512,128]{1,0:T(8,128)(2,1)S(1)}, bf16[512,128]{1,0:T(8,128)(2,1)S(...) custom-call(s32[1]{0:T(128)} %bitcast.1.refs_0_, s32[4]{0:T(128)S(1)} %bitcast.103, ...), custom_call_target="tpu_custom_call" | custom-call | flops 14300000256 | bytes 46800000 | tf_op jit(solution)/shard_map/attend/pallas_call | solution.py:87
  72.7 4.0 collective-permute-done.5.refs_2_
  84.9 8.4 %feed.2 = (f32[256,1024]{1,0:T(8,128)S(1)}, bf16[256,1024]{1,0:T(8,128)(2,1)S(1)}, bf16[256,1024]{1,0:T(8,128)(2,1)S(1)}, bf16[512,1024]{1,0:T(8,128)(2,1)}) custom-call(s32[1]{0:T(128)} %bitcast.refs_1_.refs_0_, bf16[512,1024]{1,0:T(8,128)(2,1)S(1)} %get-tuple-element.90.refs_1_, bf16[512,1024]{1,0:T(8,128)(2,1)S(1)} %get-tuple-element.101.refs_2_, ...), custom_call_target="tpu_custom_call" | custom-call | flops 7699999744 | bytes 25200000 | tf_op jit(solution)/shard_map/feed/pallas_call | solution.py:87
  96.8 4.7 %collective-permute-start.11 = (bf16[256,1024]{1,0:T(8,128)(2,1)S(1)}, bf16[256,1024]{1,0:T(8,128)(2,1)S(1)}, u32[]{:S(2)}, u32[]{:S(2)}) collective-permute-start(bf16[256,1024]{1,0:T(8,128)(2,1)S(1)} %close.2), channel_id=1, source_target_pairs={{0,64},{1,65},{2,66},{3,67},{4,68},{5,69},{6,70},{7,71},{8,72},{9,... | collective-permute-start | bytes 1572872 | tf_op jit(solution)/shard_map/ppermute | solution.py:855
  101.5 11.0 %collective-permute-done.11 = bf16[256,1024]{1,0:T(8,128)(2,1)S(1)} collective-permute-done((bf16[256,1024]{1,0:T(8,128)(2,1)S(1)}, bf16[256,1024]{1,0:T(8,128)(2,1)S(1)}, u32[]{:S(2)}, u32[]{:S(2)}) %collective-permute-start.11) | collective-permute-done | bytes 524320 | tf_op jit(solution)/shard_map/ppermute | solution.py:855
  114.6 4.1 project.3
  122.5 3.8 collective-permute-start.19
  126.3 13.3 %collective-permute-done.13.refs_3_.refs_4_ = bf16[3,512,128]{2,1,0:T(8,128)(2,1)S(1)} collective-permute-done((bf16[3,512,128]{2,1,0:T(8,128)(2,1)S(1)}, bf16[3,512,128]{2,1,0:T(8,128)(2,1)S(1)}, u32[]{:S(2)}, u32[]{:S(2)}) %collective-permute-start.13) | collective-permute-done | bytes 393248 | tf_op jit(solution)/shard_map/ppermute | solution.py:40
  140.2 12.7 %attend.3 = (bf16[512,128]{1,0:T(8,128)(2,1)S(1)}, bf16[512,128]{1,0:T(8,128)(2,1)S(1)}, bf16[512,128]{1,0:T(8,128)(2,1)S(1)}, bf16[512,128]{1,0:T(8,128)(2,1)S(...) custom-call(s32[1]{0:T(128)} %bitcast.1.refs_0_, s32[4]{0:T(128)S(1)} %bitcast.104, ...), custom_call_target="tpu_custom_call" | custom-call | flops 14300000256 | bytes 46800000 | tf_op jit(solution)/shard_map/attend/pallas_call | solution.py:87
  156.4 4.5 collective-permute-done.16.refs_2_
  169.4 7.2 %feed.3 = (f32[256,1024]{1,0:T(8,128)S(1)}, bf16[256,1024]{1,0:T(8,128)(2,1)S(1)}, bf16[256,1024]{1,0:T(8,128)(2,1)S(1)}, bf16[512,1024]{1,0:T(8,128)(2,1)S(1)},...) custom-call(s32[1]{0:T(128)} %bitcast.refs_1_.refs_0_, ...), custom_call_target="tpu_custom_call" | custom-call | flops 7699999744 | bytes 25200000 | tf_op jit(solution)/shard_map/feed/pallas_call | solution.py:87
  178.8 7.2 %feed_back.2 = (bf16[512,1408]{1,0:T(8,128)(2,1)}, bf16[512,1408]{1,0:T(8,128)(2,1)}, bf16[512,1024]{1,0:T(8,128)(2,1)S(1)}, bf16[512,1024]{1,0:T(8,128)(2,1)S(1)}) custom-call(s32[1]{0:T(128)} %bitcast.refs_1_.refs_0_, bf16[256,1024]{1,0:T(8,128)(2,1)S(1)} %bitcast.89, bf16[256,1024]{1,0:T(8,128)(2,1)S(1)} %collective-permute-done.22.refs_2_, ...), custom_call_target="tpu_custom_call" | custom-call | flops 7699999744 | bytes 25200000 | tf_op jit(solution)/shard_map/feed_back/pallas_call | solution.py:87
  195.4 6.2 %collective-permute-done.24.refs_8_ = bf16[512,128]{1,0:T(8,128)(2,1)S(1)} collective-permute-done((bf16[512,128]{1,0:T(8,128)(2,1)S(1)}, bf16[512,128]{1,0:T(8,128)(2,1)S(1)}, u32[]{:S(2)}, u32[]{:S(2)}) %collective-permute-start.24) | collective-permute-done | bytes 131104 | tf_op jit(solution)/shard_map/ppermute | solution.py:40
  202.2 20.0 %attend_back.2 = (bf16[3,512,128]{2,1,0:T(8,128)(2,1)S(1)}, bf16[3,512,128]{2,1,0:T(8,128)(2,1)S(1)}, bf16[3,512,128]{2,1,0:T(8,128)(2,1)S(1)}, bf16[3,512,128]{2,1,0:T(8,128)(2,1)S(1)}, bf16[4,512,128]{2,1,0:T(8,128)(2,1)S(1)}) custom-call(s32[1]{0:T(128)} %bitcast.1.refs_0_, s32[4]{0:T(128)S(1)} %bitcast.105, f32[2]{0:T(128)S(1)} %broadcast_select_fusion.2.refs_2_, ...), custom_call_target="tpu_custom_call" | custom-call | flops 22000001024 | bytes 72000000 | tf_op jit(solution)/shard_map/attend_back/pallas_call | solution.py:87
  222.5 3.7 collective-permute-start.27
  231.8 12.7 %collective-permute-done.31.refs_13_ = bf16[4,512,128]{2,1,0:T(8,128)(2,1)S(1)} collective-permute-done((bf16[4,512,128]{2,1,0:T(8,128)(2,1)S(1)}, bf16[4,512,128]{2,1,0:T(8,128)(2,1)S(1)}, u32[]{:S(2)}, u32[]{:S(2)}) %collective-permute-start.31) | collective-permute-done | bytes 524320 | tf_op jit(solution)/shard_map/ppermute | solution.py:855
  258.8 14.8 %collective-permute-done.33 = bf16[256,1024]{1,0:T(8,128)(2,1)S(1)} collective-permute-done((bf16[256,1024]{1,0:T(8,128)(2,1)}, bf16[256,1024]{1,0:T(8,128)(2,1)S(1)}, u32[]{:S(2)}, u32[]{:S(2)}) %collective-permute-start.33) | collective-permute-done | bytes 524320 | tf_op jit(solution)/shard_map/ppermute | solution.py:855
  282.8 7.2 %feed_back.3 = (bf16[512,1408]{1,0:T(8,128)(2,1)S(1)}, bf16[512,1408]{1,0:T(8,128)(2,1)S(1)}, bf16[512,1024]{1,0:T(8,128)(2,1)S(1)}, bf16[512,1024]{1,0:T(8,128)(2,1)S(1)}) custom-call(s32[1]{0:T(128)} %bitcast.refs_1_.refs_0_, bf16[256,1024]{1,0:T(8,128)(2,1)S(1)} %broadcast_select_fusion.refs_1_, bf16[256,1024]{1,0:T(8,128)(2,1)S(1)} %collective-permute-done.34.refs_2_, ...), custom_call_target="tpu_custom_call" | custom-call | flops 1100000 | bytes 3600 | tf_op jit(solution)/shard_map/feed_back/pallas_call | solution.py:87
  310.9 3.9 early_terms.1
  319.8 6.4 %collective-permute-done.36.refs_8_ = bf16[512,128]{1,0:T(8,128)(2,1)S(1)} collective-permute-done((bf16[512,128]{1,0:T(8,128)(2,1)}, bf16[512,128]{1,0:T(8,128)(2,1)S(1)}, u32[]{:S(2)}, u32[]{:S(2)}) %collective-permute-start.36) | collective-permute-done | bytes 131104 | tf_op jit(solution)/shard_map/ppermute | solution.py:40
  327.0 20.8 %attend_back.3 = (bf16[3,512,128]{2,1,0:T(8,128)(2,1)S(1)}, bf16[3,512,128]{2,1,0:T(8,128)(2,1)S(1)}, bf16[3,512,128]{2,1,0:T(8,128)(2,1)S(1)}, bf16[3,512,128]{2,1,0:T(8,128)(2,1)S(1)}, bf16[4,512,128]{2,1,0:T(8,128)(2,1)}) custom-call(s32[1]{0:T(128)} %bitcast.1.refs_0_, s32[4]{0:T(128)S(1)} %bitcast.106, f32[2]{0:T(128)S(1)} %copy-done.65, ...), custom_call_target="tpu_custom_call" | custom-call | flops 1100000 | bytes 3600 | tf_op jit(solution)/shard_map/attend_back/pallas_call | solution.py:87
  357.2 15.4 %collective-permute-done.40.refs_3_ = bf16[3,512,128]{2,1,0:T(8,128)(2,1)S(1)} collective-permute-done((bf16[3,512,128]{2,1,0:T(8,128)(2,1)S(1)}, bf16[3,512,128]{2,1,0:T(8,128)(2,1)S(1)}, u32[]{:S(2)}, u32[]{:S(2)}) %collective-permute-start.40) | collective-permute-done | bytes 393248 | tf_op jit(solution)/shard_map/ppermute | solution.py:40
  382.6 4.7 %all-to-all-start = ((bf16[16,80,1024]{2,1,0:T(8,128)(2,1)}), bf16[16,80,1024]{2,1,0:T(8,128)(2,1)S(1)}, u32[]{:S(2)}, u32[]{:S(2)}) async-start(bf16[16,80,1024]{2,1,0:T(8,128)(2,1)} %rest_sum.1), calls=%async_computation | async-start | bytes 5242880 | tf_op jit(solution)/shard_map/all_to_all | solution.py:825
  397.2 8.3 %collective-permute-done.44 = bf16[128,1024]{1,0:T(8,128)(2,1)S(1)} collective-permute-done((bf16[128,1024]{1,0:T(8,128)(2,1)S(1)}, bf16[128,1024]{1,0:T(8,128)(2,1)S(1)}, u32[]{:S(2)}, u32[]{:S(2)}) %collective-permute-start.44) | collective-permute-done | bytes 262176 | tf_op jit(solution)/shard_map/ppermute | solution.py:40
  409.3 17.8 %all-to-all-done.refs_0_ = bf16[16,80,1024]{2,1,0:T(8,128)(2,1)S(1)} async-done(((bf16[16,80,1024]{2,1,0:T(8,128)(2,1)}), bf16[16,80,1024]{2,1,0:T(8,128)(2,1)S(1)}, u32[]{:S(2)}, u32[]{:S(2)}) %all-to-all-start) | async-done | bytes 2621472 | tf_op jit(solution)/shard_map/all_to_all | solution.py:825
  427.1 4.3 all-to-all-start.1
  434.0 18.0 %all-to-all-done.1 = bf16[8,64,1408]{2,1,0:T(8,128)(2,1)} async-done(((bf16[8,64,1408]{2,1,0:T(8,128)(2,1)}), bf16[8,64,1408]{2,1,0:T(8,128)(2,1)}, u32[]{:S(2)}, u32[]{:S(2)}) %all-to-all-start.1) | async-done | bytes 1441824 | tf_op jit(solution)/shard_map/all_to_all | solution.py:825
  (307 shorter events, 158.7 us)
Async XLA Ops:
  8.0 297.4 %all-gather.3.cloned.1.call-start = ((), (), s32[]{:S(2)}) async-start(), calls=%async_computation.4 | async-start | bytes 2621440 | tf_op jit(solution)/shard_map/all_gather | solution.py:918
  9.2 10.3 %collective-permute-start = (bf16[128,1024]{1,0:T(8,128)(2,1)S(1)}, bf16[128,1024]{1,0:T(8,128)(2,1)S(1)}, u32[]{:S(2)}, u32[]{:S(2)}) collective-permute-start(bf16[128,1024]{1,0:T(8,128)(2,1)S(1)} %get-tuple-element.190), channel_id=1, source_target_pairs={{0,4},{1,5},{2,6},{3,7},{4,0},{5,1},{6,2},{7,3},{8,12},{9,13},{10,... | collective-permute-start | bytes 786440 | tf_op jit(solution)/shard_map/ppermute | solution.py:40
  33.3 12.4 %collective-permute-start.2 = (bf16[3,512,128]{2,1,0:T(8,128)(2,1)S(1)}, bf16[3,512,128]{2,1,0:T(8,128)(2,1)S(1)}, u32[]{:S(2)}, u32[]{:S(2)}) collective-permute-start(bf16[3,512,128]{2,1,0:T(8,128)(2,1)S(1)} %get-tuple-element.92), channel_id=1, source_target_pairs={{0,1},{1,2},{2,3},{3,0},{4,5},{5,6},{6,7},{7,4},{8,9},{9,10},{10,1... | collective-permute-start | bytes 1179656 | tf_op jit(solution)/shard_map/ppermute | solution.py:40
  34.8 20.3 %collective-permute-start.3 = (bf16[3,512,128]{2,1,0:T(8,128)(2,1)S(1)}, bf16[3,512,128]{2,1,0:T(8,128)(2,1)S(1)}, u32[]{:S(2)}, u32[]{:S(2)}) collective-permute-start(bf16[3,512,128]{2,1,0:T(8,128)(2,1)S(1)} %get-tuple-element.93), channel_id=1, source_target_pairs={{0,2},{1,3},{2,0},{3,1},{4,6},{5,7},{6,4},{7,5},{8,10},{9,11},{10,... | collective-permute-start | bytes 1179656 | tf_op jit(solution)/shard_map/ppermute | solution.py:40
  37.5 17.6 %collective-permute-start.4 = (bf16[3,512,128]{2,1,0:T(8,128)(2,1)S(1)}, bf16[3,512,128]{2,1,0:T(8,128)(2,1)S(1)}, u32[]{:S(2)}, u32[]{:S(2)}) collective-permute-start(bf16[3,512,128]{2,1,0:T(8,128)(2,1)S(1)} %get-tuple-element.94), channel_id=1, source_target_pairs={{0,3},{1,0},{2,1},{3,2},{4,7},{5,4},{6,5},{7,6},{8,11},{9,8},{10,9... | collective-permute-start | bytes 1179656 | tf_op jit(solution)/shard_map/ppermute | solution.py:40
  81.6 15.0 %collective-permute-start.10 = (bf16[4,512,128]{2,1,0:T(8,128)(2,1)S(1)}, bf16[4,512,128]{2,1,0:T(8,128)(2,1)S(1)}, u32[]{:S(2)}, u32[]{:S(2)}) collective-permute-start(bf16[4,512,128]{2,1,0:T(8,128)(2,1)S(1)} %get-tuple-element.105), channel_id=1, source_target_pairs={{0,64},{1,65},{2,66},{3,67},{4,68},{5,69},{6,70},{7,71},{8,72},{9,... | collective-permute-start | bytes 1572872 | tf_op jit(solution)/shard_map/ppermute | solution.py:855
  96.8 15.7 %collective-permute-start.11 = (bf16[256,1024]{1,0:T(8,128)(2,1)S(1)}, bf16[256,1024]{1,0:T(8,128)(2,1)S(1)}, u32[]{:S(2)}, u32[]{:S(2)}) collective-permute-start(bf16[256,1024]{1,0:T(8,128)(2,1)S(1)} %close.2), channel_id=1, source_target_pairs={{0,64},{1,65},{2,66},{3,67},{4,68},{5,69},{6,70},{7,71},{8,72},{9,... | collective-permute-start | bytes 1572872 | tf_op jit(solution)/shard_map/ppermute | solution.py:855
  118.8 20.8 %collective-permute-start.13 = (bf16[3,512,128]{2,1,0:T(8,128)(2,1)S(1)}, bf16[3,512,128]{2,1,0:T(8,128)(2,1)S(1)}, u32[]{:S(2)}, u32[]{:S(2)}) collective-permute-start(bf16[3,512,128]{2,1,0:T(8,128)(2,1)S(1)} %get-tuple-element.108), channel_id=1, source_target_pairs={{0,1},{1,2},{2,3},{3,0},{4,5},{5,6},{6,7},{7,4},{8,9},{9,10},{10,1... | collective-permute-start | bytes 1179656 | tf_op jit(solution)/shard_map/ppermute | solution.py:40
  118.8 20.8 %collective-permute-start.14 = (bf16[3,512,128]{2,1,0:T(8,128)(2,1)S(1)}, bf16[3,512,128]{2,1,0:T(8,128)(2,1)S(1)}, u32[]{:S(2)}, u32[]{:S(2)}) collective-permute-start(bf16[3,512,128]{2,1,0:T(8,128)(2,1)S(1)} %get-tuple-element.109), channel_id=1, source_target_pairs={{0,2},{1,3},{2,0},{3,1},{4,6},{5,7},{6,4},{7,5},{8,10},{9,11},{10,... | collective-permute-start | bytes 1179656 | tf_op jit(solution)/shard_map/ppermute | solution.py:40
  120.8 19.4 %collective-permute-start.15 = (bf16[3,512,128]{2,1,0:T(8,128)(2,1)S(1)}, bf16[3,512,128]{2,1,0:T(8,128)(2,1)S(1)}, u32[]{:S(2)}, u32[]{:S(2)}) collective-permute-start(bf16[3,512,128]{2,1,0:T(8,128)(2,1)S(1)} %get-tuple-element.110), channel_id=1, source_target_pairs={{0,3},{1,0},{2,1},{3,2},{4,7},{5,4},{6,5},{7,6},{8,11},{9,8},{10,9... | collective-permute-start | bytes 1179656 | tf_op jit(solution)/shard_map/ppermute | solution.py:40
  122.5 33.9 %collective-permute-start.19 = (bf16[128,1024]{1,0:T(8,128)(2,1)S(1)}, bf16[128,1024]{1,0:T(8,128)(2,1)S(1)}, u32[]{:S(2)}, u32[]{:S(2)}) collective-permute-start(bf16[128,1024]{1,0:T(8,128)(2,1)S(1)} %get-tuple-element.117), channel_id=1, source_target_pairs={{0,4},{1,5},{2,6},{3,7},{4,0},{5,1},{6,2},{7,3},{8,12},{9,13},{10,... | collective-permute-start | bytes 786440 | tf_op jit(solution)/shard_map/ppermute | solution.py:40
  166.7 12.0 %collective-permute-start.22 = (bf16[256,1024]{1,0:T(8,128)(2,1)S(1)}, bf16[256,1024]{1,0:T(8,128)(2,1)S(1)}, u32[]{:S(2)}, u32[]{:S(2)}) collective-permute-start(bf16[256,1024]{1,0:T(8,128)(2,1)S(1)} %bitcast.88), channel_id=1, source_target_pairs={{0,32},{32,0},{1,33},{33,1},{2,34},{34,2},{3,35},{35,3},{4,36},{36... | collective-permute-start | bytes 1572872 | tf_op jit(solution)/shard_map/ppermute | solution.py:44
  192.0 9.6 %collective-permute-start.24 = (bf16[512,128]{1,0:T(8,128)(2,1)S(1)}, bf16[512,128]{1,0:T(8,128)(2,1)S(1)}, u32[]{:S(2)}, u32[]{:S(2)}) collective-permute-start(bf16[512,128]{1,0:T(8,128)(2,1)S(1)} %get-tuple-element.128), channel_id=1, source_target_pairs={{0,1},{1,2},{2,3},{3,0},{4,5},{5,6},{6,7},{7,4},{8,9},{9,10},{10,1... | collective-permute-start | bytes 393224 | tf_op jit(solution)/shard_map/ppermute | solution.py:40
  192.0 9.6 %collective-permute-start.25 = (bf16[512,128]{1,0:T(8,128)(2,1)S(1)}, bf16[512,128]{1,0:T(8,128)(2,1)S(1)}, u32[]{:S(2)}, u32[]{:S(2)}) collective-permute-start(bf16[512,128]{1,0:T(8,128)(2,1)S(1)} %get-tuple-element.129), channel_id=1, source_target_pairs={{0,2},{1,3},{2,0},{3,1},{4,6},{5,7},{6,4},{7,5},{8,10},{9,11},{10,... | collective-permute-start | bytes 393224 | tf_op jit(solution)/shard_map/ppermute | solution.py:40
  195.3 27.0 %collective-permute-start.21 = (bf16[256,1024]{1,0:T(8,128)(2,1)S(1)}, bf16[256,1024]{1,0:T(8,128)(2,1)S(1)}, u32[]{:S(2)}, u32[]{:S(2)}) collective-permute-start(bf16[256,1024]{1,0:T(8,128)(2,1)S(1)} %get-tuple-element.121), channel_id=1, source_target_pairs={{0,32},{32,0},{1,33},{33,1},{2,34},{34,2},{3,35},{35,3},{4,36},{36... | collective-permute-start | bytes 1572872 | tf_op jit(solution)/shard_map/ppermute | solution.py:44
  226.2 18.3 %collective-permute-start.31 = (bf16[4,512,128]{2,1,0:T(8,128)(2,1)S(1)}, bf16[4,512,128]{2,1,0:T(8,128)(2,1)S(1)}, u32[]{:S(2)}, u32[]{:S(2)}) collective-permute-start(bf16[4,512,128]{2,1,0:T(8,128)(2,1)S(1)} %get-tuple-element.133), channel_id=1, source_target_pairs={{64,0},{65,1},{66,2},{67,3},{68,4},{69,5},{70,6},{71,7},{72,8},{73... | collective-permute-start | bytes 1572872 | tf_op jit(solution)/shard_map/ppermute | solution.py:855
  227.5 18.8 %collective-permute-start.28 = (bf16[3,512,128]{2,1,0:T(8,128)(2,1)S(1)}, bf16[3,512,128]{2,1,0:T(8,128)(2,1)S(1)}, u32[]{:S(2)}, u32[]{:S(2)}) collective-permute-start(bf16[3,512,128]{2,1,0:T(8,128)(2,1)S(1)} %get-tuple-element.136), channel_id=1, source_target_pairs={{0,3},{1,0},{2,1},{3,2},{4,7},{5,4},{6,5},{7,6},{8,11},{9,8},{10,9... | collective-permute-start | bytes 1179656 | tf_op jit(solution)/shard_map/ppermute | solution.py:40
  229.9 16.4 %collective-permute-start.29 = (bf16[3,512,128]{2,1,0:T(8,128)(2,1)S(1)}, bf16[3,512,128]{2,1,0:T(8,128)(2,1)S(1)}, u32[]{:S(2)}, u32[]{:S(2)}) collective-permute-start(bf16[3,512,128]{2,1,0:T(8,128)(2,1)S(1)} %get-tuple-element.137), channel_id=1, source_target_pairs={{0,2},{1,3},{2,0},{3,1},{4,6},{5,7},{6,4},{7,5},{8,10},{9,11},{10,... | collective-permute-start | bytes 1179656 | tf_op jit(solution)/shard_map/ppermute | solution.py:40
  229.9 19.8 %collective-permute-start.30 = (bf16[3,512,128]{2,1,0:T(8,128)(2,1)S(1)}, bf16[3,512,128]{2,1,0:T(8,128)(2,1)S(1)}, u32[]{:S(2)}, u32[]{:S(2)}) collective-permute-start(bf16[3,512,128]{2,1,0:T(8,128)(2,1)S(1)} %get-tuple-element.138), channel_id=1, source_target_pairs={{0,1},{1,2},{2,3},{3,0},{4,5},{5,6},{6,7},{7,4},{8,9},{9,10},{10,1... | collective-permute-start | bytes 1179656 | tf_op jit(solution)/shard_map/ppermute | solution.py:40
  257.3 149.4 %reduce-scatter.2.cloned.1.call-start = ((), (), s32[]{:S(2)}) async-start(), calls=%async_computation.3 | async-start | bytes 7208960 | tf_op jit(solution)/shard_map/reduce_scatter | solution.py:924
  257.4 16.2 %collective-permute-start.33 = (bf16[256,1024]{1,0:T(8,128)(2,1)}, bf16[256,1024]{1,0:T(8,128)(2,1)S(1)}, u32[]{:S(2)}, u32[]{:S(2)}) collective-permute-start(bf16[256,1024]{1,0:T(8,128)(2,1)} %copy-done.70), channel_id=1, source_target_pairs={{64,0},{65,1},{66,2},{67,3},{68,4},{69,5},{70,6},{71,7},{72,8},{73... | collective-permute-start | bytes 1572872 | tf_op jit(solution)/shard_map/ppermute | solution.py:855
  305.5 14.3 %collective-permute-start.39 = (bf16[4,256,1024]{2,1,0:T(8,128)(2,1)}, bf16[4,256,1024]{2,1,0:T(8,128)(2,1)S(1)}, u32[]{:S(2)}, u32[]{:S(2)}) collective-permute-start(bf16[4,256,1024]{2,1,0:T(8,128)(2,1)} %bitcast.92), channel_id=1, source_target_pairs={{0,32},{32,0},{1,33},{33,1},{2,34},{34,2},{3,35},{35,3},{4,36},{36... | collective-permute-start | bytes 6291464 | tf_op jit(solution)/shard_map/ppermute | solution.py:44
  314.7 65.5 %collective-permute-start.45 = (bf16[16,64,1024]{2,1,0:T(8,128)(2,1)S(1)}, bf16[16,64,1024]{2,1,0:T(8,128)(2,1)S(1)}, u32[]{:S(2)}, u32[]{:S(2)}) collective-permute-start(bf16[16,64,1024]{2,1,0:T(8,128)(2,1)S(1)} %get-tuple-element.167), channel_id=1, source_target_pairs={{0,4},{1,5},{2,6},{3,7},{4,0},{5,1},{6,2},{7,3},{8,12},{9,13},{10,... | collective-permute-start | bytes 6291464 | tf_op jit(solution)/shard_map/ppermute | solution.py:40
  316.5 9.8 %collective-permute-start.36 = (bf16[512,128]{1,0:T(8,128)(2,1)}, bf16[512,128]{1,0:T(8,128)(2,1)S(1)}, u32[]{:S(2)}, u32[]{:S(2)}) collective-permute-start(bf16[512,128]{1,0:T(8,128)(2,1)} %copy-done.73), channel_id=1, source_target_pairs={{0,1},{1,2},{2,3},{3,0},{4,5},{5,6},{6,7},{7,4},{8,9},{9,10},{10,1... | collective-permute-start | bytes 393224 | tf_op jit(solution)/shard_map/ppermute | solution.py:40
  316.6 9.7 %collective-permute-start.37 = (bf16[512,128]{1,0:T(8,128)(2,1)}, bf16[512,128]{1,0:T(8,128)(2,1)S(1)}, u32[]{:S(2)}, u32[]{:S(2)}) collective-permute-start(bf16[512,128]{1,0:T(8,128)(2,1)} %copy-done.72), channel_id=1, source_target_pairs={{0,2},{1,3},{2,0},{3,1},{4,6},{5,7},{6,4},{7,5},{8,10},{9,11},{10,... | collective-permute-start | bytes 393224 | tf_op jit(solution)/shard_map/ppermute | solution.py:40
  350.8 29.4 %collective-permute-start.46 = (bf16[16,16,1024]{2,1,0:T(8,128)(2,1)S(1)}, bf16[16,16,1024]{2,1,0:T(8,128)(2,1)S(1)}, u32[]{:S(2)}, u32[]{:S(2)}) collective-permute-start(bf16[16,16,1024]{2,1,0:T(8,128)(2,1)S(1)} %get-tuple-element.168), channel_id=1, source_target_pairs={{0,4},{1,5},{2,6},{3,7},{4,0},{5,1},{6,2},{7,3},{8,12},{9,13},{10,... | collective-permute-start | bytes 1572872 | tf_op jit(solution)/shard_map/ppermute | solution.py:40
  353.7 18.9 %collective-permute-start.40 = (bf16[3,512,128]{2,1,0:T(8,128)(2,1)S(1)}, bf16[3,512,128]{2,1,0:T(8,128)(2,1)S(1)}, u32[]{:S(2)}, u32[]{:S(2)}) collective-permute-start(bf16[3,512,128]{2,1,0:T(8,128)(2,1)S(1)} %get-tuple-element.159.refs_7_), channel_id=1, source_target_pairs={{0,3},{1,0},{2,1},{3,2},{4,7},{5,4},{6,5},{7,6},{8,11},{9,8},{10,9... | collective-permute-start | bytes 1179656 | tf_op jit(solution)/shard_map/ppermute | solution.py:40
  356.1 16.5 %collective-permute-start.41 = (bf16[3,512,128]{2,1,0:T(8,128)(2,1)S(1)}, bf16[3,512,128]{2,1,0:T(8,128)(2,1)S(1)}, u32[]{:S(2)}, u32[]{:S(2)}) collective-permute-start(bf16[3,512,128]{2,1,0:T(8,128)(2,1)S(1)} %get-tuple-element.160.refs_8_), channel_id=1, source_target_pairs={{0,2},{1,3},{2,0},{3,1},{4,6},{5,7},{6,4},{7,5},{8,10},{9,11},{10,... | collective-permute-start | bytes 1179656 | tf_op jit(solution)/shard_map/ppermute | solution.py:40
  356.1 20.1 %collective-permute-start.42 = (bf16[3,512,128]{2,1,0:T(8,128)(2,1)S(1)}, bf16[3,512,128]{2,1,0:T(8,128)(2,1)S(1)}, u32[]{:S(2)}, u32[]{:S(2)}) collective-permute-start(bf16[3,512,128]{2,1,0:T(8,128)(2,1)S(1)} %get-tuple-element.161.refs_9_), channel_id=1, source_target_pairs={{0,1},{1,2},{2,3},{3,0},{4,5},{5,6},{6,7},{7,4},{8,9},{9,10},{10,1... | collective-permute-start | bytes 1179656 | tf_op jit(solution)/shard_map/ppermute | solution.py:40
  382.6 44.5 %all-to-all-start = ((bf16[16,80,1024]{2,1,0:T(8,128)(2,1)}), bf16[16,80,1024]{2,1,0:T(8,128)(2,1)S(1)}, u32[]{:S(2)}, u32[]{:S(2)}) async-start(bf16[16,80,1024]{2,1,0:T(8,128)(2,1)} %rest_sum.1), calls=%async_computation | async-start | bytes 5242880 | tf_op jit(solution)/shard_map/all_to_all | solution.py:825
  395.5 9.9 %collective-permute-start.44 = (bf16[128,1024]{1,0:T(8,128)(2,1)S(1)}, bf16[128,1024]{1,0:T(8,128)(2,1)S(1)}, u32[]{:S(2)}, u32[]{:S(2)}) collective-permute-start(bf16[128,1024]{1,0:T(8,128)(2,1)S(1)} %fusion.1), channel_id=1, source_target_pairs={{0,4},{1,5},{2,6},{3,7},{4,0},{5,1},{6,2},{7,3},{8,12},{9,13},{10,... | collective-permute-start | bytes 786440 | tf_op jit(solution)/shard_map/ppermute | solution.py:40
  427.1 24.9 %all-to-all-start.1 = ((bf16[8,64,1408]{2,1,0:T(8,128)(2,1)}), bf16[8,64,1408]{2,1,0:T(8,128)(2,1)}, u32[]{:S(2)}, u32[]{:S(2)}) async-start(bf16[8,64,1408]{2,1,0:T(8,128)(2,1)} %copy-done.7), calls=%async_computation.2 | async-start | bytes 2883584 | tf_op jit(solution)/shard_map/all_to_all | solution.py:825
  (100 other events, 1421.8 us)
Sparse Core Ops, SparseCore 0:
  257.4 29.4 all-gather.2
Sparse Core Ops, SparseCore 1:
  305.5 56.5 reduce-scatter.1

commit v4 on v3

--- a/solution.py
+++ b/solution.py
@@ -15,9 +15,7 @@
 BRIEF = 0.001
 NEGATIVE = -1e30
 KEYS = 512
-QUERIES = 1024
 BACK_KEYS = 256
-BACK_QUERIES = 512
 BF = jnp.bfloat16
 F32 = jnp.float32
 
@@ -642,7 +640,7 @@
 
 
 def attend_kernel(x_ref, ends_ref, m0, m1, m2, m3, o0, o1, o2, o3, lse_ref, out_t, keys, query_t,
-                  value_t, acc):
+                  value_t, totals):
     x = x_ref[0]
     lanes = lax.broadcasted_iota(jnp.int32, (BLOCK, PAIR), 1)
     for shift, message in enumerate((m0, m1, m2, m3)):
@@ -656,49 +654,32 @@
             query_t[:, at] = message[0, inside, :].T
             value_t[:, at] = message[2, inside, :].T
 
-    def one_query_block(qi, _):
-        q_at = pl.ds(pl.multiple_of(qi * QUERIES, QUERIES), QUERIES)
-        places = qi * QUERIES + lax.broadcasted_iota(jnp.int32, (1, QUERIES), 1)
-        start = first_visible(ends_ref, places)
-        acc[...] = jnp.zeros_like(acc)
-
-        def one_key_block(kj, carry, diagonal):
-            k_at = pl.ds(pl.multiple_of(kj * KEYS, KEYS), KEYS)
-            key_places = kj * KEYS + lax.broadcasted_iota(jnp.int32, (KEYS, QUERIES), 0)
-            visible = key_places >= start
-            if diagonal:
-                visible = visible & (key_places <= places)
-            after = []
-            for head in range(2):
-                highest, total = carry[head]
-                scores = jnp.dot(keys[head, k_at, :], query_t[:, q_at], preferred_element_type=F32)
-                scores = jnp.where(visible, scores, NEGATIVE)
-                higher = jnp.maximum(highest, jnp.max(scores, axis=0, keepdims=True))
-                shrink = jnp.exp(highest - higher)
-                weight = jnp.exp(scores - higher)
-                total = total * shrink + jnp.sum(weight, axis=0, keepdims=True)
-                part = slice(head * HD, (head + 1) * HD)
-                acc[part, :] = acc[part, :] * shrink + jnp.dot(
-                    value_t[part, k_at], weight.astype(BF), preferred_element_type=F32
-                )
-                after.append((higher, total))
-            return tuple(after)
-
-        begin = (jnp.full((1, QUERIES), NEGATIVE, F32), jnp.zeros((1, QUERIES), F32))
-        ratio = QUERIES // KEYS
-        done = lax.fori_loop(
-            0, qi * ratio, lambda kj, carry: one_key_block(kj, carry, False), (begin, begin)
-        )
-        for step in range(ratio):
-            done = one_key_block(qi * ratio + step, done, True)
+    places = lax.broadcasted_iota(jnp.int32, (1, LEN), 1)
+    start = first_visible(ends_ref, places)
+    out_t[...] = jnp.zeros_like(out_t)
+    lse_ref[...] = jnp.full_like(lse_ref, NEGATIVE)
+    totals[...] = jnp.zeros_like(totals)
+    for low in range(0, LEN, KEYS):
+        k_at, q_at = slice(low, low + KEYS), slice(low, LEN)
+        key_places = low + lax.broadcasted_iota(jnp.int32, (KEYS, LEN - low), 0)
+        visible = (key_places >= start[:, q_at]) & (key_places <= places[:, q_at])
         for head in range(2):
-            highest, total = done[head]
-            part = slice(head * HD, (head + 1) * HD)
-            out_t[part, q_at] = acc[part, :] / total
-            lse_ref[head : head + 1, q_at] = highest + jnp.log(total)
-        return 0
-
-    lax.fori_loop(0, LEN // QUERIES, one_query_block, 0)
+            row, part = slice(head, head + 1), slice(head * HD, (head + 1) * HD)
+            scores = jnp.dot(keys[head, k_at, :], query_t[:, q_at], preferred_element_type=F32)
+            scores = jnp.where(visible, scores, NEGATIVE)
+            highest = lse_ref[row, q_at]
+            higher = jnp.maximum(highest, jnp.max(scores, axis=0, keepdims=True))
+            shrink = jnp.exp(highest - higher)
+            weight = jnp.exp(scores - higher)
+            lse_ref[row, q_at] = higher
+            totals[row, q_at] = totals[row, q_at] * shrink + jnp.sum(weight, axis=0, keepdims=True)
+            out_t[part, q_at] = out_t[part, q_at] * shrink + jnp.dot(
+                value_t[part, k_at], weight.astype(BF), preferred_element_type=F32
+            )
+    for head in range(2):
+        row, part = slice(head, head + 1), slice(head * HD, (head + 1) * HD)
+        out_t[part, :] = out_t[part, :] / totals[row, :]
+        lse_ref[row, :] = lse_ref[row, :] + jnp.log(totals[row, :])
     for shift, out in enumerate((o0, o1, o2, o3)):
         source = lax.rem(x + RING - shift, RING)
         for part in range(4):
@@ -716,9 +697,9 @@
             pltpu.VMEM((2, LEN, PAIR), BF),
             pltpu.VMEM((PAIR, LEN), BF),
             pltpu.VMEM((PAIR, LEN), BF),
-            pltpu.VMEM((PAIR, QUERIES), F32),
+            pltpu.VMEM((2, LEN), F32),
         ],
-        smem=2, waits=waits, limit=12, us=13, name="attend",
+        smem=2, waits=waits, limit=12, us=11, name="attend",
     )
 
 
@@ -745,38 +726,25 @@
             product = out_t[:, at] * turned_grad.astype(F32)
             delta[0:1, at] = jnp.sum(product[:HD], axis=0, keepdims=True)
             delta[1:2, at] = jnp.sum(product[HD:], axis=0, keepdims=True)
-    grad_k[...] = jnp.zeros_like(grad_k)
-    grad_v[...] = jnp.zeros_like(grad_v)
     grad_q_t[...] = jnp.zeros_like(grad_q_t)
-
-    def one_query_block(qi, _):
-        q_at = pl.ds(pl.multiple_of(qi * BACK_QUERIES, BACK_QUERIES), BACK_QUERIES)
-        places = qi * BACK_QUERIES + lax.broadcasted_iota(jnp.int32, (1, BACK_QUERIES), 1)
-        start = first_visible(ends_ref, places)
-
-        def one_key_block(kj, carry):
-            k_at = pl.ds(pl.multiple_of(kj * BACK_KEYS, BACK_KEYS), BACK_KEYS)
-            key_places = kj * BACK_KEYS + lax.broadcasted_iota(jnp.int32, (BACK_KEYS, BACK_QUERIES), 0)
-            visible = (key_places <= places) & (key_places >= start)
-            for head in range(2):
-                part = slice(head * HD, (head + 1) * HD)
-                scores = jnp.dot(keys[head, k_at, :], query_t[:, q_at], preferred_element_type=F32)
-                scores = jnp.where(visible, scores, NEGATIVE)
-                weight = jnp.exp(scores - lse_ref[head : head + 1, q_at])
-                grad_w = jnp.dot(values[head, k_at, :], grad_t[:, q_at], preferred_element_type=F32)
-                grad_s = (weight * (grad_w - delta[head : head + 1, q_at])).astype(BF)
-                grad_v[k_at, :] += jnp.dot(
-                    weight.astype(BF), grads[head, q_at, :], preferred_element_type=F32
-                )
-                grad_k[k_at, :] += jnp.dot(grad_s, queries[head, q_at, :], preferred_element_type=F32)
-                grad_q_t[part, q_at] += jnp.dot(
-                    key_t[part, k_at], grad_s, preferred_element_type=F32
-                )
-            return carry
-
-        return lax.fori_loop(0, (qi + 1) * (BACK_QUERIES // BACK_KEYS), one_key_block, 0)
-
-    lax.fori_loop(0, LEN // BACK_QUERIES, one_query_block, 0)
+    places = lax.broadcasted_iota(jnp.int32, (1, LEN), 1)
+    start = first_visible(ends_ref, places)
+    for low in range(0, LEN, BACK_KEYS):
+        k_at, q_at = slice(low, low + BACK_KEYS), slice(low, LEN)
+        key_places = low + lax.broadcasted_iota(jnp.int32, (BACK_KEYS, LEN - low), 0)
+        visible = (key_places >= start[:, q_at]) & (key_places <= places[:, q_at])
+        sum_k = sum_v = jnp.zeros((BACK_KEYS, PAIR), F32)
+        for head in range(2):
+            row, part = slice(head, head + 1), slice(head * HD, (head + 1) * HD)
+            scores = jnp.dot(keys[head, k_at, :], query_t[:, q_at], preferred_element_type=F32)
+            weight = jnp.exp(jnp.where(visible, scores, NEGATIVE) - lse_ref[row, q_at])
+            grad_w = jnp.dot(values[head, k_at, :], grad_t[:, q_at], preferred_element_type=F32)
+            grad_s = (weight * (grad_w - delta[row, q_at])).astype(BF)
+            sum_v += jnp.dot(weight.astype(BF), grads[head, q_at, :], preferred_element_type=F32)
+            sum_k += jnp.dot(grad_s, queries[head, q_at, :], preferred_element_type=F32)
+            grad_q_t[part, q_at] += jnp.dot(key_t[part, k_at], grad_s, preferred_element_type=F32)
+        grad_k[k_at, :] = sum_k
+        grad_v[k_at, :] = sum_v
     for shift, out in enumerate((g0, g1, g2, g3)):
         source = lax.rem(x + RING - shift, RING)
         for part in range(4):
@@ -791,7 +759,7 @@
             dv_ref[shift, inside, :] = grad_value.astype(BF)
 
 
-def attend_back(x_index, ends, mix, messages, arrived, lse, out_t, dv1, cosine, sine, waits=(), us=20):
+def attend_back(x_index, ends, mix, messages, arrived, lse, out_t, dv1, cosine, sine, waits=(), us=18):
     rows = messages[0].shape[1]
     return on_core(
         attend_back_kernel,
@@ -805,7 +773,7 @@
             pltpu.VMEM((LEN, PAIR), F32),
             pltpu.VMEM((PAIR, LEN), F32),
         ],
-        smem=3, waits=waits, limit=13, us=us, name="attend_back",
+        smem=3, waits=waits, limit=17, us=us, name="attend_back",
     )
 
 

time: 468 us -> 455 us (0.972)
  Pallas kernels: 135 us -> 122 us
    pallas_call x25, Pallas kernels: 133 us -> 119 us  [on_core(): pl.pallas_call(body, in_specs=spots, out_specs=[pl.BlockSpec(memory_space...]
  transfers between devices with their start and end apart: 52 -> 52, of which waited for: 36 -> 36; matrix products, arithmetic and copies ran while one was open for 2% -> 2% of each run, Pallas kernels for 21% -> 19%
where the time goes in v4:
time: 455 us; the launch traced here: 449 us
  waiting for transfers between devices  189 us (42%)
  Pallas kernels  122 us (27%)
  starting transfers between devices  70.3 us (15%)
  local copies, waits for them, and re-layouts  45.9 us (10%)
  between operations  16.7 us (4%)
  other arithmetic  5.65 us (1%)
    pallas_call x25, Pallas kernels, on_core(): pl.pallas_call(body, in_specs=spots, out_specs=[pl.BlockSpec(memory_space...  119 us
    ppermute x30, waiting for transfers between devices, moved(): return lax.ppermute(value, 'dp', along(kind, shift))  95.9 us
    ppermute x30, starting transfers between devices, moved(): return lax.ppermute(value, 'dp', along(kind, shift))  48 us
    ppermute x4, waiting for transfers between devices, handed(): return lax.ppermute(value, 'section', pairs)  42 us
    unnamed x162, local copies, waits for them, and re-layouts  41.9 us
    all_to_all x2, waiting for transfers between devices, all_to_all(): return lax.all_to_all(value, 'dp', 0, 0, axis_index_groups=groups(kinds))  35 us
    ppermute x14, waiting for transfers between devices, swapped(): return lax.ppermute(value, 'tensor', [(0, 1), (1, 0)])  16 us
    ppermute x4, starting transfers between devices, handed(): return lax.ppermute(value, 'section', pairs)  10.6 us
  transfers between devices with their start and end apart: 52, of which 36 were waited for; matrix products, arithmetic and copies ran while one was open for 2% of the time, Pallas kernels for 19%

profile of v4, /device:TPU:0, one launch (start us, length us, event | category | flops | bytes accessed | tf_op | source)
XLA Modules:
  0.0 449.4 jit_solution(8157388818937096509)
XLA Ops:
  9.2 4.0 collective-permute-start
  13.2 6.3 %collective-permute-done = bf16[128,1024]{1,0:T(8,128)(2,1)S(1)} collective-permute-done((bf16[128,1024]{1,0:T(8,128)(2,1)S(1)}, bf16[128,1024]{1,0:T(8,128)(2,1)S(1)}, u32[]{:S(2)}, u32[]{:S(2)}) %collective-permute-start) | collective-permute-done | bytes 262176 | tf_op jit(solution)/shard_map/ppermute | solution.py:38
  28.9 3.9 project.2
  41.3 4.4 collective-permute-done.2.refs_3_
  45.7 9.4 %collective-permute-done.3.refs_4_ = bf16[3,512,128]{2,1,0:T(8,128)(2,1)S(1)} collective-permute-done((bf16[3,512,128]{2,1,0:T(8,128)(2,1)S(1)}, bf16[3,512,128]{2,1,0:T(8,128)(2,1)S(1)}, u32[]{:S(2)}, u32[]{:S(2)}) %collective-permute-start.3) | collective-permute-done | bytes 393248 | tf_op jit(solution)/shard_map/ppermute | solution.py:38
  55.1 11.3 %attend.2 = (bf16[512,128]{1,0:T(8,128)(2,1)S(1)}, bf16[512,128]{1,0:T(8,128)(2,1)S(1)}, bf16[512,128]{1,0:T(8,128)(2,1)S(1)}, bf16[512,128]{1,0:T(8,128)(2,1)S(...) custom-call(s32[1]{0:T(128)} %bitcast.1.refs_0_, s32[4]{0:T(128)S(1)} %bitcast.103, ...), custom_call_target="tpu_custom_call" | custom-call | flops 12099999744 | bytes 39600000 | tf_op jit(solution)/shard_map/attend/pallas_call | solution.py:85
  70.6 3.8 collective-permute-done.5.refs_2_
  82.6 7.9 %feed.2 = (f32[256,1024]{1,0:T(8,128)S(1)}, bf16[256,1024]{1,0:T(8,128)(2,1)S(1)}, bf16[256,1024]{1,0:T(8,128)(2,1)S(1)}, bf16[512,1024]{1,0:T(8,128)(2,1)}) custom-call(s32[1]{0:T(128)} %bitcast.refs_1_.refs_0_, bf16[512,1024]{1,0:T(8,128)(2,1)S(1)} %get-tuple-element.90.refs_1_, bf16[512,1024]{1,0:T(8,128)(2,1)S(1)} %get-tuple-element.101.refs_2_, ...), custom_call_target="tpu_custom_call" | custom-call | flops 7699999744 | bytes 25200000 | tf_op jit(solution)/shard_map/feed/pallas_call | solution.py:85
  94.5 4.7 %collective-permute-start.11 = (bf16[256,1024]{1,0:T(8,128)(2,1)S(1)}, bf16[256,1024]{1,0:T(8,128)(2,1)S(1)}, u32[]{:S(2)}, u32[]{:S(2)}) collective-permute-start(bf16[256,1024]{1,0:T(8,128)(2,1)S(1)} %close.2), channel_id=1, source_target_pairs={{0,64},{1,65},{2,66},{3,67},{4,68},{5,69},{6,70},{7,71},{8,72},{9,... | collective-permute-start | bytes 1572872 | tf_op jit(solution)/shard_map/ppermute | solution.py:823
  99.2 11.0 %collective-permute-done.11 = bf16[256,1024]{1,0:T(8,128)(2,1)S(1)} collective-permute-done((bf16[256,1024]{1,0:T(8,128)(2,1)S(1)}, bf16[256,1024]{1,0:T(8,128)(2,1)S(1)}, u32[]{:S(2)}, u32[]{:S(2)}) %collective-permute-start.11) | collective-permute-done | bytes 524320 | tf_op jit(solution)/shard_map/ppermute | solution.py:823
  112.3 4.1 project.3
  120.6 4.1 collective-permute-start.19
  124.6 12.7 %collective-permute-done.13.refs_3_.refs_4_ = bf16[3,512,128]{2,1,0:T(8,128)(2,1)S(1)} collective-permute-done((bf16[3,512,128]{2,1,0:T(8,128)(2,1)S(1)}, bf16[3,512,128]{2,1,0:T(8,128)(2,1)S(1)}, u32[]{:S(2)}, u32[]{:S(2)}) %collective-permute-start.13) | collective-permute-done | bytes 393248 | tf_op jit(solution)/shard_map/ppermute | solution.py:38
  138.0 10.4 %attend.3 = (bf16[512,128]{1,0:T(8,128)(2,1)S(1)}, bf16[512,128]{1,0:T(8,128)(2,1)S(1)}, bf16[512,128]{1,0:T(8,128)(2,1)S(1)}, bf16[512,128]{1,0:T(8,128)(2,1)S(...) custom-call(s32[1]{0:T(128)} %bitcast.1.refs_0_, s32[4]{0:T(128)S(1)} %bitcast.104, ...), custom_call_target="tpu_custom_call" | custom-call | flops 12099999744 | bytes 39600000 | tf_op jit(solution)/shard_map/attend/pallas_call | solution.py:85
  152.1 4.7 %collective-permute-done.16.refs_2_ = bf16[512,128]{1,0:T(8,128)(2,1)S(1)} collective-permute-done((bf16[512,128]{1,0:T(8,128)(2,1)S(1)}, bf16[512,128]{1,0:T(8,128)(2,1)S(1)}, u32[]{:S(2)}, u32[]{:S(2)}) %collective-permute-start.16) | collective-permute-done | bytes 131104 | tf_op jit(solution)/shard_map/ppermute | solution.py:38
  165.2 7.0 %feed.3 = (f32[256,1024]{1,0:T(8,128)S(1)}, bf16[256,1024]{1,0:T(8,128)(2,1)S(1)}, bf16[256,1024]{1,0:T(8,128)(2,1)S(1)}, bf16[512,1024]{1,0:T(8,128)(2,1)S(1)},...) custom-call(s32[1]{0:T(128)} %bitcast.refs_1_.refs_0_, ...), custom_call_target="tpu_custom_call" | custom-call | flops 7699999744 | bytes 25200000 | tf_op jit(solution)/shard_map/feed/pallas_call | solution.py:85
  174.4 7.2 %feed_back.2 = (bf16[512,1408]{1,0:T(8,128)(2,1)}, bf16[512,1408]{1,0:T(8,128)(2,1)}, bf16[512,1024]{1,0:T(8,128)(2,1)S(1)}, bf16[512,1024]{1,0:T(8,128)(2,1)S(1)}) custom-call(s32[1]{0:T(128)} %bitcast.refs_1_.refs_0_, bf16[256,1024]{1,0:T(8,128)(2,1)S(1)} %bitcast.89, bf16[256,1024]{1,0:T(8,128)(2,1)S(1)} %collective-permute-done.22.refs_2_, ...), custom_call_target="tpu_custom_call" | custom-call | flops 7699999744 | bytes 25200000 | tf_op jit(solution)/shard_map/feed_back/pallas_call | solution.py:85
  190.7 6.0 %collective-permute-done.24.refs_8_ = bf16[512,128]{1,0:T(8,128)(2,1)S(1)} collective-permute-done((bf16[512,128]{1,0:T(8,128)(2,1)S(1)}, bf16[512,128]{1,0:T(8,128)(2,1)S(1)}, u32[]{:S(2)}, u32[]{:S(2)}) %collective-permute-start.24) | collective-permute-done | bytes 131104 | tf_op jit(solution)/shard_map/ppermute | solution.py:38
  197.4 16.4 %attend_back.2 = (bf16[3,512,128]{2,1,0:T(8,128)(2,1)S(1)}, bf16[3,512,128]{2,1,0:T(8,128)(2,1)S(1)}, bf16[3,512,128]{2,1,0:T(8,128)(2,1)S(1)}, bf16[3,512,128]{2,1,0:T(8,128)(2,1)S(1)}, bf16[4,512,128]{2,1,0:T(8,128)(2,1)S(1)}) custom-call(s32[1]{0:T(128)} %bitcast.1.refs_0_, s32[4]{0:T(128)S(1)} %bitcast.105, f32[2]{0:T(128)S(1)} %broadcast_select_fusion.2.refs_2_, ...), custom_call_target="tpu_custom_call" | custom-call | flops 22000001024 | bytes 72000000 | tf_op jit(solution)/shard_map/attend_back/pallas_call | solution.py:85
  214.1 3.7 collective-permute-start.27
  223.4 12.7 %collective-permute-done.31.refs_13_ = bf16[4,512,128]{2,1,0:T(8,128)(2,1)S(1)} collective-permute-done((bf16[4,512,128]{2,1,0:T(8,128)(2,1)S(1)}, bf16[4,512,128]{2,1,0:T(8,128)(2,1)S(1)}, u32[]{:S(2)}, u32[]{:S(2)}) %collective-permute-start.31) | collective-permute-done | bytes 524320 | tf_op jit(solution)/shard_map/ppermute | solution.py:823
  250.3 14.8 %collective-permute-done.33 = bf16[256,1024]{1,0:T(8,128)(2,1)S(1)} collective-permute-done((bf16[256,1024]{1,0:T(8,128)(2,1)}, bf16[256,1024]{1,0:T(8,128)(2,1)S(1)}, u32[]{:S(2)}, u32[]{:S(2)}) %collective-permute-start.33) | collective-permute-done | bytes 524320 | tf_op jit(solution)/shard_map/ppermute | solution.py:823
  274.3 7.2 %feed_back.3 = (bf16[512,1408]{1,0:T(8,128)(2,1)S(1)}, bf16[512,1408]{1,0:T(8,128)(2,1)S(1)}, bf16[512,1024]{1,0:T(8,128)(2,1)S(1)}, bf16[512,1024]{1,0:T(8,128)(2,1)S(1)}) custom-call(s32[1]{0:T(128)} %bitcast.refs_1_.refs_0_, bf16[256,1024]{1,0:T(8,128)(2,1)S(1)} %broadcast_select_fusion.refs_1_, bf16[256,1024]{1,0:T(8,128)(2,1)S(1)} %collective-permute-done.34.refs_2_, ...), custom_call_target="tpu_custom_call" | custom-call | flops 1100000 | bytes 3600 | tf_op jit(solution)/shard_map/feed_back/pallas_call | solution.py:85
  302.2 3.9 early_terms.1
  311.6 6.0 %collective-permute-done.36.refs_8_ = bf16[512,128]{1,0:T(8,128)(2,1)S(1)} collective-permute-done((bf16[512,128]{1,0:T(8,128)(2,1)}, bf16[512,128]{1,0:T(8,128)(2,1)S(1)}, u32[]{:S(2)}, u32[]{:S(2)}) %collective-permute-start.36) | collective-permute-done | bytes 131104 | tf_op jit(solution)/shard_map/ppermute | solution.py:38
  318.3 16.9 %attend_back.3 = (bf16[3,512,128]{2,1,0:T(8,128)(2,1)S(1)}, bf16[3,512,128]{2,1,0:T(8,128)(2,1)S(1)}, bf16[3,512,128]{2,1,0:T(8,128)(2,1)S(1)}, bf16[3,512,128]{2,1,0:T(8,128)(2,1)S(1)}, bf16[4,512,128]{2,1,0:T(8,128)(2,1)}) custom-call(s32[1]{0:T(128)} %bitcast.1.refs_0_, s32[4]{0:T(128)S(1)} %bitcast.106, f32[2]{0:T(128)S(1)} %copy-done.65, ...), custom_call_target="tpu_custom_call" | custom-call | flops 1100000 | bytes 3600 | tf_op jit(solution)/shard_map/attend_back/pallas_call | solution.py:85
  344.6 15.9 %collective-permute-done.40.refs_3_ = bf16[3,512,128]{2,1,0:T(8,128)(2,1)S(1)} collective-permute-done((bf16[3,512,128]{2,1,0:T(8,128)(2,1)S(1)}, bf16[3,512,128]{2,1,0:T(8,128)(2,1)S(1)}, u32[]{:S(2)}, u32[]{:S(2)}) %collective-permute-start.40) | collective-permute-done | bytes 393248 | tf_op jit(solution)/shard_map/ppermute | solution.py:38
  370.4 4.8 %all-to-all-start = ((bf16[16,80,1024]{2,1,0:T(8,128)(2,1)}), bf16[16,80,1024]{2,1,0:T(8,128)(2,1)S(1)}, u32[]{:S(2)}, u32[]{:S(2)}) async-start(bf16[16,80,1024]{2,1,0:T(8,128)(2,1)} %rest_sum.1), calls=%async_computation | async-start | bytes 5242880 | tf_op jit(solution)/shard_map/all_to_all | solution.py:793
  385.2 8.2 %collective-permute-done.44 = bf16[128,1024]{1,0:T(8,128)(2,1)S(1)} collective-permute-done((bf16[128,1024]{1,0:T(8,128)(2,1)S(1)}, bf16[128,1024]{1,0:T(8,128)(2,1)S(1)}, u32[]{:S(2)}, u32[]{:S(2)}) %collective-permute-start.44) | collective-permute-done | bytes 262176 | tf_op jit(solution)/shard_map/ppermute | solution.py:38
  397.2 17.2 %all-to-all-done.refs_0_ = bf16[16,80,1024]{2,1,0:T(8,128)(2,1)S(1)} async-done(((bf16[16,80,1024]{2,1,0:T(8,128)(2,1)}), bf16[16,80,1024]{2,1,0:T(8,128)(2,1)S(1)}, u32[]{:S(2)}, u32[]{:S(2)}) %all-to-all-start) | async-done | bytes 2621472 | tf_op jit(solution)/shard_map/all_to_all | solution.py:793
  414.4 4.3 all-to-all-start.1
  421.3 17.8 %all-to-all-done.1 = bf16[8,64,1408]{2,1,0:T(8,128)(2,1)} async-done(((bf16[8,64,1408]{2,1,0:T(8,128)(2,1)}), bf16[8,64,1408]{2,1,0:T(8,128)(2,1)}, u32[]{:S(2)}, u32[]{:S(2)}) %all-to-all-start.1) | async-done | bytes 1441824 | tf_op jit(solution)/shard_map/all_to_all | solution.py:793
  (307 shorter events, 160.0 us)
Async XLA Ops:
  8.0 289.0 %all-gather.3.cloned.1.call-start = ((), (), s32[]{:S(2)}) async-start(), calls=%async_computation.4 | async-start | bytes 2621440 | tf_op jit(solution)/shard_map/all_gather | solution.py:886
  9.2 10.3 %collective-permute-start = (bf16[128,1024]{1,0:T(8,128)(2,1)S(1)}, bf16[128,1024]{1,0:T(8,128)(2,1)S(1)}, u32[]{:S(2)}, u32[]{:S(2)}) collective-permute-start(bf16[128,1024]{1,0:T(8,128)(2,1)S(1)} %get-tuple-element.190), channel_id=1, source_target_pairs={{0,4},{1,5},{2,6},{3,7},{4,0},{5,1},{6,2},{7,3},{8,12},{9,13},{10,... | collective-permute-start | bytes 786440 | tf_op jit(solution)/shard_map/ppermute | solution.py:38
  33.3 12.4 %collective-permute-start.2 = (bf16[3,512,128]{2,1,0:T(8,128)(2,1)S(1)}, bf16[3,512,128]{2,1,0:T(8,128)(2,1)S(1)}, u32[]{:S(2)}, u32[]{:S(2)}) collective-permute-start(bf16[3,512,128]{2,1,0:T(8,128)(2,1)S(1)} %get-tuple-element.92), channel_id=1, source_target_pairs={{0,1},{1,2},{2,3},{3,0},{4,5},{5,6},{6,7},{7,4},{8,9},{9,10},{10,1... | collective-permute-start | bytes 1179656 | tf_op jit(solution)/shard_map/ppermute | solution.py:38
  34.8 20.3 %collective-permute-start.3 = (bf16[3,512,128]{2,1,0:T(8,128)(2,1)S(1)}, bf16[3,512,128]{2,1,0:T(8,128)(2,1)S(1)}, u32[]{:S(2)}, u32[]{:S(2)}) collective-permute-start(bf16[3,512,128]{2,1,0:T(8,128)(2,1)S(1)} %get-tuple-element.93), channel_id=1, source_target_pairs={{0,2},{1,3},{2,0},{3,1},{4,6},{5,7},{6,4},{7,5},{8,10},{9,11},{10,... | collective-permute-start | bytes 1179656 | tf_op jit(solution)/shard_map/ppermute | solution.py:38
  37.5 17.6 %collective-permute-start.4 = (bf16[3,512,128]{2,1,0:T(8,128)(2,1)S(1)}, bf16[3,512,128]{2,1,0:T(8,128)(2,1)S(1)}, u32[]{:S(2)}, u32[]{:S(2)}) collective-permute-start(bf16[3,512,128]{2,1,0:T(8,128)(2,1)S(1)} %get-tuple-element.94), channel_id=1, source_target_pairs={{0,3},{1,0},{2,1},{3,2},{4,7},{5,4},{6,5},{7,6},{8,11},{9,8},{10,9... | collective-permute-start | bytes 1179656 | tf_op jit(solution)/shard_map/ppermute | solution.py:38
  79.3 15.0 %collective-permute-start.10 = (bf16[4,512,128]{2,1,0:T(8,128)(2,1)S(1)}, bf16[4,512,128]{2,1,0:T(8,128)(2,1)S(1)}, u32[]{:S(2)}, u32[]{:S(2)}) collective-permute-start(bf16[4,512,128]{2,1,0:T(8,128)(2,1)S(1)} %get-tuple-element.105), channel_id=1, source_target_pairs={{0,64},{1,65},{2,66},{3,67},{4,68},{5,69},{6,70},{7,71},{8,72},{9,... | collective-permute-start | bytes 1572872 | tf_op jit(solution)/shard_map/ppermute | solution.py:823
  94.5 15.7 %collective-permute-start.11 = (bf16[256,1024]{1,0:T(8,128)(2,1)S(1)}, bf16[256,1024]{1,0:T(8,128)(2,1)S(1)}, u32[]{:S(2)}, u32[]{:S(2)}) collective-permute-start(bf16[256,1024]{1,0:T(8,128)(2,1)S(1)} %close.2), channel_id=1, source_target_pairs={{0,64},{1,65},{2,66},{3,67},{4,68},{5,69},{6,70},{7,71},{8,72},{9,... | collective-permute-start | bytes 1572872 | tf_op jit(solution)/shard_map/ppermute | solution.py:823
  116.5 20.8 %collective-permute-start.13 = (bf16[3,512,128]{2,1,0:T(8,128)(2,1)S(1)}, bf16[3,512,128]{2,1,0:T(8,128)(2,1)S(1)}, u32[]{:S(2)}, u32[]{:S(2)}) collective-permute-start(bf16[3,512,128]{2,1,0:T(8,128)(2,1)S(1)} %get-tuple-element.108), channel_id=1, source_target_pairs={{0,1},{1,2},{2,3},{3,0},{4,5},{5,6},{6,7},{7,4},{8,9},{9,10},{10,1... | collective-permute-start | bytes 1179656 | tf_op jit(solution)/shard_map/ppermute | solution.py:38
  116.6 20.8 %collective-permute-start.14 = (bf16[3,512,128]{2,1,0:T(8,128)(2,1)S(1)}, bf16[3,512,128]{2,1,0:T(8,128)(2,1)S(1)}, u32[]{:S(2)}, u32[]{:S(2)}) collective-permute-start(bf16[3,512,128]{2,1,0:T(8,128)(2,1)S(1)} %get-tuple-element.109), channel_id=1, source_target_pairs={{0,2},{1,3},{2,0},{3,1},{4,6},{5,7},{6,4},{7,5},{8,10},{9,11},{10,... | collective-permute-start | bytes 1179656 | tf_op jit(solution)/shard_map/ppermute | solution.py:38
  118.6 19.4 %collective-permute-start.15 = (bf16[3,512,128]{2,1,0:T(8,128)(2,1)S(1)}, bf16[3,512,128]{2,1,0:T(8,128)(2,1)S(1)}, u32[]{:S(2)}, u32[]{:S(2)}) collective-permute-start(bf16[3,512,128]{2,1,0:T(8,128)(2,1)S(1)} %get-tuple-element.110), channel_id=1, source_target_pairs={{0,3},{1,0},{2,1},{3,2},{4,7},{5,4},{6,5},{7,6},{8,11},{9,8},{10,9... | collective-permute-start | bytes 1179656 | tf_op jit(solution)/shard_map/ppermute | solution.py:38
  120.6 31.4 %collective-permute-start.19 = (bf16[128,1024]{1,0:T(8,128)(2,1)S(1)}, bf16[128,1024]{1,0:T(8,128)(2,1)S(1)}, u32[]{:S(2)}, u32[]{:S(2)}) collective-permute-start(bf16[128,1024]{1,0:T(8,128)(2,1)S(1)} %get-tuple-element.117), channel_id=1, source_target_pairs={{0,4},{1,5},{2,6},{3,7},{4,0},{5,1},{6,2},{7,3},{8,12},{9,13},{10,... | collective-permute-start | bytes 786440 | tf_op jit(solution)/shard_map/ppermute | solution.py:38
  162.6 11.8 %collective-permute-start.22 = (bf16[256,1024]{1,0:T(8,128)(2,1)S(1)}, bf16[256,1024]{1,0:T(8,128)(2,1)S(1)}, u32[]{:S(2)}, u32[]{:S(2)}) collective-permute-start(bf16[256,1024]{1,0:T(8,128)(2,1)S(1)} %bitcast.88), channel_id=1, source_target_pairs={{0,32},{32,0},{1,33},{33,1},{2,34},{34,2},{3,35},{35,3},{4,36},{36... | collective-permute-start | bytes 1572872 | tf_op jit(solution)/shard_map/ppermute | solution.py:42
  187.2 9.6 %collective-permute-start.24 = (bf16[512,128]{1,0:T(8,128)(2,1)S(1)}, bf16[512,128]{1,0:T(8,128)(2,1)S(1)}, u32[]{:S(2)}, u32[]{:S(2)}) collective-permute-start(bf16[512,128]{1,0:T(8,128)(2,1)S(1)} %get-tuple-element.128), channel_id=1, source_target_pairs={{0,1},{1,2},{2,3},{3,0},{4,5},{5,6},{6,7},{7,4},{8,9},{9,10},{10,1... | collective-permute-start | bytes 393224 | tf_op jit(solution)/shard_map/ppermute | solution.py:38
  187.2 9.6 %collective-permute-start.25 = (bf16[512,128]{1,0:T(8,128)(2,1)S(1)}, bf16[512,128]{1,0:T(8,128)(2,1)S(1)}, u32[]{:S(2)}, u32[]{:S(2)}) collective-permute-start(bf16[512,128]{1,0:T(8,128)(2,1)S(1)} %get-tuple-element.129), channel_id=1, source_target_pairs={{0,2},{1,3},{2,0},{3,1},{4,6},{5,7},{6,4},{7,5},{8,10},{9,11},{10,... | collective-permute-start | bytes 393224 | tf_op jit(solution)/shard_map/ppermute | solution.py:38
  190.4 23.4 %collective-permute-start.21 = (bf16[256,1024]{1,0:T(8,128)(2,1)S(1)}, bf16[256,1024]{1,0:T(8,128)(2,1)S(1)}, u32[]{:S(2)}, u32[]{:S(2)}) collective-permute-start(bf16[256,1024]{1,0:T(8,128)(2,1)S(1)} %get-tuple-element.121), channel_id=1, source_target_pairs={{0,32},{32,0},{1,33},{33,1},{2,34},{34,2},{3,35},{35,3},{4,36},{36... | collective-permute-start | bytes 1572872 | tf_op jit(solution)/shard_map/ppermute | solution.py:42
  217.8 18.3 %collective-permute-start.31 = (bf16[4,512,128]{2,1,0:T(8,128)(2,1)S(1)}, bf16[4,512,128]{2,1,0:T(8,128)(2,1)S(1)}, u32[]{:S(2)}, u32[]{:S(2)}) collective-permute-start(bf16[4,512,128]{2,1,0:T(8,128)(2,1)S(1)} %get-tuple-element.133), channel_id=1, source_target_pairs={{64,0},{65,1},{66,2},{67,3},{68,4},{69,5},{70,6},{71,7},{72,8},{73... | collective-permute-start | bytes 1572872 | tf_op jit(solution)/shard_map/ppermute | solution.py:823
  219.0 18.8 %collective-permute-start.28 = (bf16[3,512,128]{2,1,0:T(8,128)(2,1)S(1)}, bf16[3,512,128]{2,1,0:T(8,128)(2,1)S(1)}, u32[]{:S(2)}, u32[]{:S(2)}) collective-permute-start(bf16[3,512,128]{2,1,0:T(8,128)(2,1)S(1)} %get-tuple-element.136), channel_id=1, source_target_pairs={{0,3},{1,0},{2,1},{3,2},{4,7},{5,4},{6,5},{7,6},{8,11},{9,8},{10,9... | collective-permute-start | bytes 1179656 | tf_op jit(solution)/shard_map/ppermute | solution.py:38
  221.4 16.4 %collective-permute-start.29 = (bf16[3,512,128]{2,1,0:T(8,128)(2,1)S(1)}, bf16[3,512,128]{2,1,0:T(8,128)(2,1)S(1)}, u32[]{:S(2)}, u32[]{:S(2)}) collective-permute-start(bf16[3,512,128]{2,1,0:T(8,128)(2,1)S(1)} %get-tuple-element.137), channel_id=1, source_target_pairs={{0,2},{1,3},{2,0},{3,1},{4,6},{5,7},{6,4},{7,5},{8,10},{9,11},{10,... | collective-permute-start | bytes 1179656 | tf_op jit(solution)/shard_map/ppermute | solution.py:38
  221.4 19.8 %collective-permute-start.30 = (bf16[3,512,128]{2,1,0:T(8,128)(2,1)S(1)}, bf16[3,512,128]{2,1,0:T(8,128)(2,1)S(1)}, u32[]{:S(2)}, u32[]{:S(2)}) collective-permute-start(bf16[3,512,128]{2,1,0:T(8,128)(2,1)S(1)} %get-tuple-element.138), channel_id=1, source_target_pairs={{0,1},{1,2},{2,3},{3,0},{4,5},{5,6},{6,7},{7,4},{8,9},{9,10},{10,1... | collective-permute-start | bytes 1179656 | tf_op jit(solution)/shard_map/ppermute | solution.py:38
  248.8 145.7 %reduce-scatter.2.cloned.1.call-start = ((), (), s32[]{:S(2)}) async-start(), calls=%async_computation.3 | async-start | bytes 7208960 | tf_op jit(solution)/shard_map/reduce_scatter | solution.py:892
  248.9 16.2 %collective-permute-start.33 = (bf16[256,1024]{1,0:T(8,128)(2,1)}, bf16[256,1024]{1,0:T(8,128)(2,1)S(1)}, u32[]{:S(2)}, u32[]{:S(2)}) collective-permute-start(bf16[256,1024]{1,0:T(8,128)(2,1)} %copy-done.70), channel_id=1, source_target_pairs={{64,0},{65,1},{66,2},{67,3},{68,4},{69,5},{70,6},{71,7},{72,8},{73... | collective-permute-start | bytes 1572872 | tf_op jit(solution)/shard_map/ppermute | solution.py:823
  297.0 14.5 %collective-permute-start.39 = (bf16[4,256,1024]{2,1,0:T(8,128)(2,1)}, bf16[4,256,1024]{2,1,0:T(8,128)(2,1)S(1)}, u32[]{:S(2)}, u32[]{:S(2)}) collective-permute-start(bf16[4,256,1024]{2,1,0:T(8,128)(2,1)} %bitcast.92), channel_id=1, source_target_pairs={{0,32},{32,0},{1,33},{33,1},{2,34},{34,2},{3,35},{35,3},{4,36},{36... | collective-permute-start | bytes 6291464 | tf_op jit(solution)/shard_map/ppermute | solution.py:42
  306.1 61.9 %collective-permute-start.45 = (bf16[16,64,1024]{2,1,0:T(8,128)(2,1)S(1)}, bf16[16,64,1024]{2,1,0:T(8,128)(2,1)S(1)}, u32[]{:S(2)}, u32[]{:S(2)}) collective-permute-start(bf16[16,64,1024]{2,1,0:T(8,128)(2,1)S(1)} %get-tuple-element.167), channel_id=1, source_target_pairs={{0,4},{1,5},{2,6},{3,7},{4,0},{5,1},{6,2},{7,3},{8,12},{9,13},{10,... | collective-permute-start | bytes 6291464 | tf_op jit(solution)/shard_map/ppermute | solution.py:38
  307.8 9.8 %collective-permute-start.36 = (bf16[512,128]{1,0:T(8,128)(2,1)}, bf16[512,128]{1,0:T(8,128)(2,1)S(1)}, u32[]{:S(2)}, u32[]{:S(2)}) collective-permute-start(bf16[512,128]{1,0:T(8,128)(2,1)} %copy-done.73), channel_id=1, source_target_pairs={{0,1},{1,2},{2,3},{3,0},{4,5},{5,6},{6,7},{7,4},{8,9},{9,10},{10,1... | collective-permute-start | bytes 393224 | tf_op jit(solution)/shard_map/ppermute | solution.py:38
  307.9 9.7 %collective-permute-start.37 = (bf16[512,128]{1,0:T(8,128)(2,1)}, bf16[512,128]{1,0:T(8,128)(2,1)S(1)}, u32[]{:S(2)}, u32[]{:S(2)}) collective-permute-start(bf16[512,128]{1,0:T(8,128)(2,1)} %copy-done.72), channel_id=1, source_target_pairs={{0,2},{1,3},{2,0},{3,1},{4,6},{5,7},{6,4},{7,5},{8,10},{9,11},{10,... | collective-permute-start | bytes 393224 | tf_op jit(solution)/shard_map/ppermute | solution.py:38
  338.1 29.9 %collective-permute-start.46 = (bf16[16,16,1024]{2,1,0:T(8,128)(2,1)S(1)}, bf16[16,16,1024]{2,1,0:T(8,128)(2,1)S(1)}, u32[]{:S(2)}, u32[]{:S(2)}) collective-permute-start(bf16[16,16,1024]{2,1,0:T(8,128)(2,1)S(1)} %get-tuple-element.168), channel_id=1, source_target_pairs={{0,4},{1,5},{2,6},{3,7},{4,0},{5,1},{6,2},{7,3},{8,12},{9,13},{10,... | collective-permute-start | bytes 1572872 | tf_op jit(solution)/shard_map/ppermute | solution.py:38
  341.1 19.5 %collective-permute-start.40 = (bf16[3,512,128]{2,1,0:T(8,128)(2,1)S(1)}, bf16[3,512,128]{2,1,0:T(8,128)(2,1)S(1)}, u32[]{:S(2)}, u32[]{:S(2)}) collective-permute-start(bf16[3,512,128]{2,1,0:T(8,128)(2,1)S(1)} %get-tuple-element.159.refs_7_), channel_id=1, source_target_pairs={{0,3},{1,0},{2,1},{3,2},{4,7},{5,4},{6,5},{7,6},{8,11},{9,8},{10,9... | collective-permute-start | bytes 1179656 | tf_op jit(solution)/shard_map/ppermute | solution.py:38
  343.8 16.8 %collective-permute-start.41 = (bf16[3,512,128]{2,1,0:T(8,128)(2,1)S(1)}, bf16[3,512,128]{2,1,0:T(8,128)(2,1)S(1)}, u32[]{:S(2)}, u32[]{:S(2)}) collective-permute-start(bf16[3,512,128]{2,1,0:T(8,128)(2,1)S(1)} %get-tuple-element.160.refs_8_), channel_id=1, source_target_pairs={{0,2},{1,3},{2,0},{3,1},{4,6},{5,7},{6,4},{7,5},{8,10},{9,11},{10,... | collective-permute-start | bytes 1179656 | tf_op jit(solution)/shard_map/ppermute | solution.py:38
  343.8 20.2 %collective-permute-start.42 = (bf16[3,512,128]{2,1,0:T(8,128)(2,1)S(1)}, bf16[3,512,128]{2,1,0:T(8,128)(2,1)S(1)}, u32[]{:S(2)}, u32[]{:S(2)}) collective-permute-start(bf16[3,512,128]{2,1,0:T(8,128)(2,1)S(1)} %get-tuple-element.161.refs_9_), channel_id=1, source_target_pairs={{0,1},{1,2},{2,3},{3,0},{4,5},{5,6},{6,7},{7,4},{8,9},{9,10},{10,1... | collective-permute-start | bytes 1179656 | tf_op jit(solution)/shard_map/ppermute | solution.py:38
  370.4 44.0 %all-to-all-start = ((bf16[16,80,1024]{2,1,0:T(8,128)(2,1)}), bf16[16,80,1024]{2,1,0:T(8,128)(2,1)S(1)}, u32[]{:S(2)}, u32[]{:S(2)}) async-start(bf16[16,80,1024]{2,1,0:T(8,128)(2,1)} %rest_sum.1), calls=%async_computation | async-start | bytes 5242880 | tf_op jit(solution)/shard_map/all_to_all | solution.py:793
  383.4 9.9 %collective-permute-start.44 = (bf16[128,1024]{1,0:T(8,128)(2,1)S(1)}, bf16[128,1024]{1,0:T(8,128)(2,1)S(1)}, u32[]{:S(2)}, u32[]{:S(2)}) collective-permute-start(bf16[128,1024]{1,0:T(8,128)(2,1)S(1)} %fusion.1), channel_id=1, source_target_pairs={{0,4},{1,5},{2,6},{3,7},{4,0},{5,1},{6,2},{7,3},{8,12},{9,13},{10,... | collective-permute-start | bytes 786440 | tf_op jit(solution)/shard_map/ppermute | solution.py:38
  414.4 24.7 %all-to-all-start.1 = ((bf16[8,64,1408]{2,1,0:T(8,128)(2,1)}), bf16[8,64,1408]{2,1,0:T(8,128)(2,1)}, u32[]{:S(2)}, u32[]{:S(2)}) async-start(bf16[8,64,1408]{2,1,0:T(8,128)(2,1)} %copy-done.7), calls=%async_computation.2 | async-start | bytes 2883584 | tf_op jit(solution)/shard_map/all_to_all | solution.py:793
  (100 other events, 1384.0 us)
Sparse Core Ops, SparseCore 0:
  249.0 29.4 all-gather.2
Sparse Core Ops, SparseCore 1:
  297.1 56.4 reduce-scatter.1

commit v5 on v4

--- a/solution.py
+++ b/solution.py
@@ -127,15 +127,7 @@
 
 
 def project_kernel(x_ref, t_ref, mix_ref, own_ref, other_ref, gain_ref, w_ref, v1_ref, cos_ref, sin_ref,
-                   m0, m1, m2, m3, n_ref, v_ref, h_ref, zero_ref, cos_buf, sin_buf, sems):
-    copies = []
-    for part in range(4):
-        at = pl.ds(pl.multiple_of(place_block(x_ref[0], part) * BLOCK, BLOCK), BLOCK)
-        to = pl.ds(part * BLOCK, BLOCK)
-        copies.append(pltpu.make_async_copy(cos_ref.at[at], cos_buf.at[to], sems.at[part, 0]))
-        copies.append(pltpu.make_async_copy(sin_ref.at[at], sin_buf.at[to], sems.at[part, 1]))
-    for copy in copies:
-        copy.start()
+                   m0, m1, m2, m3, n_ref, v_ref, h_ref, zero_ref):
     zero_ref[...] = jnp.zeros_like(zero_ref)
     rows = h_ref.shape[0]
     h_ref[own_half(t_ref, rows), :] = own_ref[...]
@@ -143,8 +135,6 @@
     for part in halves(rows):
         h = h_ref[part].astype(F32)
         n_ref[part] = (h * rms_scale(h) * gain_ref[...]).astype(BF)
-    for copy in copies:
-        copy.wait()
     outs = (m0, m1, m2, m3)
     for pair in ((0, 1), (2, 3)):
         weight = jnp.concatenate(
@@ -152,7 +142,7 @@
         )
         for part in halves(rows):
             both = jnp.dot(n_ref[part], weight, preferred_element_type=F32)
-            cosine, sine = cos_buf[part], sin_buf[part]
+            cosine, sine = cos_ref[part], sin_ref[part]
             for index, k in enumerate(pair):
                 query, key, value = [
                     both[:, (3 * index + c) * PAIR : (3 * index + c + 1) * PAIR] for c in range(3)
@@ -171,8 +161,7 @@
         (x_index, t_index, mix, own, other, gain, w_qkv, value_first, cosine, sine),
         [shaped(3, rows, PAIR)] * 4
         + [shaped(rows, width), shaped(RING, rows, PAIR), shaped(rows, width), shaped(8, PAIR)],
-        scratch=[pltpu.VMEM((rows, PAIR), F32)] * 2 + [pltpu.SemaphoreType.DMA((4, 2))],
-        smem=3, far=2, waits=waits, limit=5, us=3, name="project",
+        smem=3, waits=waits, limit=5, us=3, name="project",
     )
 
 
@@ -813,6 +802,15 @@
     lens = lax.dynamic_slice(doc_lengths, (z, y, 0), (1, 1, 4))
     ends = jnp.cumsum(lens.reshape(4), dtype=jnp.int32)
     cosine, sine = rotary_tables()
+    own_cosine, own_sine = [
+        jnp.concatenate(
+            [
+                lax.dynamic_slice_in_dim(table, place_block(x, part) * BLOCK, BLOCK, 0)
+                for part in range(4)
+            ]
+        )
+        for table in (cosine, sine)
+    ]
     w_qkv = jnp.transpose(wqkv[0], (1, 0, 2))
     w_out, w_down = wo[0], wd[0]
     gain_one, gain_two = gains[0, 0:1], gains[0, 1:2]
@@ -824,7 +822,7 @@
 
     def first_half(own, value_first):
         *messages, normed, value, hidden, zero = project(
-            x_index, t_index, mix, own, swapped(own), gain_one, w_qkv, value_first, cosine, sine
+            x_index, t_index, mix, own, swapped(own), gain_one, w_qkv, value_first, own_cosine, own_sine
         )
         return out_and_back(messages, 1), normed, value, hidden, zero
 
@@ -877,11 +875,9 @@
     _, _, part, grad = first_back(top_grad)
     grad_middle, _, arrived, _ = second_back(grad, part)
     *grads, grad_value = third_back(arrived, no_value)
-    result = close(mine, keep, got, waits=(seen(grad_value),))
-    acts = regrouped(result.reshape(2, BLOCK, width))[None]
     gv_in = handed(grad_value, [(1, 0)])
     _, grad_hidden, half, _ = fourth_back(
-        grads, grad_middle, waits=(seen(gv_in), seen(acts[0, 0]))
+        grads, grad_middle, waits=(seen(gv_in),)
     )
     near = lax.all_gather(half, "dp", axis_index_groups=groups("x"))
     own_grad = jnp.where(first, handed(grad_hidden, [(1, 0)]), top_grad)
@@ -903,7 +899,9 @@
     grad_hidden, _, _, last = fourth_back(grads, grad_middle, waits=(seen(late),), us=BRIEF)
     rest = rest_sum(early, early_got, late, late_got, waits=(seen(last),))
     dins = regrouped(grad_hidden.reshape(2, BLOCK, width))[None]
-    feed_sum = summed([feed_sum], waits=(seen(rest), seen(dins[0, 0])))
+    result = close(mine, keep, got, waits=(seen(last),))
+    acts = regrouped(result.reshape(2, BLOCK, width))[None]
+    feed_sum = summed([feed_sum], waits=(seen(rest), seen(dins[0, 0]), seen(acts[0, 0])))
     feed_share = jnp.sum(all_to_all(feed_sum, "zx").astype(F32), axis=0)
     feed_share = feed_share.reshape(2, width // 32, -1)
     down_share, out_share, qkv_share, gain_total = finish(all_to_all(rest, "yx"))

time: 455 us -> 450 us (0.989)
  waiting for transfers between devices: 189 us -> 182 us
    all_to_all x2, waiting for transfers between devices: 35 us -> 27.8 us  [all_to_all(): return lax.all_to_all(value, 'dp', 0, 0, axis_index_groups=groups(kinds))]
    unnamed x162 -> x166, local copies, waits for them, and re-layouts: 41.9 us -> 35.3 us
  transfers between devices with their start and end apart: 52 -> 52, of which waited for: 36 -> 36; matrix products, arithmetic and copies ran while one was open for 2% -> 3% of each run, Pallas kernels for 19% -> 16%
where the time goes in v5:
time: 450 us; the launch traced here: 445 us
  waiting for transfers between devices  182 us (40%)
  Pallas kernels  122 us (27%)
  starting transfers between devices  73.3 us (16%)
  local copies, waits for them, and re-layouts  41.8 us (9%)
  between operations  16.7 us (4%)
  other arithmetic  9.38 us (2%)
    pallas_call x25, Pallas kernels, on_core(): pl.pallas_call(body, in_specs=spots, out_specs=[pl.BlockSpec(memory_space...  119 us
    ppermute x30, waiting for transfers between devices, moved(): return lax.ppermute(value, 'dp', along(kind, shift))  98.8 us
    ppermute x30, starting transfers between devices, moved(): return lax.ppermute(value, 'dp', along(kind, shift))  50.8 us
    ppermute x4, waiting for transfers between devices, handed(): return lax.ppermute(value, 'section', pairs)  39.5 us
    unnamed x166, local copies, waits for them, and re-layouts  35.3 us
    all_to_all x2, waiting for transfers between devices, all_to_all(): return lax.all_to_all(value, 'dp', 0, 0, axis_index_groups=groups(kinds))  27.8 us
    ppermute x14, waiting for transfers between devices, swapped(): return lax.ppermute(value, 'tensor', [(0, 1), (1, 0)])  15.6 us
    ppermute x4, starting transfers between devices, handed(): return lax.ppermute(value, 'section', pairs)  10.3 us
  transfers between devices with their start and end apart: 52, of which 36 were waited for; matrix products, arithmetic and copies ran while one was open for 3% of the time, Pallas kernels for 16%

profile of v5, /device:TPU:0, one launch (start us, length us, event | category | flops | bytes accessed | tf_op | source)
XLA Modules:
  0.0 444.6 jit_solution(3340526611200656172)
XLA Ops:
  9.9 4.0 collective-permute-start
  15.2 5.3 %collective-permute-done = bf16[128,1024]{1,0:T(8,128)(2,1)} collective-permute-done((bf16[128,1024]{1,0:T(8,128)(2,1)}, bf16[128,1024]{1,0:T(8,128)(2,1)}, u32[]{:S(2)}, u32[]{:S(2)}) %collective-permute-start) | collective-permute-done | bytes 262176 | tf_op jit(solution)/shard_map/ppermute | solution.py:38
  34.8 4.3 fusion.refs_5_
  41.1 9.4 %collective-permute-done.3.refs_4_ = bf16[3,512,128]{2,1,0:T(8,128)(2,1)S(1)} collective-permute-done((bf16[3,512,128]{2,1,0:T(8,128)(2,1)S(1)}, bf16[3,512,128]{2,1,0:T(8,128)(2,1)S(1)}, u32[]{:S(2)}, u32[]{:S(2)}) %collective-permute-start.3) | collective-permute-done | bytes 393248 | tf_op jit(solution)/shard_map/ppermute | solution.py:38
  50.5 11.4 %attend.2 = (bf16[512,128]{1,0:T(8,128)(2,1)S(1)}, bf16[512,128]{1,0:T(8,128)(2,1)S(1)}, bf16[512,128]{1,0:T(8,128)(2,1)S(1)}, bf16[512,128]{1,0:T(8,128)(2,1)S(...) custom-call(s32[1]{0:T(128)} %bitcast.1.refs_0_, s32[4]{0:T(128)S(1)} %bitcast.101, ...), custom_call_target="tpu_custom_call" | custom-call | flops 12099999744 | bytes 39600000 | tf_op jit(solution)/shard_map/attend/pallas_call | solution.py:85
  66.1 3.9 collective-permute-done.5.refs_2_
  78.1 7.9 %feed.2 = (f32[256,1024]{1,0:T(8,128)S(1)}, bf16[256,1024]{1,0:T(8,128)(2,1)S(1)}, bf16[256,1024]{1,0:T(8,128)(2,1)S(1)}, bf16[512,1024]{1,0:T(8,128)(2,1)}) custom-call(s32[1]{0:T(128)} %bitcast.refs_1_.refs_0_, bf16[512,1024]{1,0:T(8,128)(2,1)S(1)} %copy-done.77, bf16[512,1024]{1,0:T(8,128)(2,1)S(1)} %get-tuple-element.101.refs_2_, ...), custom_call_target="tpu_custom_call" | custom-call | flops 7699999744 | bytes 25200000 | tf_op jit(solution)/shard_map/feed/pallas_call | solution.py:85
  90.0 4.4 collective-permute-start.11
  94.5 11.0 %collective-permute-done.11 = bf16[256,1024]{1,0:T(8,128)(2,1)S(1)} collective-permute-done((bf16[256,1024]{1,0:T(8,128)(2,1)S(1)}, bf16[256,1024]{1,0:T(8,128)(2,1)S(1)}, u32[]{:S(2)}, u32[]{:S(2)}) %collective-permute-start.11) | collective-permute-done | bytes 524320 | tf_op jit(solution)/shard_map/ppermute | solution.py:821
  115.1 4.1 collective-permute-start.19
  119.2 12.6 %collective-permute-done.13.refs_3_.refs_4_ = bf16[3,512,128]{2,1,0:T(8,128)(2,1)S(1)} collective-permute-done((bf16[3,512,128]{2,1,0:T(8,128)(2,1)S(1)}, bf16[3,512,128]{2,1,0:T(8,128)(2,1)S(1)}, u32[]{:S(2)}, u32[]{:S(2)}) %collective-permute-start.13) | collective-permute-done | bytes 393248 | tf_op jit(solution)/shard_map/ppermute | solution.py:38
  132.5 10.4 %attend.3 = (bf16[512,128]{1,0:T(8,128)(2,1)S(1)}, bf16[512,128]{1,0:T(8,128)(2,1)S(1)}, bf16[512,128]{1,0:T(8,128)(2,1)S(1)}, bf16[512,128]{1,0:T(8,128)(2,1)S(...) custom-call(s32[1]{0:T(128)} %bitcast.1.refs_0_, s32[4]{0:T(128)S(1)} %bitcast.102, ...), custom_call_target="tpu_custom_call" | custom-call | flops 12099999744 | bytes 39600000 | tf_op jit(solution)/shard_map/attend/pallas_call | solution.py:85
  146.6 4.7 %collective-permute-done.16.refs_2_ = bf16[512,128]{1,0:T(8,128)(2,1)S(1)} collective-permute-done((bf16[512,128]{1,0:T(8,128)(2,1)S(1)}, bf16[512,128]{1,0:T(8,128)(2,1)S(1)}, u32[]{:S(2)}, u32[]{:S(2)}) %collective-permute-start.16) | collective-permute-done | bytes 131104 | tf_op jit(solution)/shard_map/ppermute | solution.py:38
  159.8 7.0 %feed.3 = (f32[256,1024]{1,0:T(8,128)S(1)}, bf16[256,1024]{1,0:T(8,128)(2,1)S(1)}, bf16[256,1024]{1,0:T(8,128)(2,1)S(1)}, bf16[512,1024]{1,0:T(8,128)(2,1)S(1)},...) custom-call(s32[1]{0:T(128)} %bitcast.refs_1_.refs_0_, ...), custom_call_target="tpu_custom_call" | custom-call | flops 7699999744 | bytes 25200000 | tf_op jit(solution)/shard_map/feed/pallas_call | solution.py:85
  171.6 7.3 %feed_back.2 = (bf16[512,1408]{1,0:T(8,128)(2,1)}, bf16[512,1408]{1,0:T(8,128)(2,1)}, bf16[512,1024]{1,0:T(8,128)(2,1)S(1)}, bf16[512,1024]{1,0:T(8,128)(2,1)S(1)}) custom-call(s32[1]{0:T(128)} %bitcast.refs_1_.refs_0_, bf16[256,1024]{1,0:T(8,128)(2,1)S(1)} %bitcast.87, bf16[256,1024]{1,0:T(8,128)(2,1)S(1)} %collective-permute-done.22.refs_2_, ...), custom_call_target="tpu_custom_call" | custom-call | flops 7699999744 | bytes 25200000 | tf_op jit(solution)/shard_map/feed_back/pallas_call | solution.py:85
  187.9 6.1 %collective-permute-done.24.refs_8_ = bf16[512,128]{1,0:T(8,128)(2,1)S(1)} collective-permute-done((bf16[512,128]{1,0:T(8,128)(2,1)S(1)}, bf16[512,128]{1,0:T(8,128)(2,1)S(1)}, u32[]{:S(2)}, u32[]{:S(2)}) %collective-permute-start.24) | collective-permute-done | bytes 131104 | tf_op jit(solution)/shard_map/ppermute | solution.py:38
  194.8 16.4 %attend_back.2 = (bf16[3,512,128]{2,1,0:T(8,128)(2,1)S(1)}, bf16[3,512,128]{2,1,0:T(8,128)(2,1)S(1)}, bf16[3,512,128]{2,1,0:T(8,128)(2,1)S(1)}, bf16[3,512,128]{2,1,0:T(8,128)(2,1)S(1)}, bf16[4,512,128]{2,1,0:T(8,128)(2,1)S(1)}) custom-call(s32[1]{0:T(128)} %bitcast.1.refs_0_, s32[4]{0:T(128)S(1)} %bitcast.103, f32[2]{0:T(128)S(1)} %broadcast_select_fusion.2.refs_2_, ...), custom_call_target="tpu_custom_call" | custom-call | flops 22000001024 | bytes 72000000 | tf_op jit(solution)/shard_map/attend_back/pallas_call | solution.py:85
  216.1 10.0 %collective-permute-done.30.refs_13_ = bf16[4,512,128]{2,1,0:T(8,128)(2,1)S(1)} collective-permute-done((bf16[4,512,128]{2,1,0:T(8,128)(2,1)S(1)}, bf16[4,512,128]{2,1,0:T(8,128)(2,1)S(1)}, u32[]{:S(2)}, u32[]{:S(2)}) %collective-permute-start.30) | collective-permute-done | bytes 524320 | tf_op jit(solution)/shard_map/ppermute | solution.py:821
  226.1 5.9 %collective-permute-done.27.refs_3_ = bf16[3,512,128]{2,1,0:T(8,128)(2,1)S(1)} collective-permute-done((bf16[3,512,128]{2,1,0:T(8,128)(2,1)S(1)}, bf16[3,512,128]{2,1,0:T(8,128)(2,1)S(1)}, u32[]{:S(2)}, u32[]{:S(2)}) %collective-permute-start.27) | collective-permute-done | bytes 393248 | tf_op jit(solution)/shard_map/ppermute | solution.py:38
  244.5 14.9 %collective-permute-done.32 = bf16[256,1024]{1,0:T(8,128)(2,1)S(1)} collective-permute-done((bf16[256,1024]{1,0:T(8,128)(2,1)}, bf16[256,1024]{1,0:T(8,128)(2,1)S(1)}, u32[]{:S(2)}, u32[]{:S(2)}) %collective-permute-start.32) | collective-permute-done | bytes 524320 | tf_op jit(solution)/shard_map/ppermute | solution.py:821
  268.7 7.3 %feed_back.3 = (bf16[512,1408]{1,0:T(8,128)(2,1)S(1)}, bf16[512,1408]{1,0:T(8,128)(2,1)S(1)}, bf16[512,1024]{1,0:T(8,128)(2,1)S(1)}, bf16[512,1024]{1,0:T(8,128)(2,1)S(1)}) custom-call(s32[1]{0:T(128)} %bitcast.refs_1_.refs_0_, bf16[256,1024]{1,0:T(8,128)(2,1)S(1)} %broadcast_select_fusion.refs_1_, bf16[256,1024]{1,0:T(8,128)(2,1)S(1)} %collective-permute-done.33.refs_2_, ...), custom_call_target="tpu_custom_call" | custom-call | flops 1100000 | bytes 3600 | tf_op jit(solution)/shard_map/feed_back/pallas_call | solution.py:85
  296.7 3.9 early_terms.1
  300.5 3.7 collective-permute-start.45
  309.0 6.0 %collective-permute-done.35.refs_8_ = bf16[512,128]{1,0:T(8,128)(2,1)S(1)} collective-permute-done((bf16[512,128]{1,0:T(8,128)(2,1)}, bf16[512,128]{1,0:T(8,128)(2,1)S(1)}, u32[]{:S(2)}, u32[]{:S(2)}) %collective-permute-start.35) | collective-permute-done | bytes 131104 | tf_op jit(solution)/shard_map/ppermute | solution.py:38
  315.6 17.1 %attend_back.3 = (bf16[3,512,128]{2,1,0:T(8,128)(2,1)S(1)}, bf16[3,512,128]{2,1,0:T(8,128)(2,1)S(1)}, bf16[3,512,128]{2,1,0:T(8,128)(2,1)S(1)}, bf16[3,512,128]{2,1,0:T(8,128)(2,1)S(1)}, bf16[4,512,128]{2,1,0:T(8,128)(2,1)}) custom-call(s32[1]{0:T(128)} %bitcast.1.refs_0_, s32[4]{0:T(128)S(1)} %bitcast.104, f32[2]{0:T(128)S(1)} %copy-done.63, ...), custom_call_target="tpu_custom_call" | custom-call | flops 1100000 | bytes 3600 | tf_op jit(solution)/shard_map/attend_back/pallas_call | solution.py:85
  339.6 16.0 %collective-permute-done.39.refs_3_ = bf16[3,512,128]{2,1,0:T(8,128)(2,1)S(1)} collective-permute-done((bf16[3,512,128]{2,1,0:T(8,128)(2,1)S(1)}, bf16[3,512,128]{2,1,0:T(8,128)(2,1)S(1)}, u32[]{:S(2)}, u32[]{:S(2)}) %collective-permute-start.39) | collective-permute-done | bytes 393248 | tf_op jit(solution)/shard_map/ppermute | solution.py:38
  365.4 5.0 %all-to-all-start = ((bf16[16,80,1024]{2,1,0:T(8,128)(2,1)}), bf16[16,80,1024]{2,1,0:T(8,128)(2,1)S(1)}, u32[]{:S(2)}, u32[]{:S(2)}) async-start(bf16[16,80,1024]{2,1,0:T(8,128)(2,1)} %rest_sum.1), calls=%async_computation | async-start | bytes 5242880 | tf_op jit(solution)/shard_map/all_to_all | solution.py:782
  379.1 5.7 %collective-permute-done.42 = bf16[128,1024]{1,0:T(8,128)(2,1)S(1)} collective-permute-done((bf16[128,1024]{1,0:T(8,128)(2,1)S(1)}, bf16[128,1024]{1,0:T(8,128)(2,1)S(1)}, u32[]{:S(2)}, u32[]{:S(2)}) %collective-permute-start.42) | collective-permute-done | bytes 262176 | tf_op jit(solution)/shard_map/ppermute | solution.py:38
  389.9 5.8 %collective-permute-done.44 = bf16[128,1024]{1,0:T(8,128)(2,1)S(1)} collective-permute-done((bf16[128,1024]{1,0:T(8,128)(2,1)S(1)}, bf16[128,1024]{1,0:T(8,128)(2,1)S(1)}, u32[]{:S(2)}, u32[]{:S(2)}) %collective-permute-start.44) | collective-permute-done | bytes 262176 | tf_op jit(solution)/shard_map/ppermute | solution.py:38
  399.5 10.1 %all-to-all-done.refs_0_ = bf16[16,80,1024]{2,1,0:T(8,128)(2,1)S(1)} async-done(((bf16[16,80,1024]{2,1,0:T(8,128)(2,1)}), bf16[16,80,1024]{2,1,0:T(8,128)(2,1)S(1)}, u32[]{:S(2)}, u32[]{:S(2)}) %all-to-all-start) | async-done | bytes 2621472 | tf_op jit(solution)/shard_map/all_to_all | solution.py:782
  409.6 4.4 %all-to-all-start.1 = ((bf16[8,64,1408]{2,1,0:T(8,128)(2,1)}), bf16[8,64,1408]{2,1,0:T(8,128)(2,1)}, u32[]{:S(2)}, u32[]{:S(2)}) async-start(bf16[8,64,1408]{2,1,0:T(8,128)(2,1)} %copy-done.6), calls=%async_computation.2 | async-start | bytes 2883584 | tf_op jit(solution)/shard_map/all_to_all | solution.py:782
  416.7 17.7 %all-to-all-done.1 = bf16[8,64,1408]{2,1,0:T(8,128)(2,1)} async-done(((bf16[8,64,1408]{2,1,0:T(8,128)(2,1)}), bf16[8,64,1408]{2,1,0:T(8,128)(2,1)}, u32[]{:S(2)}, u32[]{:S(2)}) %all-to-all-start.1) | async-done | bytes 1441824 | tf_op jit(solution)/shard_map/all_to_all | solution.py:782
  (313 shorter events, 164.3 us)
Async XLA Ops:
  8.0 283.5 %all-gather.3.cloned.1.call-start = ((), (), s32[]{:S(2)}) async-start(), calls=%async_computation.4 | async-start | bytes 2621440 | tf_op jit(solution)/shard_map/all_gather | solution.py:882
  9.9 10.6 %collective-permute-start = (bf16[128,1024]{1,0:T(8,128)(2,1)}, bf16[128,1024]{1,0:T(8,128)(2,1)}, u32[]{:S(2)}, u32[]{:S(2)}) collective-permute-start(bf16[128,1024]{1,0:T(8,128)(2,1)} %get-tuple-element.198), channel_id=1, source_target_pairs={{0,4},{1,5},{2,6},{3,7},{4,0},{5,1},{6,2},{7,3},{8,12},{9,13},{10,... | collective-permute-start | bytes 786440 | tf_op jit(solution)/shard_map/ppermute | solution.py:38
  28.7 12.4 %collective-permute-start.2 = (bf16[3,512,128]{2,1,0:T(8,128)(2,1)S(1)}, bf16[3,512,128]{2,1,0:T(8,128)(2,1)S(1)}, u32[]{:S(2)}, u32[]{:S(2)}) collective-permute-start(bf16[3,512,128]{2,1,0:T(8,128)(2,1)S(1)} %get-tuple-element.92), channel_id=1, source_target_pairs={{0,1},{1,2},{2,3},{3,0},{4,5},{5,6},{6,7},{7,4},{8,9},{9,10},{10,1... | collective-permute-start | bytes 1179656 | tf_op jit(solution)/shard_map/ppermute | solution.py:38
  30.2 20.2 %collective-permute-start.3 = (bf16[3,512,128]{2,1,0:T(8,128)(2,1)S(1)}, bf16[3,512,128]{2,1,0:T(8,128)(2,1)S(1)}, u32[]{:S(2)}, u32[]{:S(2)}) collective-permute-start(bf16[3,512,128]{2,1,0:T(8,128)(2,1)S(1)} %get-tuple-element.93), channel_id=1, source_target_pairs={{0,2},{1,3},{2,0},{3,1},{4,6},{5,7},{6,4},{7,5},{8,10},{9,11},{10,... | collective-permute-start | bytes 1179656 | tf_op jit(solution)/shard_map/ppermute | solution.py:38
  32.9 17.6 %collective-permute-start.4 = (bf16[3,512,128]{2,1,0:T(8,128)(2,1)S(1)}, bf16[3,512,128]{2,1,0:T(8,128)(2,1)S(1)}, u32[]{:S(2)}, u32[]{:S(2)}) collective-permute-start(bf16[3,512,128]{2,1,0:T(8,128)(2,1)S(1)} %get-tuple-element.94), channel_id=1, source_target_pairs={{0,3},{1,0},{2,1},{3,2},{4,7},{5,4},{6,5},{7,6},{8,11},{9,8},{10,9... | collective-permute-start | bytes 1179656 | tf_op jit(solution)/shard_map/ppermute | solution.py:38
  74.9 15.0 %collective-permute-start.10 = (bf16[4,512,128]{2,1,0:T(8,128)(2,1)S(1)}, bf16[4,512,128]{2,1,0:T(8,128)(2,1)S(1)}, u32[]{:S(2)}, u32[]{:S(2)}) collective-permute-start(bf16[4,512,128]{2,1,0:T(8,128)(2,1)S(1)} %get-tuple-element.105), channel_id=1, source_target_pairs={{0,64},{1,65},{2,66},{3,67},{4,68},{5,69},{6,70},{7,71},{8,72},{9,... | collective-permute-start | bytes 1572872 | tf_op jit(solution)/shard_map/ppermute | solution.py:821
  90.0 15.4 %collective-permute-start.11 = (bf16[256,1024]{1,0:T(8,128)(2,1)S(1)}, bf16[256,1024]{1,0:T(8,128)(2,1)S(1)}, u32[]{:S(2)}, u32[]{:S(2)}) collective-permute-start(bf16[256,1024]{1,0:T(8,128)(2,1)S(1)} %close.2), channel_id=1, source_target_pairs={{0,64},{1,65},{2,66},{3,67},{4,68},{5,69},{6,70},{7,71},{8,72},{9,... | collective-permute-start | bytes 1572872 | tf_op jit(solution)/shard_map/ppermute | solution.py:821
  111.0 20.8 %collective-permute-start.13 = (bf16[3,512,128]{2,1,0:T(8,128)(2,1)S(1)}, bf16[3,512,128]{2,1,0:T(8,128)(2,1)S(1)}, u32[]{:S(2)}, u32[]{:S(2)}) collective-permute-start(bf16[3,512,128]{2,1,0:T(8,128)(2,1)S(1)} %get-tuple-element.108), channel_id=1, source_target_pairs={{0,1},{1,2},{2,3},{3,0},{4,5},{5,6},{6,7},{7,4},{8,9},{9,10},{10,1... | collective-permute-start | bytes 1179656 | tf_op jit(solution)/shard_map/ppermute | solution.py:38
  111.0 20.8 %collective-permute-start.14 = (bf16[3,512,128]{2,1,0:T(8,128)(2,1)S(1)}, bf16[3,512,128]{2,1,0:T(8,128)(2,1)S(1)}, u32[]{:S(2)}, u32[]{:S(2)}) collective-permute-start(bf16[3,512,128]{2,1,0:T(8,128)(2,1)S(1)} %get-tuple-element.109), channel_id=1, source_target_pairs={{0,2},{1,3},{2,0},{3,1},{4,6},{5,7},{6,4},{7,5},{8,10},{9,11},{10,... | collective-permute-start | bytes 1179656 | tf_op jit(solution)/shard_map/ppermute | solution.py:38
  113.1 19.3 %collective-permute-start.15 = (bf16[3,512,128]{2,1,0:T(8,128)(2,1)S(1)}, bf16[3,512,128]{2,1,0:T(8,128)(2,1)S(1)}, u32[]{:S(2)}, u32[]{:S(2)}) collective-permute-start(bf16[3,512,128]{2,1,0:T(8,128)(2,1)S(1)} %get-tuple-element.110), channel_id=1, source_target_pairs={{0,3},{1,0},{2,1},{3,2},{4,7},{5,4},{6,5},{7,6},{8,11},{9,8},{10,9... | collective-permute-start | bytes 1179656 | tf_op jit(solution)/shard_map/ppermute | solution.py:38
  115.1 31.4 %collective-permute-start.19 = (bf16[128,1024]{1,0:T(8,128)(2,1)S(1)}, bf16[128,1024]{1,0:T(8,128)(2,1)S(1)}, u32[]{:S(2)}, u32[]{:S(2)}) collective-permute-start(bf16[128,1024]{1,0:T(8,128)(2,1)S(1)} %get-tuple-element.117), channel_id=1, source_target_pairs={{0,4},{1,5},{2,6},{3,7},{4,0},{5,1},{6,2},{7,3},{8,12},{9,13},{10,... | collective-permute-start | bytes 786440 | tf_op jit(solution)/shard_map/ppermute | solution.py:38
  157.1 14.4 %collective-permute-start.22 = (bf16[256,1024]{1,0:T(8,128)(2,1)S(1)}, bf16[256,1024]{1,0:T(8,128)(2,1)S(1)}, u32[]{:S(2)}, u32[]{:S(2)}) collective-permute-start(bf16[256,1024]{1,0:T(8,128)(2,1)S(1)} %bitcast.86), channel_id=1, source_target_pairs={{0,32},{32,0},{1,33},{33,1},{2,34},{34,2},{3,35},{35,3},{4,36},{36... | collective-permute-start | bytes 1572872 | tf_op jit(solution)/shard_map/ppermute | solution.py:42
  184.5 9.6 %collective-permute-start.24 = (bf16[512,128]{1,0:T(8,128)(2,1)S(1)}, bf16[512,128]{1,0:T(8,128)(2,1)S(1)}, u32[]{:S(2)}, u32[]{:S(2)}) collective-permute-start(bf16[512,128]{1,0:T(8,128)(2,1)S(1)} %get-tuple-element.129), channel_id=1, source_target_pairs={{0,1},{1,2},{2,3},{3,0},{4,5},{5,6},{6,7},{7,4},{8,9},{9,10},{10,1... | collective-permute-start | bytes 393224 | tf_op jit(solution)/shard_map/ppermute | solution.py:38
  184.5 9.6 %collective-permute-start.25 = (bf16[512,128]{1,0:T(8,128)(2,1)S(1)}, bf16[512,128]{1,0:T(8,128)(2,1)S(1)}, u32[]{:S(2)}, u32[]{:S(2)}) collective-permute-start(bf16[512,128]{1,0:T(8,128)(2,1)S(1)} %get-tuple-element.130), channel_id=1, source_target_pairs={{0,2},{1,3},{2,0},{3,1},{4,6},{5,7},{6,4},{7,5},{8,10},{9,11},{10,... | collective-permute-start | bytes 393224 | tf_op jit(solution)/shard_map/ppermute | solution.py:38
  211.2 14.9 %collective-permute-start.30 = (bf16[4,512,128]{2,1,0:T(8,128)(2,1)S(1)}, bf16[4,512,128]{2,1,0:T(8,128)(2,1)S(1)}, u32[]{:S(2)}, u32[]{:S(2)}) collective-permute-start(bf16[4,512,128]{2,1,0:T(8,128)(2,1)S(1)} %get-tuple-element.138), channel_id=1, source_target_pairs={{64,0},{65,1},{66,2},{67,3},{68,4},{69,5},{70,6},{71,7},{72,8},{73... | collective-permute-start | bytes 1572872 | tf_op jit(solution)/shard_map/ppermute | solution.py:821
  212.5 19.5 %collective-permute-start.27 = (bf16[3,512,128]{2,1,0:T(8,128)(2,1)S(1)}, bf16[3,512,128]{2,1,0:T(8,128)(2,1)S(1)}, u32[]{:S(2)}, u32[]{:S(2)}) collective-permute-start(bf16[3,512,128]{2,1,0:T(8,128)(2,1)S(1)} %get-tuple-element.135), channel_id=1, source_target_pairs={{0,3},{1,0},{2,1},{3,2},{4,7},{5,4},{6,5},{7,6},{8,11},{9,8},{10,9... | collective-permute-start | bytes 1179656 | tf_op jit(solution)/shard_map/ppermute | solution.py:38
  215.1 16.9 %collective-permute-start.28 = (bf16[3,512,128]{2,1,0:T(8,128)(2,1)S(1)}, bf16[3,512,128]{2,1,0:T(8,128)(2,1)S(1)}, u32[]{:S(2)}, u32[]{:S(2)}) collective-permute-start(bf16[3,512,128]{2,1,0:T(8,128)(2,1)S(1)} %get-tuple-element.136), channel_id=1, source_target_pairs={{0,2},{1,3},{2,0},{3,1},{4,6},{5,7},{6,4},{7,5},{8,10},{9,11},{10,... | collective-permute-start | bytes 1179656 | tf_op jit(solution)/shard_map/ppermute | solution.py:38
  215.1 20.3 %collective-permute-start.29 = (bf16[3,512,128]{2,1,0:T(8,128)(2,1)S(1)}, bf16[3,512,128]{2,1,0:T(8,128)(2,1)S(1)}, u32[]{:S(2)}, u32[]{:S(2)}) collective-permute-start(bf16[3,512,128]{2,1,0:T(8,128)(2,1)S(1)} %get-tuple-element.137), channel_id=1, source_target_pairs={{0,1},{1,2},{2,3},{3,0},{4,5},{5,6},{6,7},{7,4},{8,9},{9,10},{10,1... | collective-permute-start | bytes 1179656 | tf_op jit(solution)/shard_map/ppermute | solution.py:38
  243.0 153.9 %reduce-scatter.2.cloned.1.call-start = ((), (), s32[]{:S(2)}) async-start(), calls=%async_computation.3 | async-start | bytes 7208960 | tf_op jit(solution)/shard_map/reduce_scatter | solution.py:888
  243.1 16.3 %collective-permute-start.32 = (bf16[256,1024]{1,0:T(8,128)(2,1)}, bf16[256,1024]{1,0:T(8,128)(2,1)S(1)}, u32[]{:S(2)}, u32[]{:S(2)}) collective-permute-start(bf16[256,1024]{1,0:T(8,128)(2,1)} %copy-done.68), channel_id=1, source_target_pairs={{64,0},{65,1},{66,2},{67,3},{68,4},{69,5},{70,6},{71,7},{72,8},{73... | collective-permute-start | bytes 1572872 | tf_op jit(solution)/shard_map/ppermute | solution.py:821
  291.5 17.4 %collective-permute-start.38 = (bf16[4,256,1024]{2,1,0:T(8,128)(2,1)}, bf16[4,256,1024]{2,1,0:T(8,128)(2,1)S(1)}, u32[]{:S(2)}, u32[]{:S(2)}) collective-permute-start(bf16[4,256,1024]{2,1,0:T(8,128)(2,1)} %bitcast.90), channel_id=1, source_target_pairs={{0,32},{32,0},{1,33},{33,1},{2,34},{34,2},{3,35},{35,3},{4,36},{36... | collective-permute-start | bytes 6291464 | tf_op jit(solution)/shard_map/ppermute | solution.py:42
  300.5 62.5 %collective-permute-start.45 = (bf16[16,64,1024]{2,1,0:T(8,128)(2,1)S(1)}, bf16[16,64,1024]{2,1,0:T(8,128)(2,1)S(1)}, u32[]{:S(2)}, u32[]{:S(2)}) collective-permute-start(bf16[16,64,1024]{2,1,0:T(8,128)(2,1)S(1)} %get-tuple-element.167), channel_id=1, source_target_pairs={{0,4},{1,5},{2,6},{3,7},{4,0},{5,1},{6,2},{7,3},{8,12},{9,13},{10,... | collective-permute-start | bytes 6291464 | tf_op jit(solution)/shard_map/ppermute | solution.py:38
  305.2 9.7 %collective-permute-start.35 = (bf16[512,128]{1,0:T(8,128)(2,1)}, bf16[512,128]{1,0:T(8,128)(2,1)S(1)}, u32[]{:S(2)}, u32[]{:S(2)}) collective-permute-start(bf16[512,128]{1,0:T(8,128)(2,1)} %copy-done.71), channel_id=1, source_target_pairs={{0,1},{1,2},{2,3},{3,0},{4,5},{5,6},{6,7},{7,4},{8,9},{9,10},{10,1... | collective-permute-start | bytes 393224 | tf_op jit(solution)/shard_map/ppermute | solution.py:38
  305.3 9.6 %collective-permute-start.36 = (bf16[512,128]{1,0:T(8,128)(2,1)}, bf16[512,128]{1,0:T(8,128)(2,1)S(1)}, u32[]{:S(2)}, u32[]{:S(2)}) collective-permute-start(bf16[512,128]{1,0:T(8,128)(2,1)} %copy-done.70), channel_id=1, source_target_pairs={{0,2},{1,3},{2,0},{3,1},{4,6},{5,7},{6,4},{7,5},{8,10},{9,11},{10,... | collective-permute-start | bytes 393224 | tf_op jit(solution)/shard_map/ppermute | solution.py:38
  335.7 27.4 %collective-permute-start.46 = (bf16[16,16,1024]{2,1,0:T(8,128)(2,1)S(1)}, bf16[16,16,1024]{2,1,0:T(8,128)(2,1)S(1)}, u32[]{:S(2)}, u32[]{:S(2)}) collective-permute-start(bf16[16,16,1024]{2,1,0:T(8,128)(2,1)S(1)} %get-tuple-element.168), channel_id=1, source_target_pairs={{0,4},{1,5},{2,6},{3,7},{4,0},{5,1},{6,2},{7,3},{8,12},{9,13},{10,... | collective-permute-start | bytes 1572872 | tf_op jit(solution)/shard_map/ppermute | solution.py:38
  336.1 19.4 %collective-permute-start.39 = (bf16[3,512,128]{2,1,0:T(8,128)(2,1)S(1)}, bf16[3,512,128]{2,1,0:T(8,128)(2,1)S(1)}, u32[]{:S(2)}, u32[]{:S(2)}) collective-permute-start(bf16[3,512,128]{2,1,0:T(8,128)(2,1)S(1)} %get-tuple-element.158.refs_7_), channel_id=1, source_target_pairs={{0,3},{1,0},{2,1},{3,2},{4,7},{5,4},{6,5},{7,6},{8,11},{9,8},{10,9... | collective-permute-start | bytes 1179656 | tf_op jit(solution)/shard_map/ppermute | solution.py:38
  338.7 16.8 %collective-permute-start.40 = (bf16[3,512,128]{2,1,0:T(8,128)(2,1)S(1)}, bf16[3,512,128]{2,1,0:T(8,128)(2,1)S(1)}, u32[]{:S(2)}, u32[]{:S(2)}) collective-permute-start(bf16[3,512,128]{2,1,0:T(8,128)(2,1)S(1)} %get-tuple-element.159.refs_8_), channel_id=1, source_target_pairs={{0,2},{1,3},{2,0},{3,1},{4,6},{5,7},{6,4},{7,5},{8,10},{9,11},{10,... | collective-permute-start | bytes 1179656 | tf_op jit(solution)/shard_map/ppermute | solution.py:38
  338.7 20.2 %collective-permute-start.41 = (bf16[3,512,128]{2,1,0:T(8,128)(2,1)S(1)}, bf16[3,512,128]{2,1,0:T(8,128)(2,1)S(1)}, u32[]{:S(2)}, u32[]{:S(2)}) collective-permute-start(bf16[3,512,128]{2,1,0:T(8,128)(2,1)S(1)} %get-tuple-element.160.refs_9_), channel_id=1, source_target_pairs={{0,1},{1,2},{2,3},{3,0},{4,5},{5,6},{6,7},{7,4},{8,9},{9,10},{10,1... | collective-permute-start | bytes 1179656 | tf_op jit(solution)/shard_map/ppermute | solution.py:38
  365.4 44.2 %all-to-all-start = ((bf16[16,80,1024]{2,1,0:T(8,128)(2,1)}), bf16[16,80,1024]{2,1,0:T(8,128)(2,1)S(1)}, u32[]{:S(2)}, u32[]{:S(2)}) async-start(bf16[16,80,1024]{2,1,0:T(8,128)(2,1)} %rest_sum.1), calls=%async_computation | async-start | bytes 5242880 | tf_op jit(solution)/shard_map/all_to_all | solution.py:782
  370.5 14.4 %collective-permute-start.43 = (bf16[256,1024]{1,0:T(8,128)(2,1)}, bf16[256,1024]{1,0:T(8,128)(2,1)S(1)}, u32[]{:S(2)}, u32[]{:S(2)}) collective-permute-start(bf16[256,1024]{1,0:T(8,128)(2,1)} %copy-done.67), channel_id=1, source_target_pairs={{0,32},{32,0},{1,33},{33,1},{2,34},{34,2},{3,35},{35,3},{4,36},{36... | collective-permute-start | bytes 1572872 | tf_op jit(solution)/shard_map/ppermute | solution.py:42
  374.9 9.9 %collective-permute-start.42 = (bf16[128,1024]{1,0:T(8,128)(2,1)S(1)}, bf16[128,1024]{1,0:T(8,128)(2,1)S(1)}, u32[]{:S(2)}, u32[]{:S(2)}) collective-permute-start(bf16[128,1024]{1,0:T(8,128)(2,1)S(1)} %get-tuple-element.196), channel_id=1, source_target_pairs={{0,4},{1,5},{2,6},{3,7},{4,0},{5,1},{6,2},{7,3},{8,12},{9,13},{10,... | collective-permute-start | bytes 786440 | tf_op jit(solution)/shard_map/ppermute | solution.py:38
  409.6 24.7 %all-to-all-start.1 = ((bf16[8,64,1408]{2,1,0:T(8,128)(2,1)}), bf16[8,64,1408]{2,1,0:T(8,128)(2,1)}, u32[]{:S(2)}, u32[]{:S(2)}) async-start(bf16[8,64,1408]{2,1,0:T(8,128)(2,1)} %copy-done.6), calls=%async_computation.2 | async-start | bytes 2883584 | tf_op jit(solution)/shard_map/all_to_all | solution.py:782
  (102 other events, 1602.0 us)
Sparse Core Ops, SparseCore 0:
  243.2 31.6 all-gather.2
Sparse Core Ops, SparseCore 1:
  291.5 59.3 reduce-scatter.1
